TPU v7x, 256 devices: a whole 4x4x8 slice. The times are simulated.
256 devices in a mesh: rx: 16 (over z, y_lo), ry: 4 (over x), ma: 4 (over y_hi, core).
Axes of the slice: x: 4, y: 4 (y_hi: 2, y_lo: 2; y = y_hi * 2 + y_lo), z: 8, core: 2. Of those that a mesh axis runs over, the one named last changes fastest.
Arguments:
- numerator: float32 [16, 4, 120, 13824], P('rx', 'ry', None, 'ma'), may hold values from -6 to 6
- weight: float32 [16, 4], P('rx', 'ry'), may hold values from 0.5 to 2
- inputs: bfloat16 [16, 4, 2, 256, 13824], P('rx', 'ry', None, None, 'ma'), may hold values from -0.125 to 0.125
- targets: float32 [16, 4, 2, 120, 256], P('rx', 'ry'), may hold values from -6 to 6
- first_moment: float32 [16, 4, 120, 13824], P('rx', 'ry', None, 'ma'), may hold values from -1.5 to 1.5
- second_moment: float32 [16, 4, 120, 13824], P('rx', 'ry', None, 'ma'), may hold values from 0.005 to 0.2
Outputs:
- new_numerator: float32 [16, 4, 120, 13824], P('rx', 'ry', None, 'ma')
- new_weight: float32 [16, 4], P('rx', 'ry')
- new_first: float32 [16, 4, 120, 13824], P('rx', 'ry', None, 'ma')
- new_second: float32 [16, 4, 120, 13824], P('rx', 'ry', None, 'ma')
All inputs are finite; a program needn't handle non-finite values.
Results may differ from a plain program's by a relative error of at most 0.0003.
Values sent between devices are 32-bit elements; how exact they have to be, the bound alone decides.
No kernel may reach another device: no remote copies, remote signals or barrier semaphores. Data moves between devices by JAX's collectives and lax.ppermute only.
A program may use at most 64 MiB of HBM per device.

v0:
```python
import jax
import jax.numpy as jnp
from jax import lax
from jax.sharding import PartitionSpec as P

PRIOR_STEPS = 100


BETA_ONE = 0.9
BETA_TWO = 0.999
LEARN_RATE = 0.05
EPSILON = 1e-08


def shifted(block, axis, distance):
    devices = range(lax.axis_size(axis))
    route = [((i - distance) % len(devices), i) for i in devices]
    return lax.ppermute(block, axis, route)


def adam_update(params, gradient, first, second, count):
    first = BETA_ONE * first + (1.0 - BETA_ONE) * gradient
    second = BETA_TWO * second + (1.0 - BETA_TWO) * gradient * gradient
    first_corr = 1.0 - BETA_ONE**count
    second_corr = 1.0 - BETA_TWO**count
    params = params - LEARN_RATE * (first / first_corr) / (jnp.sqrt(second / second_corr) + EPSILON)
    return (params, first, second)


def mix_row(values, scales):
    left_values, left_scales = shifted((values, scales), "rx", 1)
    right_values, right_scales = shifted((values, scales), "rx", -1)
    return (
        (values + left_values + right_values) / 3.0,
        (scales + left_scales + right_scales) / 3.0,
    )


def mix_column(values, scales):
    left_values, left_scales = shifted((values, scales), "ry", 1)
    right_values, right_scales = shifted((values, scales), "ry", -1)
    return (
        (values + left_values + right_values) / 3.0,
        (scales + left_scales + right_scales) / 3.0,
    )


def one_round(values, scales, first, second, inputs_narrow, targets_round, mixer, count):
    inputs_round = inputs_narrow.astype(jnp.float32)
    values, scales = mixer(values, scales)
    params = values[0, 0] / scales[0, 0]
    partial_pred = jnp.einsum("cf,tf->ct", params, inputs_round, precision=lax.Precision.HIGHEST)
    predicted = lax.psum(partial_pred, "ma")
    gradient = jnp.einsum(
        "ct,tf->cf", predicted - targets_round, inputs_round, precision=lax.Precision.HIGHEST
    )
    params, new_first, new_second = adam_update(params, gradient, first[0, 0], second[0, 0], count)
    values = (scales[0, 0] * params)[None, None]
    return (values, scales, new_first[None, None], new_second[None, None])


def local(numerator, weight, inputs, targets, first_moment, second_moment):
    values, scales, first, second = one_round(
        numerator,
        weight,
        first_moment,
        second_moment,
        inputs[0, 0, 0],
        targets[0, 0, 0],
        mix_row,
        PRIOR_STEPS + 1,
    )
    values, scales, first, second = one_round(
        values,
        scales,
        first,
        second,
        inputs[0, 0, 1],
        targets[0, 0, 1],
        mix_column,
        PRIOR_STEPS + 2,
    )
    return (values, scales, first, second)


def solution(mesh):
    return jax.shard_map(
        local,
        mesh=mesh,
        in_specs=(
            P("rx", "ry", None, "ma"),
            P("rx", "ry"),
            P("rx", "ry", None, None, "ma"),
            P("rx", "ry", None, None, None),
            P("rx", "ry", None, "ma"),
            P("rx", "ry", None, "ma"),
        ),
        out_specs=(
            P("rx", "ry", None, "ma"),
            P("rx", "ry"),
            P("rx", "ry", None, "ma"),
            P("rx", "ry", None, "ma"),
        ),
        check_vma=False,
    )
```

profile of v0, /device:TPU:1, one launch (start us, length us, event | category | flops | bytes accessed | tf_op | source)
XLA Modules:
  0.0 253.2 jit_solution(13335298537395719774)
XLA Ops:
  7.2 0.0 all-reduce.3.cloned.1.call-start
  7.2 2.2 collective-permute-start.4
  9.4 5.4 %collective-permute-start.5 = (f32[1,1,120,3456]{3,2,1,0:T(8,128)}, f32[1,1,120,3456]{3,2,1,0:T(8,128)S(1)}, u32[]{:S(2)}, u32[]{:S(2)}) collective-permute-start(f32[1,1,120,3456]{3,2,1,0:T(8,128)} %param.6), channel_id=1, source_target_pairs={{16,0},{32,16},{48,32},{64,48},{80,64},{96,80},{112,96},{128,112},... | collective-permute-start | bytes 4976648 | tf_op jit(solution)/shard_map/ppermute | solution.py:18
  14.8 0.0 collective-permute-start
  14.8 3.6 %collective-permute-start.1 = (f32[1,1]{1,0:T(1,128)}, f32[1,1]{1,0:T(1,128)}, u32[]{:S(2)}, u32[]{:S(2)}) collective-permute-start(f32[1,1]{1,0:T(1,128)} %param.7), channel_id=1, source_target_pairs={{16,0},{32,16},{48,32},{64,48},{80,64},{96,80},{112,96},{128,112},... | collective-permute-start | bytes 20 | tf_op jit(solution)/shard_map/ppermute | solution.py:18
  19.1 60.9 %collective-permute-done = f32[1,1]{1,0:T(1,128)} collective-permute-done((f32[1,1]{1,0:T(1,128)}, f32[1,1]{1,0:T(1,128)}, u32[]{:S(2)}, u32[]{:S(2)}) %collective-permute-start) | collective-permute-done | bytes 36 | tf_op jit(solution)/shard_map/ppermute | solution.py:18
  80.6 1.3 collective-permute-done.1
  82.6 0.0 collective-permute-done.4
  82.6 0.0 copy-start.3
  82.6 0.0 copy-start.4
  82.6 1.1 copy-done.3
  83.8 0.5 copy-done.4
  84.3 4.4 %fusion.6 = f32[120,256]{1,0:T(8,128)} fusion(bf16[1,1,2,256,3456]{4,3,2,1,0:T(8,128)(2,1)} %param.8, f32[1,1,120,3456]{3,2,1,0:T(8,128)S(1)} %collective-permute-done.5, f32[1,1,120,3456]{3,2,1,0:T(8,128)} %param.6, f32[1,1,120,3456]{3,2,1,0:T(8,128)S(1)} %collective-permute-done.4, f32[]{:T(128)} %bitcast.1), kind=kOutput, calls=%fused_computation.8 | convolution fusion | flops 1275678720 | bytes 6869504 | tf_op jit(solution)/shard_map/cf,tf->ct/dot_general | solution.py:52
  88.7 0.0 all-reduce.3.cloned.1.call-update
  88.8 0.0 copy-start
  88.8 0.0 all-reduce.5.cloned.1.call-start
  88.8 49.7 %all-reduce.3.cloned.1.call-done = f32[120,256]{1,0:T(8,128)} async-done(((f32[120,256]{1,0:T(8,128)}), f32[120,256]{1,0:T(8,128)}) %all-reduce.3.cloned.1.call-update) | async-done | bytes 122896 | tf_op jit(solution)/shard_map/psum | solution.py:53
  138.6 2.5 fusion.4
  141.1 0.0 copy-start.5
  141.1 4.5 %fusion.15 = f32[1,1,120,3456]{3,2,1,0:T(8,128)S(1)} fusion(f32[]{:T(128)} %bitcast.1, f32[120,3456]{1,0:T(8,128)S(1)} %fusion.4, f32[1,1,120,3456]{3,2,1,0:T(8,128)} %param.10, f32[1,1,120,3456]{3,2,1,0:T(8,128)} %param.11, f32[1,1,120,3456]{3,2,1,0:T(8,128)} %copy-done.4, f32[1,1,120,3456]{3,2,1,0:T(8,128)S(1)} %copy-done, f32[1,1,120,3456]{3,2,1,0:T(8,128)} %copy-done.3), kind=kLoop, calls=%fused_computation.20 | loop fusion | flops 7050240 | bytes 11612164 | tf_op jit(solution)/shard_map/broadcast_in_dim | solution.py:58
  145.6 2.5 collective-permute-start.7
  148.1 35.5 %collective-permute-start.3 = (f32[1,1]{1,0:T(1,128)}, f32[1,1]{1,0:T(1,128)}, u32[]{:S(2)}, u32[]{:S(2)}) collective-permute-start(f32[1,1]{1,0:T(1,128)} %div.50), channel_id=1, source_target_pairs={{4,0},{8,4},{12,8},{0,12},{5,1},{9,5},{13,9},{1,13},{6,2},{10,6},{... | collective-permute-start | bytes 20 | tf_op jit(solution)/shard_map/ppermute | solution.py:18
  183.6 0.7 collective-permute-start.2
  184.3 3.2 %collective-permute-done.2 = f32[1,1]{1,0:T(1,128)} collective-permute-done((f32[1,1]{1,0:T(1,128)}, f32[1,1]{1,0:T(1,128)}, u32[]{:S(2)}, u32[]{:S(2)}) %collective-permute-start.2) | collective-permute-done | bytes 36 | tf_op jit(solution)/shard_map/ppermute | solution.py:18
  188.8 0.0 copy-start.6
  188.8 0.0 copy-start.7
  188.8 1.1 copy-done.6
  190.0 0.5 copy-done.7
  190.5 2.4 fusion.2
  192.9 0.0 all-reduce.5.cloned.1.call-update
  193.0 43.8 %all-reduce.5.cloned.1.call-done = f32[120,256]{1,0:T(8,128)} async-done(((f32[120,256]{1,0:T(8,128)}), f32[120,256]{1,0:T(8,128)}) %all-reduce.5.cloned.1.call-update) | async-done | bytes 122896 | tf_op jit(solution)/shard_map/psum | solution.py:53
  236.8 8.4 %fusion.21 = (f32[1,1,120,3456]{3,2,1,0:T(8,128)}, f32[1,1,120,3456]{3,2,1,0:T(8,128)}, f32[1,1,120,3456]{3,2,1,0:T(8,128)}) fusion(f32[120,3456]{1,0:T(8,128)S(1)} %fusion.4, f32[1,1,120,3456]{3,2,1,0:T(8,128)S(1)} %copy-done.1, f32[1,1,120,3456]{3,2,1,0:T(8,128)} %param.10, f32[]{:T(128)} %bitcast, f32[1,1,120,3456]{3,2,1,0:T(8,128)} %copy-done.6, ...), kind=kOutput, calls=%fused_computation.29 | convolution fusion | flops 1284003840 | bytes 16946176 | tf_op jit(solution)/shard_map/ct,tf->cf/dot_general | solution.py:54
  (11 shorter events, 0.0 us)
Async XLA Ops:
  7.2 131.4 %all-reduce.3.cloned.1.call-start = ((), (), s32[]{:S(2)}) async-start(), calls=%async_computation | async-start | bytes 245760 | tf_op jit(solution)/shard_map/psum | solution.py:53
  7.2 75.4 %collective-permute-start.4 = (f32[1,1,120,3456]{3,2,1,0:T(8,128)}, f32[1,1,120,3456]{3,2,1,0:T(8,128)S(1)}, u32[]{:S(2)}, u32[]{:S(2)}) collective-permute-start(f32[1,1,120,3456]{3,2,1,0:T(8,128)} %param.6), channel_id=1, source_target_pairs={{240,0},{0,16},{16,32},{32,48},{48,64},{64,80},{80,96},{96,112},{1... | collective-permute-start | bytes 4976648 | tf_op jit(solution)/shard_map/ppermute | solution.py:18
  9.4 73.2 %collective-permute-start.5 = (f32[1,1,120,3456]{3,2,1,0:T(8,128)}, f32[1,1,120,3456]{3,2,1,0:T(8,128)S(1)}, u32[]{:S(2)}, u32[]{:S(2)}) collective-permute-start(f32[1,1,120,3456]{3,2,1,0:T(8,128)} %param.6), channel_id=1, source_target_pairs={{16,0},{32,16},{48,32},{64,48},{80,64},{96,80},{112,96},{128,112},... | collective-permute-start | bytes 4976648 | tf_op jit(solution)/shard_map/ppermute | solution.py:18
  14.8 65.2 %collective-permute-start = (f32[1,1]{1,0:T(1,128)}, f32[1,1]{1,0:T(1,128)}, u32[]{:S(2)}, u32[]{:S(2)}) collective-permute-start(f32[1,1]{1,0:T(1,128)} %param.7), channel_id=1, source_target_pairs={{240,0},{0,16},{16,32},{32,48},{48,64},{64,80},{80,96},{96,112},{1... | collective-permute-start | bytes 20 | tf_op jit(solution)/shard_map/ppermute | solution.py:18
  14.8 67.1 %collective-permute-start.1 = (f32[1,1]{1,0:T(1,128)}, f32[1,1]{1,0:T(1,128)}, u32[]{:S(2)}, u32[]{:S(2)}) collective-permute-start(f32[1,1]{1,0:T(1,128)} %param.7), channel_id=1, source_target_pairs={{16,0},{32,16},{48,32},{64,48},{80,64},{96,80},{112,96},{128,112},... | collective-permute-start | bytes 20 | tf_op jit(solution)/shard_map/ppermute | solution.py:18
  82.6 1.2 copy-start.3
  82.6 1.7 copy-start.4
  88.8 52.3 %copy-start = (f32[1,1,120,3456]{3,2,1,0:T(8,128)S(1)}, f32[1,1,120,3456]{3,2,1,0:T(8,128)}, u32[]{:S(2)}) copy-start(f32[1,1,120,3456]{3,2,1,0:T(8,128)} %param.6) | copy-start | bytes 4976644
  88.8 148.0 %all-reduce.5.cloned.1.call-start = ((), (), s32[]{:S(2)}) async-start(), calls=%async_computation.1 | async-start | bytes 245760 | tf_op jit(solution)/shard_map/psum | solution.py:53
  141.1 49.4 %copy-start.5 = (bf16[1,1,2,256,3456]{4,3,2,1,0:T(8,128)(2,1)S(1)}, bf16[1,1,2,256,3456]{4,3,2,1,0:T(8,128)(2,1)}, u32[]{:S(2)}) copy-start(bf16[1,1,2,256,3456]{4,3,2,1,0:T(8,128)(2,1)} %param.8) | copy-start | bytes 10616836
  145.6 43.2 %copy-start.2 = (f32[1,1,120,3456]{3,2,1,0:T(8,128)}, f32[1,1,120,3456]{3,2,1,0:T(8,128)S(1)}, u32[]{:S(2)}) copy-start(f32[1,1,120,3456]{3,2,1,0:T(8,128)S(1)} %fusion.15) | copy-start | bytes 4976644
  145.6 43.2 %collective-permute-start.7 = (f32[1,1,120,3456]{3,2,1,0:T(8,128)S(1)}, f32[1,1,120,3456]{3,2,1,0:T(8,128)S(1)}, u32[]{:S(2)}, u32[]{:S(2)}) collective-permute-start(f32[1,1,120,3456]{3,2,1,0:T(8,128)S(1)} %fusion.15), channel_id=1, source_target_pairs={{4,0},{8,4},{12,8},{0,12},{5,1},{9,5},{13,9},{1,13},{6,2},{10,6},{... | collective-permute-start | bytes 4976648 | tf_op jit(solution)/shard_map/ppermute | solution.py:18
  148.1 40.7 %collective-permute-start.6 = (f32[1,1,120,3456]{3,2,1,0:T(8,128)S(1)}, f32[1,1,120,3456]{3,2,1,0:T(8,128)S(1)}, u32[]{:S(2)}, u32[]{:S(2)}) collective-permute-start(f32[1,1,120,3456]{3,2,1,0:T(8,128)S(1)} %fusion.15), channel_id=1, source_target_pairs={{12,0},{0,4},{4,8},{8,12},{13,1},{1,5},{5,9},{9,13},{14,2},{2,6},{... | collective-permute-start | bytes 4976648 | tf_op jit(solution)/shard_map/ppermute | solution.py:18
  148.1 40.1 %collective-permute-start.3 = (f32[1,1]{1,0:T(1,128)}, f32[1,1]{1,0:T(1,128)}, u32[]{:S(2)}, u32[]{:S(2)}) collective-permute-start(f32[1,1]{1,0:T(1,128)} %div.50), channel_id=1, source_target_pairs={{4,0},{8,4},{12,8},{0,12},{5,1},{9,5},{13,9},{1,13},{6,2},{10,6},{... | collective-permute-start | bytes 20 | tf_op jit(solution)/shard_map/ppermute | solution.py:18
  183.6 3.9 %collective-permute-start.2 = (f32[1,1]{1,0:T(1,128)}, f32[1,1]{1,0:T(1,128)}, u32[]{:S(2)}, u32[]{:S(2)}) collective-permute-start(f32[1,1]{1,0:T(1,128)} %div.50), channel_id=1, source_target_pairs={{12,0},{0,4},{4,8},{8,12},{13,1},{1,5},{5,9},{9,13},{14,2},{2,6},{... | collective-permute-start | bytes 20 | tf_op jit(solution)/shard_map/ppermute | solution.py:18
  188.8 1.2 copy-start.6
  188.8 1.7 copy-start.7
  190.5 46.3 %copy-start.1 = (f32[1,1,120,3456]{3,2,1,0:T(8,128)S(1)}, f32[1,1,120,3456]{3,2,1,0:T(8,128)}, u32[]{:S(2)}) copy-start(f32[1,1,120,3456]{3,2,1,0:T(8,128)} %param.11) | copy-start | bytes 4976644
Sparse Core Ops, SparseCore 0:
  88.9 49.6 all-reduce.2
  193.1 43.6 all-reduce.4
where the time goes:
time: 253 us
  waiting for transfers between devices  159 us (63%)
  starting transfers between devices  50 us (20%)
  between operations  18.5 us (7%)
  matrix products  17.7 us (7%)
  other arithmetic  4.47 us (2%)
  local copies, waits for them, and re-layouts  3.39 us (1%)
    psum x2, waiting for transfers between devices, one_round(): predicted = lax.psum(partial_pred, 'ma')  93.6 us
    ppermute x8, waiting for transfers between devices, shifted(): return lax.ppermute(block, axis, route)  65.5 us
    ppermute x8, starting transfers between devices, shifted(): return lax.ppermute(block, axis, route)  49.9 us
    dot_general x2, matrix products, one_round(): jnp.einsum('ct,tf->cf', predicted - targets_round, inputs_round, precisio...  10.9 us
    dot_general x2, matrix products, one_round(): jnp.einsum('cf,tf->ct', params, inputs_round, precision=lax.Precision.HIG...  6.85 us
  transfers between devices with their start and end apart: 10, of which 5 were waited for; matrix products, arithmetic and copies ran while one was open for 0% of the time, Pallas kernels for 0%

commit v1 on v0

v1 whole, which is shorter than its diff:
```python
import functools

import jax
import jax.numpy as jnp
from jax import lax
from jax.experimental import pallas as pl
from jax.experimental.pallas import tpu as pltpu
from jax.sharding import PartitionSpec as P

PRIOR_STEPS = 100
BETA_ONE = 0.9
BETA_TWO = 0.999
LEARN_RATE = 0.05
EPSILON = 1e-08

GROUPS = ((32, 32), (32, 24))
TILE = 384


def send(block, axis, target):
    return lax.ppermute(block, axis, [(i, target(i)) for i in range(lax.axis_size(axis))])


def partner(i):
    return i ^ 1


def outward(count, i):
    return (i + 2) % count if i % 2 == 0 else (i - 2) % count


def inward(count, i):
    return (i - 2) % count if i % 2 == 0 else (i + 2) % count


def in_vmem(block):
    return pltpu.with_memory_space_constraint(block, pltpu.VMEM)


def two_parts(block):
    high = block.astype(jnp.bfloat16).astype(jnp.float32)
    return jnp.concatenate([high, block - high], axis=0).astype(jnp.bfloat16)


def fold(block):
    half = block.shape[0] // 2
    return block[:half] + block[half:]


def tiles(width):
    return [(start, min(TILE, width - start)) for start in range(0, width, TILE)]


def predict_kernel(round_number, terms, n_rows, *refs):
    inputs_ref, *operands = refs[:-2]
    total_ref, pred_ref = refs[-2:]
    pred = jnp.zeros((n_rows, inputs_ref.shape[3]), jnp.float32)
    for start, width in tiles(total_ref.shape[1]):
        lanes = pl.ds(start, width)
        pieces = []
        for count, parts in terms:
            piece = None
            for which, row in parts:
                part = operands[which][pl.ds(row, count), lanes]
                piece = part if piece is None else piece + part
            pieces.append(piece)
        block = pieces[0] if len(pieces) == 1 else jnp.concatenate(pieces, axis=0)
        total_ref[:, lanes] = block
        product = lax.dot_general(
            two_parts(block),
            inputs_ref[0, 0, round_number, :, lanes],
            (((1,), (1,)), ((), ())),
            preferred_element_type=jnp.float32,
        )
        pred = pred + fold(product)
    pred_ref[...] = pred


def predict(round_number, inputs, operands, terms):
    n_rows = sum(count for count, _ in terms)
    width = operands[0].shape[-1]
    tokens = inputs.shape[3]
    vmem = pl.BlockSpec(memory_space=pltpu.VMEM)
    return pl.pallas_call(
        functools.partial(predict_kernel, round_number, terms, n_rows),
        in_specs=[vmem] * (1 + len(operands)),
        out_specs=[vmem, vmem],
        out_shape=[pltpu.VMEM((n_rows, width), jnp.float32), pltpu.VMEM((n_rows, tokens), jnp.float32)],
        compiler_params=pltpu.CompilerParams(vmem_limit_bytes=16 * 1024 * 1024),
        cost_estimate=pl.CostEstimate(
            flops=4 * n_rows * tokens * width, bytes_accessed=1 << 20, transcendentals=0
        ),
        name=f"predict{round_number}",
    )(in_vmem(inputs), *[in_vmem(block) for block in operands])


def adam_tile(count, gradient, first, second, params):
    first = BETA_ONE * first + (1.0 - BETA_ONE) * gradient
    second = BETA_TWO * second + (1.0 - BETA_TWO) * gradient * gradient
    first_corr = 1.0 - BETA_ONE**count
    second_corr = 1.0 - BETA_TWO**count
    step = (first * (LEARN_RATE / first_corr)) / (jnp.sqrt(second * (1.0 / second_corr)) + EPSILON)
    return params - step, first, second


def update_tiles(round_number, row, moment_row, n_rows, refs, store):
    inputs_ref, targets_ref, first_ref, second_ref, total_ref, mine_ref, other_ref, scale_ref = refs
    scale = scale_ref[0:1, 0:1]
    inverse = 1.0 / scale
    residual = (mine_ref[...] + other_ref[...]) * inverse - targets_ref[0, 0, round_number, pl.ds(row, n_rows), :]
    residual = two_parts(residual)
    for start, width in tiles(total_ref.shape[1]):
        lanes = pl.ds(start, width)
        gradient = fold(
            jnp.dot(residual, inputs_ref[0, 0, round_number, :, lanes], preferred_element_type=jnp.float32)
        )
        rows = pl.ds(moment_row, n_rows)
        params, first, second = adam_tile(
            PRIOR_STEPS + round_number + 1,
            gradient,
            first_ref[rows, lanes],
            second_ref[rows, lanes],
            total_ref[:, lanes] * inverse,
        )
        store(start, width, (params * (scale * (1.0 / 3.0)), first, second))


def middle_kernel(row, n_rows, *refs):
    values_ref, first_out, second_out = refs[-3:]

    def store(start, width, blocks):
        for ref, block in zip((values_ref, first_out, second_out), blocks):
            ref[:, pl.ds(start, width)] = block

    update_tiles(0, row, row, n_rows, refs[:-3], store)


def last_kernel(row, n_rows, n_aliased, *refs):
    outs = refs[8 + n_aliased : 11 + n_aliased]
    held, sems = refs[-2:]
    copies = []

    def store(start, width, blocks):
        lanes = pl.ds(start, width)
        for which, (ref, block) in enumerate(zip(outs, blocks)):
            held[which, :, lanes] = block
            copy = pltpu.make_async_copy(
                held.at[which, :, lanes],
                ref.at[0, 0, pl.ds(row, n_rows), lanes],
                sems.at[which, start // TILE],
            )
            copy.start()
            copies.append(copy)

    update_tiles(1, row, 0, n_rows, refs[:8], store)
    for copy in copies:
        copy.wait()


def update_cost(n_rows, tokens, width):
    return pl.CostEstimate(flops=4 * n_rows * tokens * width, bytes_accessed=1 << 20, transcendentals=n_rows * width)


def update_middle(row, n_rows, operands):
    width = operands[4].shape[-1]
    vmem = pl.BlockSpec(memory_space=pltpu.VMEM)
    return pl.pallas_call(
        functools.partial(middle_kernel, row, n_rows),
        in_specs=[vmem] * 8,
        out_specs=[vmem] * 3,
        out_shape=[pltpu.VMEM((n_rows, width), jnp.float32)] * 3,
        compiler_params=pltpu.CompilerParams(vmem_limit_bytes=16 * 1024 * 1024),
        cost_estimate=update_cost(n_rows, operands[0].shape[3], width),
        name="update0",
    )(*[in_vmem(block) for block in operands])


def update_last(row, n_rows, operands, whole_shape, previous):
    width = operands[4].shape[-1]
    vmem = pl.BlockSpec(memory_space=pltpu.VMEM)
    anywhere = pl.BlockSpec(memory_space=pltpu.HBM)
    return pl.pallas_call(
        functools.partial(last_kernel, row, n_rows, len(previous)),
        in_specs=[vmem] * 8 + [anywhere] * len(previous),
        out_specs=[anywhere] * 3,
        out_shape=[jax.ShapeDtypeStruct(whole_shape, jnp.float32)] * 3,
        scratch_shapes=[
            pltpu.VMEM((3, n_rows, width), jnp.float32),
            pltpu.SemaphoreType.DMA((3, len(tiles(width)))),
        ],
        input_output_aliases={8 + which: which for which in range(len(previous))},
        compiler_params=pltpu.CompilerParams(vmem_limit_bytes=24 * 1024 * 1024),
        cost_estimate=update_cost(n_rows, operands[0].shape[3], width),
        name="update1",
    )(*[in_vmem(block) for block in operands], *previous)


def summed_over_ma(pred):
    pair = pred + send(pred, "ma", lambda i: i ^ 1)
    return pair, send(pair, "ma", lambda i: i ^ 2)


def neighbours(block, axis):
    count = lax.axis_size(axis)
    return send(block, axis, lambda i: (i + 1) % count), send(block, axis, lambda i: (i - 1) % count)


def local(numerator, weight, inputs, targets, first_moment, second_moment):
    row_count = lax.axis_size("rx")
    own = numerator[0, 0]
    first = first_moment[0, 0]
    second = second_moment[0, 0]

    before, after = neighbours(weight, "ry")
    three = jnp.concatenate([weight, before, after], axis=1)
    left, right = neighbours(three, "rx")
    sums = three + left + right
    row_sum = sums[:, 0:1]
    column_sum = (sums[:, 0:1] + sums[:, 1:2] + sums[:, 2:3]) / 3.0
    new_weight = column_sum / 3.0

    out_of = functools.partial(outward, row_count)
    into = functools.partial(inward, row_count)
    starts = []
    row = 0
    for count_a, count_b in GROUPS:
        starts.append(row)
        row += count_a + count_b
    received = []
    for (count_a, count_b), row in zip(GROUPS, starts):
        mid, end = row + count_a, row + count_a + count_b
        across = send(own[row:mid], "rx", partner)
        further = send(across, "rx", out_of)
        along = send(own[mid:end], "rx", into)
        pair_sum = send(own[mid:end] + along, "rx", partner)
        received.append((across, further, pair_sum))

    outs = ()
    results = []
    for (count_a, count_b), row, (across, further, pair_sum) in zip(GROUPS, starts, received):
        n_rows = count_a + count_b
        terms = (
            (count_a, ((0, row), (1, 0), (2, 0))),
            (count_b, ((0, row + count_a), (3, 0))),
        )
        total, pred = predict(0, inputs, (own, across, further, pair_sum), terms)
        mine, other = summed_over_ma(pred)
        values, first_mid, second_mid = update_middle(
            row, n_rows, (inputs, targets, first, second, total, mine, other, row_sum)
        )
        before, after = neighbours(values, "ry")
        results.append((values, before, after, first_mid, second_mid))

    for (count_a, count_b), row, (values, before, after, first_mid, second_mid) in zip(GROUPS, starts, results):
        n_rows = count_a + count_b
        terms = ((n_rows, ((0, 0), (1, 0), (2, 0))),)
        total, pred = predict(1, inputs, (values, before, after), terms)
        mine, other = summed_over_ma(pred)
        outs = update_last(
            row,
            n_rows,
            (inputs, targets, first_mid, second_mid, total, mine, other, column_sum),
            numerator.shape,
            outs,
        )
    new_numerator, new_first, new_second = outs
    return new_numerator, new_weight, new_first, new_second


def solution(mesh):
    rows = P("rx", "ry", None, "ma")
    return jax.shard_map(
        local,
        mesh=mesh,
        in_specs=(
            rows,
            P("rx", "ry"),
            P("rx", "ry", None, None, "ma"),
            P("rx", "ry", None, None, None),
            rows,
            rows,
        ),
        out_specs=(rows, P("rx", "ry"), rows, rows),
        check_vma=False,
    )
```

time: 253 us -> 114 us (0.45)
  waiting for transfers between devices: 159 us -> 50.5 us
  matrix products: 17.7 us -> 0 us
  between operations: 18.5 us -> 4.5 us
  Pallas kernels: 0 us -> 10.5 us
  starting transfers between devices: 50 us -> 43.6 us
    psum x2 -> x0, waiting for transfers between devices: 93.6 us -> none  [one_round(): predicted = lax.psum(partial_pred, 'ma')]
    dot_general x4 -> x0, matrix products: 17.7 us -> none  [the longest x2 10.9 us: one_round(): jnp.einsum('ct,tf->cf', predicted - targets_round, inputs_round, precisio...]
    ppermute x8 -> x24, waiting for transfers between devices: 65.5 us -> 50.5 us  [send(): lax.ppermute(block, axis, [(i, target(i)) for i in range(lax.axis_size(ax...]
    pallas_call x0 -> x8, Pallas kernels: none -> 10.5 us  [the longest x2 4.21 us: update_last(): pl.pallas_call(functools.partial(last_kernel, row, n_rows, len(previous))...]
    ppermute x8 -> x24, starting transfers between devices: 49.9 us -> 43.6 us  [send(): lax.ppermute(block, axis, [(i, target(i)) for i in range(lax.axis_size(ax...]
    broadcast_in_dim x1 -> x0, other arithmetic: 4.47 us -> none  [one_round(): values = (scales[0, 0] * params)[None, None]]
    unnamed x16 -> x10, local copies, waits for them, and re-layouts: 3.39 us -> 0.02 us
  transfers between devices with their start and end apart: 10 -> 24, of which waited for: 5 -> 12; matrix products, arithmetic and copies ran while one was open for 0% -> 4% of each run, Pallas kernels for 0% -> 7%
where the time goes in v1:
time: 114 us
  waiting for transfers between devices  50.5 us (44%)
  starting transfers between devices  43.6 us (38%)
  Pallas kernels  10.5 us (9%)
  between operations  4.5 us (4%)
  other arithmetic  2.69 us (2%)
  local copies, waits for them, and re-layouts  2.15 us (2%)
    ppermute x24, waiting for transfers between devices, send(): lax.ppermute(block, axis, [(i, target(i)) for i in range(lax.axis_size(ax...  50.5 us
    ppermute x24, starting transfers between devices, send(): lax.ppermute(block, axis, [(i, target(i)) for i in range(lax.axis_size(ax...  43.6 us
    pallas_call x2, Pallas kernels, update_last(): pl.pallas_call(functools.partial(last_kernel, row, n_rows, len(previous))...  4.21 us
    pallas_call x2, Pallas kernels, update_middle(): pl.pallas_call(functools.partial(middle_kernel, row, n_rows), in_specs=[v...  3.43 us
    pallas_call x4, Pallas kernels, predict(): pl.pallas_call(functools.partial(predict_kernel, round_number, terms, n_r...  2.81 us
  transfers between devices with their start and end apart: 24, of which 12 were waited for; matrix products, arithmetic and copies ran while one was open for 4% of the time, Pallas kernels for 7%

profile of v1, /device:TPU:1, one launch (start us, length us, event | category | flops | bytes accessed | tf_op | source)
XLA Modules:
  0.0 113.8 jit_solution(4465458031148366016)
XLA Ops:
  0.6 2.1 %collective-permute-start.6 = (f32[1,1]{1,0:T(1,128)}, f32[1,1]{1,0:T(1,128)}, u32[]{:S(2)}, u32[]{:S(2)}) collective-permute-start(f32[1,1]{1,0:T(1,128)} %param.7), channel_id=1, source_target_pairs={{0,4},{4,8},{8,12},{12,0},{1,5},{5,9},{9,13},{13,1},{2,6},{6,10},{... | collective-permute-start | bytes 20 | tf_op jit(solution)/shard_map/ppermute | solution.py:21
  2.8 1.4 %collective-permute-start.7 = (f32[1,1]{1,0:T(1,128)}, f32[1,1]{1,0:T(1,128)}, u32[]{:S(2)}, u32[]{:S(2)}) collective-permute-start(f32[1,1]{1,0:T(1,128)} %param.7), channel_id=1, source_target_pairs={{0,12},{4,0},{8,4},{12,8},{1,13},{5,1},{9,5},{13,9},{2,14},{6,2},{... | collective-permute-start | bytes 20 | tf_op jit(solution)/shard_map/ppermute | solution.py:21
  4.1 1.5 %slice_bitcast_fusion = (f32[32,3456]{1,0:T(8,128)S(1)}, f32[32,3456]{1,0:T(8,128)S(1)}, f32[32,3456]{1,0:T(8,128)S(1)}) fusion(f32[1,1,120,3456]{3,2,1,0:T(8,128)} %param.6), kind=kLoop, calls=%fused_computation | loop fusion | bytes 2654208 | tf_op jit(solution)/shard_map/slice | solution.py:235
  5.6 5.8 %collective-permute-start.16 = (f32[32,3456]{1,0:T(8,128)S(1)}, f32[32,3456]{1,0:T(8,128)S(1)}, u32[]{:S(2)}, u32[]{:S(2)}) collective-permute-start(f32[32,3456]{1,0:T(8,128)S(1)} %get-tuple-element.44), channel_id=1, source_target_pairs={{0,224},{16,48},{32,0},{48,80},{64,32},{80,112},{96,64},{112,144},... | collective-permute-start | bytes 1327112 | tf_op jit(solution)/shard_map/ppermute | solution.py:21
  12.9 1.5 %collective-permute-start.14 = (f32[32,3456]{1,0:T(8,128)S(1)}, f32[32,3456]{1,0:T(8,128)S(1)}, u32[]{:S(2)}, u32[]{:S(2)}) collective-permute-start(f32[32,3456]{1,0:T(8,128)S(1)} %get-tuple-element.46), channel_id=1, source_target_pairs={{0,16},{16,0},{32,48},{48,32},{64,80},{80,64},{96,112},{112,96},{1... | collective-permute-start | bytes 1327112 | tf_op jit(solution)/shard_map/ppermute | solution.py:21
  16.2 3.4 %collective-permute-done.16 = f32[32,3456]{1,0:T(8,128)S(1)} collective-permute-done((f32[32,3456]{1,0:T(8,128)S(1)}, f32[32,3456]{1,0:T(8,128)S(1)}, u32[]{:S(2)}, u32[]{:S(2)}) %collective-permute-start.16) | collective-permute-done | bytes 442400 | tf_op jit(solution)/shard_map/ppermute | solution.py:21
  19.6 2.3 %collective-permute-start.8 = (f32[1,3]{1,0:T(1,128)S(1)}, f32[1,3]{1,0:T(1,128)S(1)}, u32[]{:S(2)}, u32[]{:S(2)}) collective-permute-start(f32[1,3]{1,0:T(1,128)S(1)} %pad_maximum_fusion), channel_id=1, source_target_pairs={{0,16},{16,32},{32,48},{48,64},{64,80},{80,96},{96,112},{112,128},... | collective-permute-start | bytes 44 | tf_op jit(solution)/shard_map/ppermute | solution.py:21
  22.0 4.7 %collective-permute-done.2 = f32[24,3456]{1,0:T(8,128)S(1)} collective-permute-done((f32[24,3456]{1,0:T(8,128)S(1)}, f32[24,3456]{1,0:T(8,128)S(1)}, u32[]{:S(2)}, u32[]{:S(2)}) %collective-permute-start.2) | collective-permute-done | bytes 331808 | tf_op jit(solution)/shard_map/ppermute | solution.py:21
  26.7 2.3 %collective-permute-start.17 = (f32[32,3456]{1,0:T(8,128)S(1)}, f32[32,3456]{1,0:T(8,128)S(1)}, u32[]{:S(2)}, u32[]{:S(2)}) collective-permute-start(f32[32,3456]{1,0:T(8,128)S(1)} %fusion.1), channel_id=1, source_target_pairs={{0,16},{16,0},{32,48},{48,32},{64,80},{80,64},{96,112},{112,96},{1... | collective-permute-start | bytes 1327112 | tf_op jit(solution)/shard_map/ppermute | solution.py:21
  29.1 2.5 %collective-permute-done.14.refs_2_ = f32[32,3456]{1,0:T(8,128)S(1)} collective-permute-done((f32[32,3456]{1,0:T(8,128)S(1)}, f32[32,3456]{1,0:T(8,128)S(1)}, u32[]{:S(2)}, u32[]{:S(2)}) %collective-permute-start.14) | collective-permute-done | bytes 442400 | tf_op jit(solution)/shard_map/ppermute | solution.py:21
  32.4 8.7 %collective-permute-done.17.refs_4_ = f32[32,3456]{1,0:T(8,128)S(1)} collective-permute-done((f32[32,3456]{1,0:T(8,128)S(1)}, f32[32,3456]{1,0:T(8,128)S(1)}, u32[]{:S(2)}, u32[]{:S(2)}) %collective-permute-start.17) | collective-permute-done | bytes 442400 | tf_op jit(solution)/shard_map/ppermute | solution.py:21
  41.4 7.9 %collective-permute-done.15.refs_3_ = f32[32,3456]{1,0:T(8,128)S(1)} collective-permute-done((f32[32,3456]{1,0:T(8,128)S(1)}, f32[32,3456]{1,0:T(8,128)S(1)}, u32[]{:S(2)}, u32[]{:S(2)}) %collective-permute-start.15) | collective-permute-done | bytes 442400 | tf_op jit(solution)/shard_map/ppermute | solution.py:21
  50.0 3.2 %collective-permute-start.18 = (f32[64,256]{1,0:T(8,128)S(1)}, f32[64,256]{1,0:T(8,128)S(1)}, u32[]{:S(2)}, u32[]{:S(2)}) collective-permute-start(f32[64,256]{1,0:T(8,128)S(1)} %get-tuple-element.32), channel_id=1, source_target_pairs={{0,1},{1,0},{2,3},{3,2},{4,5},{5,4},{6,7},{7,6},{8,9},{9,8},{10,11... | collective-permute-start | bytes 196616 | tf_op jit(solution)/shard_map/ppermute | solution.py:21
  53.2 1.3 %add_add_fusion = f32[1,3]{1,0:T(1,128)S(1)} fusion(f32[1,3]{1,0:T(1,128)S(1)} %collective-permute-done.9, f32[1,3]{1,0:T(1,128)S(1)} %collective-permute-done.8, f32[1,1]{1,0:T(1,128)} %collective-permute-done.7, f32[1,1]{1,0:T(1,128)} %collective-permute-done.6, f32[1,1]{1,0:T(1,128)S(6)} %copy.16), kind=kLoop, calls=%fused_computation.5 | loop fusion | flops 12 | bytes 48 | tf_op jit(solution)/shard_map/add | solution.py:217
  54.4 2.7 %collective-permute-start.19 = (f32[64,256]{1,0:T(8,128)S(1)}, f32[64,256]{1,0:T(8,128)S(1)}, u32[]{:S(2)}, u32[]{:S(2)}) collective-permute-start(f32[64,256]{1,0:T(8,128)S(1)} %add.38.refs_5_), channel_id=1, source_target_pairs={{0,2},{1,3},{2,0},{3,1},{4,6},{5,7},{6,4},{7,5},{8,10},{9,11},{10,... | collective-permute-start | bytes 196616 | tf_op jit(solution)/shard_map/ppermute | solution.py:21
  57.7 1.4 %collective-permute-done.19.refs_6_ = f32[64,256]{1,0:T(8,128)S(1)} collective-permute-done((f32[64,256]{1,0:T(8,128)S(1)}, f32[64,256]{1,0:T(8,128)S(1)}, u32[]{:S(2)}, u32[]{:S(2)}) %collective-permute-start.19) | collective-permute-done | bytes 65568 | tf_op jit(solution)/shard_map/ppermute | solution.py:21
  59.2 1.8 %update0.3 = (f32[64,3456]{1,0:T(8,128)S(1)}, f32[64,3456]{1,0:T(8,128)S(1)}, f32[64,3456]{1,0:T(8,128)S(1)}) custom-call(bf16[1,1,2,256,3456]{4,3,2,1,0:T(8,128)(2,1)S(1)} %copy-done, f32[1,1,2,120,256]{4,3,2,1,0:T(8,128)S(1)} %copy-done.4, f32[120,3456]{1,0:T(8,128)S(1)} %bitcast.17, f32[120,3456]{1,0:T(8,128)S(1)} %bitcast.19, ...), custom_call_target="tpu_custom_call" | custom-call | flops 226492416 | bytes 1048576 | tf_op jit(solution)/shard_map/update0/pallas_call | solution.py:167
  60.9 1.3 %collective-permute-start.21 = (f32[64,3456]{1,0:T(8,128)S(1)}, f32[64,3456]{1,0:T(8,128)S(1)}, u32[]{:S(2)}, u32[]{:S(2)}) collective-permute-start(f32[64,3456]{1,0:T(8,128)S(1)} %get-tuple-element.35.refs_1_), channel_id=1, source_target_pairs={{0,12},{4,0},{8,4},{12,8},{1,13},{5,1},{9,5},{13,9},{2,14},{6,2},{... | collective-permute-start | bytes 2654216 | tf_op jit(solution)/shard_map/ppermute | solution.py:21
  63.2 2.1 %collective-permute-start.4 = (f32[56,256]{1,0:T(8,128)S(1)}, f32[56,256]{1,0:T(8,128)S(1)}, u32[]{:S(2)}, u32[]{:S(2)}) collective-permute-start(f32[56,256]{1,0:T(8,128)S(1)} %get-tuple-element.25), channel_id=1, source_target_pairs={{0,1},{1,0},{2,3},{3,2},{4,5},{5,4},{6,7},{7,6},{8,9},{9,8},{10,11... | collective-permute-start | bytes 172040 | tf_op jit(solution)/shard_map/ppermute | solution.py:21
  66.1 2.7 %collective-permute-start.5 = (f32[56,256]{1,0:T(8,128)S(1)}, f32[56,256]{1,0:T(8,128)S(1)}, u32[]{:S(2)}, u32[]{:S(2)}) collective-permute-start(f32[56,256]{1,0:T(8,128)S(1)} %add.31.refs_5_), channel_id=1, source_target_pairs={{0,2},{1,3},{2,0},{3,1},{4,6},{5,7},{6,4},{7,5},{8,10},{9,11},{10,... | collective-permute-start | bytes 172040 | tf_op jit(solution)/shard_map/ppermute | solution.py:21
  68.8 1.9 %collective-permute-done.5.refs_6_ = f32[56,256]{1,0:T(8,128)S(1)} collective-permute-done((f32[56,256]{1,0:T(8,128)S(1)}, f32[56,256]{1,0:T(8,128)S(1)}, u32[]{:S(2)}, u32[]{:S(2)}) %collective-permute-start.5) | collective-permute-done | bytes 57376 | tf_op jit(solution)/shard_map/ppermute | solution.py:21
  70.7 1.7 %update0.2 = (f32[56,3456]{1,0:T(8,128)S(1)}, f32[56,3456]{1,0:T(8,128)S(1)}, f32[56,3456]{1,0:T(8,128)S(1)}) custom-call(bf16[1,1,2,256,3456]{4,3,2,1,0:T(8,128)(2,1)S(1)} %copy-done, f32[1,1,2,120,256]{4,3,2,1,0:T(8,128)S(1)} %copy-done.4, f32[120,3456]{1,0:T(8,128)S(1)} %bitcast.18, f32[120,3456]{1,0:T(8,128)S(1)} %bitcast.20, ...), custom_call_target="tpu_custom_call" | custom-call | flops 198180864 | bytes 1048576 | tf_op jit(solution)/shard_map/update0/pallas_call | solution.py:167
  72.4 2.6 %collective-permute-start.11 = (f32[56,3456]{1,0:T(8,128)S(1)}, f32[56,3456]{1,0:T(8,128)S(1)}, u32[]{:S(2)}, u32[]{:S(2)}) collective-permute-start(f32[56,3456]{1,0:T(8,128)S(1)} %get-tuple-element.28.refs_1_), channel_id=1, source_target_pairs={{0,12},{4,0},{8,4},{12,8},{1,13},{5,1},{9,5},{13,9},{2,14},{6,2},{... | collective-permute-start | bytes 2322440 | tf_op jit(solution)/shard_map/ppermute | solution.py:21
  74.9 5.8 %collective-permute-done.21.refs_3_ = f32[64,3456]{1,0:T(8,128)S(1)} collective-permute-done((f32[64,3456]{1,0:T(8,128)S(1)}, f32[64,3456]{1,0:T(8,128)S(1)}, u32[]{:S(2)}, u32[]{:S(2)}) %collective-permute-start.21) | collective-permute-done | bytes 884768 | tf_op jit(solution)/shard_map/ppermute | solution.py:21
  80.7 2.2 %collective-permute-done.20.refs_2_ = f32[64,3456]{1,0:T(8,128)S(1)} collective-permute-done((f32[64,3456]{1,0:T(8,128)S(1)}, f32[64,3456]{1,0:T(8,128)S(1)}, u32[]{:S(2)}, u32[]{:S(2)}) %collective-permute-start.20) | collective-permute-done | bytes 884768 | tf_op jit(solution)/shard_map/ppermute | solution.py:21
  83.7 4.9 %collective-permute-start.22 = (f32[64,256]{1,0:T(8,128)S(1)}, f32[64,256]{1,0:T(8,128)S(1)}, u32[]{:S(2)}, u32[]{:S(2)}) collective-permute-start(f32[64,256]{1,0:T(8,128)S(1)} %get-tuple-element.37), channel_id=1, source_target_pairs={{0,1},{1,0},{2,3},{3,2},{4,5},{5,4},{6,7},{7,6},{8,9},{9,8},{10,11... | collective-permute-start | bytes 196616 | tf_op jit(solution)/shard_map/ppermute | solution.py:21
  88.6 8.8 %collective-permute-done.11.refs_3_ = f32[56,3456]{1,0:T(8,128)S(1)} collective-permute-done((f32[56,3456]{1,0:T(8,128)S(1)}, f32[56,3456]{1,0:T(8,128)S(1)}, u32[]{:S(2)}, u32[]{:S(2)}) %collective-permute-start.11) | collective-permute-done | bytes 774176 | tf_op jit(solution)/shard_map/ppermute | solution.py:21
  97.3 2.2 %collective-permute-done.10.refs_2_ = f32[56,3456]{1,0:T(8,128)S(1)} collective-permute-done((f32[56,3456]{1,0:T(8,128)S(1)}, f32[56,3456]{1,0:T(8,128)S(1)}, u32[]{:S(2)}, u32[]{:S(2)}) %collective-permute-start.10) | collective-permute-done | bytes 774176 | tf_op jit(solution)/shard_map/ppermute | solution.py:21
  100.2 2.7 %collective-permute-start.12 = (f32[56,256]{1,0:T(8,128)S(1)}, f32[56,256]{1,0:T(8,128)S(1)}, u32[]{:S(2)}, u32[]{:S(2)}) collective-permute-start(f32[56,256]{1,0:T(8,128)S(1)} %get-tuple-element.30), channel_id=1, source_target_pairs={{0,1},{1,0},{2,3},{3,2},{4,5},{5,4},{6,7},{7,6},{8,9},{9,8},{10,11... | collective-permute-start | bytes 172040 | tf_op jit(solution)/shard_map/ppermute | solution.py:21
  103.0 2.7 %collective-permute-start.23 = (f32[64,256]{1,0:T(8,128)S(1)}, f32[64,256]{1,0:T(8,128)S(1)}, u32[]{:S(2)}, u32[]{:S(2)}) collective-permute-start(f32[64,256]{1,0:T(8,128)S(1)} %add.39.refs_5_), channel_id=1, source_target_pairs={{0,2},{1,3},{2,0},{3,1},{4,6},{5,7},{6,4},{7,5},{8,10},{9,11},{10,... | collective-permute-start | bytes 196616 | tf_op jit(solution)/shard_map/ppermute | solution.py:21
  108.5 2.2 %update1.2 = (f32[1,1,120,3456]{3,2,1,0:T(8,128)}, f32[1,1,120,3456]{3,2,1,0:T(8,128)}, f32[1,1,120,3456]{3,2,1,0:T(8,128)}) custom-call(bf16[1,1,2,256,3456]{4,3,2,1,0:T(8,128)(2,1)S(1)} %copy-done, f32[1,1,2,120,256]{4,3,2,1,0:T(8,128)S(1)} %copy-done.4, f32[64,3456]{1,0:T(8,128)S(1)} %get-tuple-element.33.refs_2_, ...), custom_call_target="tpu_custom_call" | custom-call | flops 226492416 | bytes 1048576 | tf_op jit(solution)/shard_map/update1/pallas_call | solution.py:182
  110.7 2.0 %update1.3 = (f32[1,1,120,3456]{3,2,1,0:T(8,128)}, f32[1,1,120,3456]{3,2,1,0:T(8,128)}, f32[1,1,120,3456]{3,2,1,0:T(8,128)}) custom-call(bf16[1,1,2,256,3456]{4,3,2,1,0:T(8,128)(2,1)S(1)} %copy-done, f32[1,1,2,120,256]{4,3,2,1,0:T(8,128)S(1)} %copy-done.4, ...), custom_call_target="tpu_custom_call", output_to_operand_aliasing={{0}: (8, {}), {1}: (9, {}), {2}: (10, {})} | custom-call | flops 198180864 | bytes 1048576 | tf_op jit(solution)/shard_map/update1/pallas_call | solution.py:182
  (45 shorter events, 9.1 us)
Async XLA Ops:
  0.6 10.8 %copy-start.1 = (f32[1,1,120,3456]{3,2,1,0:T(8,128)S(1)}, f32[1,1,120,3456]{3,2,1,0:T(8,128)}, u32[]{:S(2)}) copy-start(f32[1,1,120,3456]{3,2,1,0:T(8,128)} %param.6) | copy-start | bytes 4976644
  0.6 12.2 %collective-permute-start.6 = (f32[1,1]{1,0:T(1,128)}, f32[1,1]{1,0:T(1,128)}, u32[]{:S(2)}, u32[]{:S(2)}) collective-permute-start(f32[1,1]{1,0:T(1,128)} %param.7), channel_id=1, source_target_pairs={{0,4},{4,8},{8,12},{12,0},{1,5},{5,9},{9,13},{13,1},{2,6},{6,10},{... | collective-permute-start | bytes 20 | tf_op jit(solution)/shard_map/ppermute | solution.py:21
  2.8 11.7 %collective-permute-start.7 = (f32[1,1]{1,0:T(1,128)}, f32[1,1]{1,0:T(1,128)}, u32[]{:S(2)}, u32[]{:S(2)}) collective-permute-start(f32[1,1]{1,0:T(1,128)} %param.7), channel_id=1, source_target_pairs={{0,12},{4,0},{8,4},{12,8},{1,13},{5,1},{9,5},{13,9},{2,14},{6,2},{... | collective-permute-start | bytes 20 | tf_op jit(solution)/shard_map/ppermute | solution.py:21
  4.1 45.1 %copy-start = (bf16[1,1,2,256,3456]{4,3,2,1,0:T(8,128)(2,1)S(1)}, bf16[1,1,2,256,3456]{4,3,2,1,0:T(8,128)(2,1)}, u32[]{:S(2)}) copy-start(bf16[1,1,2,256,3456]{4,3,2,1,0:T(8,128)(2,1)} %refs_0_.15) | copy-start | bytes 10616836
  5.6 14.0 %collective-permute-start.16 = (f32[32,3456]{1,0:T(8,128)S(1)}, f32[32,3456]{1,0:T(8,128)S(1)}, u32[]{:S(2)}, u32[]{:S(2)}) collective-permute-start(f32[32,3456]{1,0:T(8,128)S(1)} %get-tuple-element.44), channel_id=1, source_target_pairs={{0,224},{16,48},{32,0},{48,80},{64,32},{80,112},{96,64},{112,144},... | collective-permute-start | bytes 1327112 | tf_op jit(solution)/shard_map/ppermute | solution.py:21
  11.4 15.3 %collective-permute-start.2 = (f32[24,3456]{1,0:T(8,128)S(1)}, f32[24,3456]{1,0:T(8,128)S(1)}, u32[]{:S(2)}, u32[]{:S(2)}) collective-permute-start(f32[24,3456]{1,0:T(8,128)S(1)} %slice_bitcast_fusion.3), channel_id=1, source_target_pairs={{0,224},{16,48},{32,0},{48,80},{64,32},{80,112},{96,64},{112,144},... | collective-permute-start | bytes 995336 | tf_op jit(solution)/shard_map/ppermute | solution.py:21
  12.2 16.8 %collective-permute-start = (f32[32,3456]{1,0:T(8,128)S(1)}, f32[32,3456]{1,0:T(8,128)S(1)}, u32[]{:S(2)}, u32[]{:S(2)}) collective-permute-start(f32[32,3456]{1,0:T(8,128)S(1)} %get-tuple-element.45), channel_id=1, source_target_pairs={{0,16},{16,0},{32,48},{48,32},{64,80},{80,64},{96,112},{112,96},{1... | collective-permute-start | bytes 1327112 | tf_op jit(solution)/shard_map/ppermute | solution.py:21
  12.9 18.7 %collective-permute-start.14 = (f32[32,3456]{1,0:T(8,128)S(1)}, f32[32,3456]{1,0:T(8,128)S(1)}, u32[]{:S(2)}, u32[]{:S(2)}) collective-permute-start(f32[32,3456]{1,0:T(8,128)S(1)} %get-tuple-element.46), channel_id=1, source_target_pairs={{0,16},{16,0},{32,48},{48,32},{64,80},{80,64},{96,112},{112,96},{1... | collective-permute-start | bytes 1327112 | tf_op jit(solution)/shard_map/ppermute | solution.py:21
  15.7 37.4 %collective-permute-start.9 = (f32[1,3]{1,0:T(1,128)S(1)}, f32[1,3]{1,0:T(1,128)S(1)}, u32[]{:S(2)}, u32[]{:S(2)}) collective-permute-start(f32[1,3]{1,0:T(1,128)S(1)} %pad_maximum_fusion), channel_id=1, source_target_pairs={{0,240},{16,0},{32,16},{48,32},{64,48},{80,64},{96,80},{112,96},{1... | collective-permute-start | bytes 44 | tf_op jit(solution)/shard_map/ppermute | solution.py:21
  19.6 33.5 %collective-permute-start.8 = (f32[1,3]{1,0:T(1,128)S(1)}, f32[1,3]{1,0:T(1,128)S(1)}, u32[]{:S(2)}, u32[]{:S(2)}) collective-permute-start(f32[1,3]{1,0:T(1,128)S(1)} %pad_maximum_fusion), channel_id=1, source_target_pairs={{0,16},{16,32},{32,48},{48,64},{64,80},{80,96},{96,112},{112,128},... | collective-permute-start | bytes 44 | tf_op jit(solution)/shard_map/ppermute | solution.py:21
  26.7 14.3 %collective-permute-start.17 = (f32[32,3456]{1,0:T(8,128)S(1)}, f32[32,3456]{1,0:T(8,128)S(1)}, u32[]{:S(2)}, u32[]{:S(2)}) collective-permute-start(f32[32,3456]{1,0:T(8,128)S(1)} %fusion.1), channel_id=1, source_target_pairs={{0,16},{16,0},{32,48},{48,32},{64,80},{80,64},{96,112},{112,96},{1... | collective-permute-start | bytes 1327112 | tf_op jit(solution)/shard_map/ppermute | solution.py:21
  29.1 33.4 %collective-permute-start.1 = (f32[32,3456]{1,0:T(8,128)S(1)}, f32[32,3456]{1,0:T(8,128)S(1)}, u32[]{:S(2)}, u32[]{:S(2)}) collective-permute-start(f32[32,3456]{1,0:T(8,128)S(1)} %collective-permute-done.refs_2_), channel_id=1, source_target_pairs={{0,32},{16,240},{32,64},{48,16},{64,96},{80,48},{96,128},{112,80},... | collective-permute-start | bytes 1327112 | tf_op jit(solution)/shard_map/ppermute | solution.py:21
  31.6 17.7 %collective-permute-start.15 = (f32[32,3456]{1,0:T(8,128)S(1)}, f32[32,3456]{1,0:T(8,128)S(1)}, u32[]{:S(2)}, u32[]{:S(2)}) collective-permute-start(f32[32,3456]{1,0:T(8,128)S(1)} %collective-permute-done.14.refs_2_), channel_id=1, source_target_pairs={{0,32},{16,240},{32,64},{48,16},{64,96},{80,48},{96,128},{112,80},... | collective-permute-start | bytes 1327112 | tf_op jit(solution)/shard_map/ppermute | solution.py:21
  41.1 21.4 %collective-permute-start.3 = (f32[24,3456]{1,0:T(8,128)S(1)}, f32[24,3456]{1,0:T(8,128)S(1)}, u32[]{:S(2)}, u32[]{:S(2)}) collective-permute-start(f32[24,3456]{1,0:T(8,128)S(1)} %fusion), channel_id=1, source_target_pairs={{0,16},{16,0},{32,48},{48,32},{64,80},{80,64},{96,112},{112,96},{1... | collective-permute-start | bytes 995336 | tf_op jit(solution)/shard_map/ppermute | solution.py:21
  49.3 9.9 %copy-start.2 = (f32[1,1,120,3456]{3,2,1,0:T(8,128)S(1)}, f32[1,1,120,3456]{3,2,1,0:T(8,128)}, u32[]{:S(2)}) copy-start(f32[1,1,120,3456]{3,2,1,0:T(8,128)} %param.10) | copy-start | bytes 4976644
  49.3 9.9 %copy-start.3 = (f32[1,1,120,3456]{3,2,1,0:T(8,128)S(1)}, f32[1,1,120,3456]{3,2,1,0:T(8,128)}, u32[]{:S(2)}) copy-start(f32[1,1,120,3456]{3,2,1,0:T(8,128)} %param.11) | copy-start | bytes 4976644
  49.3 9.9 %copy-start.4 = (f32[1,1,2,120,256]{4,3,2,1,0:T(8,128)S(1)}, f32[1,1,2,120,256]{4,3,2,1,0:T(8,128)}, u32[]{:S(2)}) copy-start(f32[1,1,2,120,256]{4,3,2,1,0:T(8,128)} %refs_1_.7) | copy-start | bytes 737284
  50.0 4.4 %collective-permute-start.18 = (f32[64,256]{1,0:T(8,128)S(1)}, f32[64,256]{1,0:T(8,128)S(1)}, u32[]{:S(2)}, u32[]{:S(2)}) collective-permute-start(f32[64,256]{1,0:T(8,128)S(1)} %get-tuple-element.32), channel_id=1, source_target_pairs={{0,1},{1,0},{2,3},{3,2},{4,5},{5,4},{6,7},{7,6},{8,9},{9,8},{10,11... | collective-permute-start | bytes 196616 | tf_op jit(solution)/shard_map/ppermute | solution.py:21
  54.4 4.7 %collective-permute-start.19 = (f32[64,256]{1,0:T(8,128)S(1)}, f32[64,256]{1,0:T(8,128)S(1)}, u32[]{:S(2)}, u32[]{:S(2)}) collective-permute-start(f32[64,256]{1,0:T(8,128)S(1)} %add.38.refs_5_), channel_id=1, source_target_pairs={{0,2},{1,3},{2,0},{3,1},{4,6},{5,7},{6,4},{7,5},{8,10},{9,11},{10,... | collective-permute-start | bytes 196616 | tf_op jit(solution)/shard_map/ppermute | solution.py:21
  60.9 19.8 %collective-permute-start.21 = (f32[64,3456]{1,0:T(8,128)S(1)}, f32[64,3456]{1,0:T(8,128)S(1)}, u32[]{:S(2)}, u32[]{:S(2)}) collective-permute-start(f32[64,3456]{1,0:T(8,128)S(1)} %get-tuple-element.35.refs_1_), channel_id=1, source_target_pairs={{0,12},{4,0},{8,4},{12,8},{1,13},{5,1},{9,5},{13,9},{2,14},{6,2},{... | collective-permute-start | bytes 2654216 | tf_op jit(solution)/shard_map/ppermute | solution.py:21
  62.3 20.7 %collective-permute-start.20 = (f32[64,3456]{1,0:T(8,128)S(1)}, f32[64,3456]{1,0:T(8,128)S(1)}, u32[]{:S(2)}, u32[]{:S(2)}) collective-permute-start(f32[64,3456]{1,0:T(8,128)S(1)} %get-tuple-element.35.refs_1_), channel_id=1, source_target_pairs={{0,4},{4,8},{8,12},{12,0},{1,5},{5,9},{9,13},{13,1},{2,6},{6,10},{... | collective-permute-start | bytes 2654216 | tf_op jit(solution)/shard_map/ppermute | solution.py:21
  63.2 2.9 %collective-permute-start.4 = (f32[56,256]{1,0:T(8,128)S(1)}, f32[56,256]{1,0:T(8,128)S(1)}, u32[]{:S(2)}, u32[]{:S(2)}) collective-permute-start(f32[56,256]{1,0:T(8,128)S(1)} %get-tuple-element.25), channel_id=1, source_target_pairs={{0,1},{1,0},{2,3},{3,2},{4,5},{5,4},{6,7},{7,6},{8,9},{9,8},{10,11... | collective-permute-start | bytes 172040 | tf_op jit(solution)/shard_map/ppermute | solution.py:21
  66.1 4.6 %collective-permute-start.5 = (f32[56,256]{1,0:T(8,128)S(1)}, f32[56,256]{1,0:T(8,128)S(1)}, u32[]{:S(2)}, u32[]{:S(2)}) collective-permute-start(f32[56,256]{1,0:T(8,128)S(1)} %add.31.refs_5_), channel_id=1, source_target_pairs={{0,2},{1,3},{2,0},{3,1},{4,6},{5,7},{6,4},{7,5},{8,10},{9,11},{10,... | collective-permute-start | bytes 172040 | tf_op jit(solution)/shard_map/ppermute | solution.py:21
  72.4 24.9 %collective-permute-start.11 = (f32[56,3456]{1,0:T(8,128)S(1)}, f32[56,3456]{1,0:T(8,128)S(1)}, u32[]{:S(2)}, u32[]{:S(2)}) collective-permute-start(f32[56,3456]{1,0:T(8,128)S(1)} %get-tuple-element.28.refs_1_), channel_id=1, source_target_pairs={{0,12},{4,0},{8,4},{12,8},{1,13},{5,1},{9,5},{13,9},{2,14},{6,2},{... | collective-permute-start | bytes 2322440 | tf_op jit(solution)/shard_map/ppermute | solution.py:21
  74.9 24.6 %collective-permute-start.10 = (f32[56,3456]{1,0:T(8,128)S(1)}, f32[56,3456]{1,0:T(8,128)S(1)}, u32[]{:S(2)}, u32[]{:S(2)}) collective-permute-start(f32[56,3456]{1,0:T(8,128)S(1)} %get-tuple-element.28.refs_1_), channel_id=1, source_target_pairs={{0,4},{4,8},{8,12},{12,0},{1,5},{5,9},{9,13},{13,1},{2,6},{6,10},{... | collective-permute-start | bytes 2322440 | tf_op jit(solution)/shard_map/ppermute | solution.py:21
  83.7 19.3 %collective-permute-start.22 = (f32[64,256]{1,0:T(8,128)S(1)}, f32[64,256]{1,0:T(8,128)S(1)}, u32[]{:S(2)}, u32[]{:S(2)}) collective-permute-start(f32[64,256]{1,0:T(8,128)S(1)} %get-tuple-element.37), channel_id=1, source_target_pairs={{0,1},{1,0},{2,3},{3,2},{4,5},{5,4},{6,7},{7,6},{8,9},{9,8},{10,11... | collective-permute-start | bytes 196616 | tf_op jit(solution)/shard_map/ppermute | solution.py:21
  100.2 5.4 %collective-permute-start.12 = (f32[56,256]{1,0:T(8,128)S(1)}, f32[56,256]{1,0:T(8,128)S(1)}, u32[]{:S(2)}, u32[]{:S(2)}) collective-permute-start(f32[56,256]{1,0:T(8,128)S(1)} %get-tuple-element.30), channel_id=1, source_target_pairs={{0,1},{1,0},{2,3},{3,2},{4,5},{5,4},{6,7},{7,6},{8,9},{9,8},{10,11... | collective-permute-start | bytes 172040 | tf_op jit(solution)/shard_map/ppermute | solution.py:21
  103.0 5.5 %collective-permute-start.23 = (f32[64,256]{1,0:T(8,128)S(1)}, f32[64,256]{1,0:T(8,128)S(1)}, u32[]{:S(2)}, u32[]{:S(2)}) collective-permute-start(f32[64,256]{1,0:T(8,128)S(1)} %add.39.refs_5_), channel_id=1, source_target_pairs={{0,2},{1,3},{2,0},{3,1},{4,6},{5,7},{6,4},{7,5},{8,10},{9,11},{10,... | collective-permute-start | bytes 196616 | tf_op jit(solution)/shard_map/ppermute | solution.py:21
  105.7 5.0 %collective-permute-start.13 = (f32[56,256]{1,0:T(8,128)S(1)}, f32[56,256]{1,0:T(8,128)S(1)}, u32[]{:S(2)}, u32[]{:S(2)}) collective-permute-start(f32[56,256]{1,0:T(8,128)S(1)} %add.34.refs_5_), channel_id=1, source_target_pairs={{0,2},{1,3},{2,0},{3,1},{4,6},{5,7},{6,4},{7,5},{8,10},{9,11},{10,... | collective-permute-start | bytes 172040 | tf_op jit(solution)/shard_map/ppermute | solution.py:21

commit v2 on v1

v2 whole, which is shorter than its diff:
```python
import functools

import jax
import jax.numpy as jnp
from jax import lax
from jax.experimental import pallas as pl
from jax.experimental.pallas import tpu as pltpu
from jax.sharding import PartitionSpec as P

PRIOR_STEPS = 100
BETA_ONE = 0.9
BETA_TWO = 0.999
LEARN_RATE = 0.05
EPSILON = 1e-08

GROUPS = ((32, 32), (24, 32))
BATCHES = ((0,), (1,))
TILE = 384
LANE_TILES = 27


def send(block, axis, target):
    return lax.ppermute(block, axis, [(i, target(i)) for i in range(lax.axis_size(axis))])


def partner(i):
    return i ^ 1


def outward(count, i):
    return (i + 2) % count if i % 2 == 0 else (i - 2) % count


def inward(count, i):
    return (i - 2) % count if i % 2 == 0 else (i + 2) % count


def after(block, *earlier):
    return lax.optimization_barrier((block, *earlier))[0]


def in_vmem(block):
    return pltpu.with_memory_space_constraint(block, pltpu.VMEM)


def two_parts(block):
    high = block.astype(jnp.bfloat16).astype(jnp.float32)
    return jnp.concatenate([high, block - high], axis=0).astype(jnp.bfloat16)


def fold(block):
    half = block.shape[0] // 2
    return block[:half] + block[half:]


def read(ref, row, count, start, width):
    if len(ref.shape) == 2:
        return ref[pl.ds(row, count), pl.ds(start, width)]
    lane_tiles = LANE_TILES
    rows = []
    for block in range(row // 8, (row + count) // 8):
        lanes = [ref[block * lane_tiles + lane] for lane in range(start // 128, (start + width) // 128)]
        rows.append(jnp.concatenate(lanes, axis=1))
    return jnp.concatenate(rows, axis=0)


def write(ref, row, start, block):
    count, width = block.shape
    if len(ref.shape) == 2:
        ref[pl.ds(row, count), pl.ds(start, width)] = block
        return
    for down in range(0, count, 8):
        for across in range(0, width, 128):
            tile = (row + down) // 8 * LANE_TILES + (start + across) // 128
            ref[tile] = block[down : down + 8, across : across + 128]


def packed_shape(n_rows):
    return (n_rows // 8 * LANE_TILES + 1, 8, 128)


def tiles(width):
    return [(start, min(TILE, width - start)) for start in range(0, width, TILE)]


def predict_kernel(round_number, terms, n_rows, scale_parts, *refs):
    n_out = 3 if scale_parts else 2
    inputs_ref, *operands = refs[:-n_out]
    total_ref, pred_ref = refs[-n_out:][:2]
    if scale_parts:
        scale = None
        for which in scale_parts:
            part = operands[which][operands[which].shape[0] - 1]
            scale = part if scale is None else scale + part
        refs[-1][...] = scale if round_number == 0 else scale * (1.0 / 3.0)
    pred = jnp.zeros((n_rows, inputs_ref.shape[3]), jnp.float32)
    for start, width in tiles(total_ref.shape[1]):
        pieces = []
        for count, parts in terms:
            piece = None
            for which, row in parts:
                part = read(operands[which], row, count, start, width)
                piece = part if piece is None else piece + part
            pieces.append(piece)
        block = pieces[0] if len(pieces) == 1 else jnp.concatenate(pieces, axis=0)
        total_ref[:, pl.ds(start, width)] = block
        product = lax.dot_general(
            two_parts(block),
            inputs_ref[0, 0, round_number, :, pl.ds(start, width)],
            (((1,), (1,)), ((), ())),
            preferred_element_type=jnp.float32,
        )
        pred = pred + fold(product)
    pred_ref[...] = pred


def predict(round_number, inputs, operands, terms, scale_parts):
    n_rows = sum(count for count, _ in terms)
    tokens, width = inputs.shape[3:]
    vmem = pl.BlockSpec(memory_space=pltpu.VMEM)
    shapes = [(n_rows, width), (n_rows, tokens)] + ([(8, 128)] if scale_parts else [])
    return pl.pallas_call(
        functools.partial(predict_kernel, round_number, terms, n_rows, scale_parts),
        in_specs=[vmem] * (1 + len(operands)),
        out_specs=[vmem] * len(shapes),
        out_shape=[pltpu.VMEM(shape, jnp.float32) for shape in shapes],
        compiler_params=pltpu.CompilerParams(vmem_limit_bytes=16 * 1024 * 1024),
        cost_estimate=pl.CostEstimate(
            flops=4 * n_rows * tokens * width, bytes_accessed=1 << 20, transcendentals=0
        ),
        name=f"predict{round_number}",
    )(in_vmem(inputs), *[in_vmem(block) for block in operands])


def adam_tile(count, gradient, first, second, params):
    first = BETA_ONE * first + (1.0 - BETA_ONE) * gradient
    second = BETA_TWO * second + (1.0 - BETA_TWO) * gradient * gradient
    first_corr = 1.0 - BETA_ONE**count
    second_corr = 1.0 - BETA_TWO**count
    step = (first * (LEARN_RATE / first_corr)) / (jnp.sqrt(second * (1.0 / second_corr)) + EPSILON)
    return params - step, first, second


def cut_kernel(row, counts, packed, numerator_ref, weight_ref, *refs):
    sems = refs[len(counts)]
    copies = []
    for which, count in enumerate(counts):
        target = refs[-1] if packed and which == 0 else refs[which]
        copy = pltpu.make_async_copy(numerator_ref.at[0, 0, pl.ds(row, count), :], target, sems.at[which])
        copy.start()
        copies.append(copy)
        row += count
    for copy in copies:
        copy.wait()
    if packed:
        for start, width in tiles(numerator_ref.shape[3]):
            write(refs[0], 0, start, refs[-1][:, pl.ds(start, width)])
        refs[0][refs[0].shape[0] - 1] = jnp.broadcast_to(weight_ref[...], (8, 128))


def cut(numerator, weight, row, counts, packed):
    width = numerator.shape[-1]
    vmem = pl.BlockSpec(memory_space=pltpu.VMEM)
    shapes = [(count, width) for count in counts]
    scratch = [pltpu.SemaphoreType.DMA((len(counts),))]
    if packed:
        shapes[0] = packed_shape(counts[0])
        scratch.append(pltpu.VMEM((counts[0], width), jnp.float32))
    return pl.pallas_call(
        functools.partial(cut_kernel, row, counts, packed),
        in_specs=[pl.BlockSpec(memory_space=pltpu.HBM), vmem],
        out_specs=[vmem] * len(counts),
        out_shape=[pltpu.VMEM(shape, jnp.float32) for shape in shapes],
        scratch_shapes=scratch,
        compiler_params=pltpu.CompilerParams(vmem_limit_bytes=4 * 1024 * 1024),
        cost_estimate=pl.CostEstimate(flops=0, bytes_accessed=1 << 20, transcendentals=0),
        name="cut",
    )(pltpu.with_memory_space_constraint(numerator, pltpu.HBM), weight)


def load_kernel(inputs_ref, held_ref, sem):
    copy = pltpu.make_async_copy(inputs_ref, held_ref, sem)
    copy.start()
    copy.wait()


def load(inputs):
    return pl.pallas_call(
        load_kernel,
        in_specs=[pl.BlockSpec(memory_space=pltpu.HBM)],
        out_specs=pl.BlockSpec(memory_space=pltpu.VMEM),
        out_shape=pltpu.VMEM(inputs.shape, inputs.dtype),
        scratch_shapes=[pltpu.SemaphoreType.DMA],
        compiler_params=pltpu.CompilerParams(vmem_limit_bytes=1024 * 1024),
        cost_estimate=pl.CostEstimate(flops=0, bytes_accessed=4 << 20, transcendentals=0),
        name="load",
    )(pltpu.with_memory_space_constraint(inputs, pltpu.HBM))


def update_tiles(round_number, row, pieces, refs, store):
    inputs_ref, targets_ref, total_ref, mine_ref, other_ref, scale_ref, *moments = refs
    n_rows, tokens = mine_ref.shape
    scale = jnp.concatenate([scale_ref[0:1, :]] * (TILE // 128), axis=1)
    inverse = 1.0 / scale
    scale = scale * (1.0 / 3.0)
    residual = (mine_ref[...] + other_ref[...]) * inverse[:, :tokens]
    residual = two_parts(residual - targets_ref[0, 0, round_number, pl.ds(row, n_rows), :])
    for start, width in tiles(total_ref.shape[1]):
        lanes = pl.ds(start, width)
        gradient = fold(
            jnp.dot(residual, inputs_ref[0, 0, round_number, :, lanes], preferred_element_type=jnp.float32)
        )
        done = 0
        for count, which, moment_row in pieces:
            rows = pl.ds(moment_row, count)
            params, first, second = adam_tile(
                PRIOR_STEPS + round_number + 1,
                gradient[done : done + count],
                moments[2 * which][rows, lanes],
                moments[2 * which + 1][rows, lanes],
                total_ref[pl.ds(done, count), lanes] * inverse[:, :width],
            )
            store(done, count, start, width, (params * scale[:, :width], first, second))
            done += count


def middle_kernel(row, pieces, n_operands, *refs):
    outs = refs[n_operands:]

    def store(done, count, start, width, blocks):
        for ref, block in zip(outs, blocks):
            write(ref, done, start, block)

    update_tiles(0, row, pieces, refs[:n_operands], store)
    if len(outs[0].shape) == 3:
        outs[0][outs[0].shape[0] - 1] = refs[5][...]


def last_kernel(row, pieces, n_operands, n_aliased, *refs):
    outs = refs[n_operands + n_aliased : n_operands + n_aliased + 3]
    weight_ref, held, sems = refs[-3:]
    copies = []
    weight_ref[...] = refs[5][0:1, 0:1] * (1.0 / 3.0)

    def store(done, count, start, width, blocks):
        lanes = pl.ds(start, width)
        for which, (ref, block) in enumerate(zip(outs, blocks)):
            held[which, pl.ds(done, count), lanes] = block
            copy = pltpu.make_async_copy(
                held.at[which, pl.ds(done, count), lanes],
                ref.at[0, 0, pl.ds(row + done, count), lanes],
                sems.at[len(copies)],
            )
            copy.start()
            copies.append(copy)

    update_tiles(1, row, pieces, refs[:n_operands], store)
    for copy in copies:
        copy.wait()


def update_cost(n_rows, tokens, width):
    return pl.CostEstimate(flops=4 * n_rows * tokens * width, bytes_accessed=1 << 20, transcendentals=n_rows * width)


def update_middle(row, operands, packed):
    n_rows, width = operands[2].shape
    vmem = pl.BlockSpec(memory_space=pltpu.VMEM)
    return pl.pallas_call(
        functools.partial(middle_kernel, row, ((n_rows, 0, row),), len(operands)),
        in_specs=[vmem] * len(operands),
        out_specs=[vmem] * 3,
        out_shape=[
            pltpu.VMEM(packed_shape(n_rows) if packed else (n_rows, width), jnp.float32),
            pltpu.VMEM((n_rows, width), jnp.float32),
            pltpu.VMEM((n_rows, width), jnp.float32),
        ],
        compiler_params=pltpu.CompilerParams(vmem_limit_bytes=16 * 1024 * 1024),
        cost_estimate=update_cost(n_rows, operands[0].shape[3], width),
        name="update0",
    )(*[in_vmem(block) for block in operands])


def update_last(row, pieces, operands, whole_shape, previous):
    n_rows, width = operands[2].shape
    vmem = pl.BlockSpec(memory_space=pltpu.VMEM)
    outer = pl.BlockSpec(memory_space=pltpu.HBM)
    return pl.pallas_call(
        functools.partial(last_kernel, row, pieces, len(operands), len(previous)),
        in_specs=[vmem] * len(operands) + [outer] * len(previous),
        out_specs=[outer] * 3 + [vmem],
        out_shape=[jax.ShapeDtypeStruct(whole_shape, jnp.float32)] * 3 + [jax.ShapeDtypeStruct((1, 1), jnp.float32)],
        scratch_shapes=[
            pltpu.VMEM((3, n_rows, width), jnp.float32),
            pltpu.SemaphoreType.DMA((3 * len(tiles(width)) * len(pieces),)),
        ],
        input_output_aliases={len(operands) + which: which for which in range(len(previous))},
        compiler_params=pltpu.CompilerParams(vmem_limit_bytes=24 * 1024 * 1024),
        cost_estimate=update_cost(n_rows, operands[0].shape[3], width),
        name="update1",
    )(*[in_vmem(block) for block in operands], *previous)


def summed_over_ma(pred):
    pair = pred + send(pred, "ma", lambda i: i ^ 1)
    return pair, send(pair, "ma", lambda i: i ^ 2)


def neighbours(block, axis):
    count = lax.axis_size(axis)
    return send(block, axis, lambda i: (i + 1) % count), send(block, axis, lambda i: (i - 1) % count)


def local(numerator, weight, inputs, targets, first_moment, second_moment):
    row_count = lax.axis_size("rx")
    first = first_moment[0, 0]
    second = second_moment[0, 0]
    out_of = functools.partial(outward, row_count)
    into = functools.partial(inward, row_count)
    own = []
    rows = []
    row = 0
    for group in GROUPS:
        own.append(cut(numerator, weight, row, group, row == 0))
        rows.append(row)
        row += sum(group)
    inputs = load(inputs)

    results = []
    across = send(own[0][0], "rx", partner)
    along = send(own[0][1], "rx", into)
    earlier = (inputs, own[1][0])
    for g, (own_a, own_b) in enumerate(own):
        pair_sum = after(own_b, *earlier) + along
        across_now = after(across, *earlier)
        if g + 1 < len(GROUPS):
            next_a, next_b = own[g + 1]
            along = send(after(next_b, pair_sum), "rx", into)
            across = send(after(next_a, pair_sum), "rx", partner)
        count_a, count_b = GROUPS[g]
        total, pred, *tile = predict(
            0,
            inputs,
            (own_a, across_now, send(across_now, "rx", out_of), own_b, send(pair_sum, "rx", partner)),
            ((count_a, ((0, 0), (1, 0), (2, 0))), (count_b, ((3, 0), (4, 0)))),
            (0, 1, 2) if g == 0 else (),
        )
        if g == 0:
            (row_sum,) = tile
        mine, other = summed_over_ma(pred)
        earlier = (other,)
        if g + 1 < len(GROUPS):
            total = after(total, along, across)
        values, first_mid, second_mid = update_middle(
            rows[g], (inputs, targets, total, mine, other, row_sum, first, second), g == 0
        )
        ready = after(values, *results[-1][1:3]) if g > 0 else values
        results.append((values, *neighbours(ready, "ry"), first_mid, second_mid))

    outs = ()
    for batch in BATCHES:
        operands = []
        terms = []
        for g in batch:
            values, before, next_one = results[g][:3]
            values = after(values, results[-1][0], *([other] if outs else []))
            terms.append((sum(GROUPS[g]), tuple((len(operands) + i, 0) for i in range(3))))
            operands += [values, before, next_one]
        total, pred, *tile = predict(1, inputs, tuple(operands), tuple(terms), (0, 1, 2) if not outs else ())
        if not outs:
            (column_sum,) = tile
        mine, other = summed_over_ma(pred)
        moments = [block for g in batch for block in results[g][3:]]
        outs = update_last(
            rows[batch[0]],
            tuple((sum(GROUPS[g]), which, 0) for which, g in enumerate(batch)),
            (inputs, targets, total, mine, other, column_sum, *moments),
            numerator.shape,
            outs[:3],
        )
    new_numerator, new_first, new_second, new_weight = outs
    return new_numerator, new_weight, new_first, new_second


def solution(mesh):
    rows = P("rx", "ry", None, "ma")
    return jax.shard_map(
        local,
        mesh=mesh,
        in_specs=(
            rows,
            P("rx", "ry"),
            P("rx", "ry", None, None, "ma"),
            P("rx", "ry", None, None, None),
            rows,
            rows,
        ),
        out_specs=(rows, P("rx", "ry"), rows, rows),
        check_vma=False,
    )
```

time: 114 us -> 99.3 us (0.87)
  waiting for transfers between devices: 50.5 us -> 39.5 us
  Pallas kernels: 10.5 us -> 14.3 us
  between operations: 4.5 us -> 1.57 us
  other arithmetic: 2.69 us -> 0.13 us
  local copies, waits for them, and re-layouts: 2.15 us -> 0.01 us
    ppermute x24 -> x20, waiting for transfers between devices: 50.5 us -> 39.5 us  [send(): lax.ppermute(block, axis, [(i, target(i)) for i in range(lax.axis_size(ax...]
    pallas_call x4 -> x7, Pallas kernels: 7.65 us -> 11.5 us  [the longest x2 5.07 us: update_last(): pl.pallas_call(functools.partial(last_kernel, row, pieces, len(operands),...]
    slice x3 -> x0, local copies, waits for them, and re-layouts: 2.13 us -> none  [the longest x2 1.54 us: local(): pair_sum = send(own[mid:end] + along, 'rx', partner)]
    add x3 -> x2, other arithmetic: 1.39 us -> 0.09 us  [local(): pair_sum = after(own_b, *earlier) + along]
    concatenate x1 -> x0, other arithmetic: 1.26 us -> none  [local(): three = jnp.concatenate([weight, before, after], axis=1)]
    ppermute x24 -> x20, starting transfers between devices: 43.6 us -> 43.6 us  [send(): lax.ppermute(block, axis, [(i, target(i)) for i in range(lax.axis_size(ax...]
  transfers between devices with their start and end apart: 24 -> 20, of which waited for: 12 -> 14; matrix products, arithmetic and copies ran while one was open for 4% -> 0% of each run, Pallas kernels for 7% -> 9%
where the time goes in v2:
time: 99.3 us; the launch traced here: 99.1 us
  starting transfers between devices  43.6 us (44%)
  waiting for transfers between devices  39.5 us (40%)
  Pallas kernels  14.3 us (14%)
  between operations  1.57 us (2%)
    ppermute x20, starting transfers between devices, send(): lax.ppermute(block, axis, [(i, target(i)) for i in range(lax.axis_size(ax...  43.6 us
    ppermute x20, waiting for transfers between devices, send(): lax.ppermute(block, axis, [(i, target(i)) for i in range(lax.axis_size(ax...  39.5 us
    pallas_call x2, Pallas kernels, update_last(): pl.pallas_call(functools.partial(last_kernel, row, pieces, len(operands),...  5.07 us
    pallas_call x4, Pallas kernels, predict(): pl.pallas_call(functools.partial(predict_kernel, round_number, terms, n_r...  2.81 us
    pallas_call x2, Pallas kernels, cut(): pl.pallas_call(functools.partial(cut_kernel, row, counts, packed), in_spe...  2.39 us
    pallas_call x1, Pallas kernels, load(): pl.pallas_call(load_kernel, in_specs=[pl.BlockSpec(memory_space=pltpu.HBM...  2.01 us
  transfers between devices with their start and end apart: 20, of which 14 were waited for; matrix products, arithmetic and copies ran while one was open for 0% of the time, Pallas kernels for 9%

profile of v2, /device:TPU:1, one launch (start us, length us, event | category | flops | bytes accessed | tf_op | source)
XLA Modules:
  0.0 99.1 jit_solution(17179081885360315418)
XLA Ops:
  1.3 1.3 %cut.3 = (f32[109,8,128]{2,1,0:T(8,128)S(1)}, f32[32,3456]{1,0:T(8,128)S(1)}) custom-call(f32[1,1,120,3456]{3,2,1,0:T(8,128)} %numerator_ref.3, f32[1,1]{1,0:T(1,128)S(6)} %copy.16.weight_ref), custom_call_target="tpu_custom_call" | custom-call | bytes 1048576 | tf_op jit(solution)/shard_map/cut/pallas_call | solution.py:169
  2.5 2.2 %collective-permute-start.2 = (f32[109,8,128]{2,1,0:T(8,128)S(1)}, f32[109,8,128]{2,1,0:T(8,128)S(1)}, u32[]{:S(2)}, u32[]{:S(2)}) collective-permute-start(f32[109,8,128]{2,1,0:T(8,128)S(1)} %get-tuple-element.45.refs_1_), channel_id=1, source_target_pairs={{0,16},{16,0},{32,48},{48,32},{64,80},{80,64},{96,112},{112,96},{1... | collective-permute-start | bytes 1339400 | tf_op jit(solution)/shard_map/ppermute | solution.py:23
  4.8 5.6 %collective-permute-start = (f32[32,3456]{1,0:T(8,128)S(1)}, f32[32,3456]{1,0:T(8,128)S(1)}, u32[]{:S(2)}, u32[]{:S(2)}) collective-permute-start(f32[32,3456]{1,0:T(8,128)S(1)} %get-tuple-element.43.refs_4_), channel_id=1, source_target_pairs={{0,224},{16,48},{32,0},{48,80},{64,32},{80,112},{96,64},{112,144},... | collective-permute-start | bytes 1327112 | tf_op jit(solution)/shard_map/ppermute | solution.py:23
  10.3 1.1 %cut.2 = (f32[24,3456]{1,0:T(8,128)S(1)}, f32[32,3456]{1,0:T(8,128)S(1)}) custom-call(f32[1,1,120,3456]{3,2,1,0:T(8,128)} %numerator_ref.3, f32[1,1]{1,0:T(1,128)S(6)} %copy.16.weight_ref), custom_call_target="tpu_custom_call" | custom-call | bytes 1048576 | tf_op jit(solution)/shard_map/cut/pallas_call | solution.py:169
  11.5 2.0 %load.1.refs_0_ = bf16[1,1,2,256,3456]{4,3,2,1,0:T(8,128)(2,1)S(1)} custom-call(bf16[1,1,2,256,3456]{4,3,2,1,0:T(8,128)(2,1)} %inputs_ref.1), custom_call_target="tpu_custom_call" | custom-call | bytes 4194304 | tf_op jit(solution)/shard_map/load/pallas_call | solution.py:188
  13.5 2.7 %collective-permute-start.3 = (f32[109,8,128]{2,1,0:T(8,128)S(1)}, f32[109,8,128]{2,1,0:T(8,128)S(1)}, u32[]{:S(2)}, u32[]{:S(2)}) collective-permute-start(f32[109,8,128]{2,1,0:T(8,128)S(1)} %collective-permute-done.2.refs_2_), channel_id=1, source_target_pairs={{0,32},{16,240},{32,64},{48,16},{64,96},{80,48},{96,128},{112,80},... | collective-permute-start | bytes 1339400 | tf_op jit(solution)/shard_map/ppermute | solution.py:23
  16.2 2.6 %collective-permute-done = f32[32,3456]{1,0:T(8,128)S(1)} collective-permute-done((f32[32,3456]{1,0:T(8,128)S(1)}, f32[32,3456]{1,0:T(8,128)S(1)}, u32[]{:S(2)}, u32[]{:S(2)}) %collective-permute-start) | collective-permute-done | bytes 442400 | tf_op jit(solution)/shard_map/ppermute | solution.py:23
  18.9 2.7 %collective-permute-start.4 = (f32[32,3456]{1,0:T(8,128)S(1)}, f32[32,3456]{1,0:T(8,128)S(1)}, u32[]{:S(2)}, u32[]{:S(2)}) collective-permute-start(f32[32,3456]{1,0:T(8,128)S(1)} %add.18), channel_id=1, source_target_pairs={{0,16},{16,0},{32,48},{48,32},{64,80},{80,64},{96,112},{112,96},{1... | collective-permute-start | bytes 1327112 | tf_op jit(solution)/shard_map/ppermute | solution.py:23
  21.6 0.9 collective-permute-start.8
  22.5 7.7 %collective-permute-done.4.refs_5_ = f32[32,3456]{1,0:T(8,128)S(1)} collective-permute-done((f32[32,3456]{1,0:T(8,128)S(1)}, f32[32,3456]{1,0:T(8,128)S(1)}, u32[]{:S(2)}, u32[]{:S(2)}) %collective-permute-start.4) | collective-permute-done | bytes 442400 | tf_op jit(solution)/shard_map/ppermute | solution.py:23
  31.0 4.6 %collective-permute-start.5 = (f32[64,256]{1,0:T(8,128)S(1)}, f32[64,256]{1,0:T(8,128)S(1)}, u32[]{:S(2)}, u32[]{:S(2)}) collective-permute-start(f32[64,256]{1,0:T(8,128)S(1)} %get-tuple-element.47), channel_id=1, source_target_pairs={{0,1},{1,0},{2,3},{3,2},{4,5},{5,4},{6,7},{7,6},{8,9},{9,8},{10,11... | collective-permute-start | bytes 196616 | tf_op jit(solution)/shard_map/ppermute | solution.py:23
  35.6 0.9 collective-permute-done.5
  36.5 2.7 %collective-permute-start.6 = (f32[64,256]{1,0:T(8,128)S(1)}, f32[64,256]{1,0:T(8,128)S(1)}, u32[]{:S(2)}, u32[]{:S(2)}) collective-permute-start(f32[64,256]{1,0:T(8,128)S(1)} %add.19.refs_3_), channel_id=1, source_target_pairs={{0,2},{1,3},{2,0},{3,1},{4,6},{5,7},{6,4},{7,5},{8,10},{9,11},{10,... | collective-permute-start | bytes 196616 | tf_op jit(solution)/shard_map/ppermute | solution.py:23
  39.2 2.8 %collective-permute-done.6.refs_4_ = f32[64,256]{1,0:T(8,128)S(1)} collective-permute-done((f32[64,256]{1,0:T(8,128)S(1)}, f32[64,256]{1,0:T(8,128)S(1)}, u32[]{:S(2)}, u32[]{:S(2)}) %collective-permute-start.6) | collective-permute-done | bytes 65568 | tf_op jit(solution)/shard_map/ppermute | solution.py:23
  42.0 1.0 %update0.3 = (f32[217,8,128]{2,1,0:T(8,128)S(1)}, f32[64,3456]{1,0:T(8,128)S(1)}, f32[64,3456]{1,0:T(8,128)S(1)}) custom-call(bf16[1,1,2,256,3456]{4,3,2,1,0:T(8,128)(2,1)S(1)} %load.1.refs_0_, f32[1,1,2,120,256]{4,3,2,1,0:T(8,128)S(1)} %copy-done.2, f32[64,3456]{1,0:T(8,128)S(1)} %get-tuple-element.57.refs_2_, f32[64,256]{1,0:T(8,128)S(1)} %add.19.refs_3_, ...), custom_call_target="tpu_custom_call" | custom-call | flops 226492416 | bytes 1048576 | tf_op jit(solution)/shard_map/update0/pallas_call | solution.py:269
  43.0 2.6 %collective-permute-start.13 = (f32[217,8,128]{2,1,0:T(8,128)S(1)}, f32[217,8,128]{2,1,0:T(8,128)S(1)}, u32[]{:S(2)}, u32[]{:S(2)}) collective-permute-start(f32[217,8,128]{2,1,0:T(8,128)S(1)} %get-tuple-element.59.refs_1_), channel_id=1, source_target_pairs={{0,12},{4,0},{8,4},{12,8},{1,13},{5,1},{9,5},{13,9},{2,14},{6,2},{... | collective-permute-start | bytes 2666504 | tf_op jit(solution)/shard_map/ppermute | solution.py:23
  45.6 1.1 %collective-permute-start.9 = (f32[32,3456]{1,0:T(8,128)S(1)}, f32[32,3456]{1,0:T(8,128)S(1)}, u32[]{:S(2)}, u32[]{:S(2)}) collective-permute-start(f32[32,3456]{1,0:T(8,128)S(1)} %add.20), channel_id=1, source_target_pairs={{0,16},{16,0},{32,48},{48,32},{64,80},{80,64},{96,112},{112,96},{1... | collective-permute-start | bytes 1327112 | tf_op jit(solution)/shard_map/ppermute | solution.py:23
  46.7 8.4 %collective-permute-done.7.refs_3_ = f32[24,3456]{1,0:T(8,128)S(1)} collective-permute-done((f32[24,3456]{1,0:T(8,128)S(1)}, f32[24,3456]{1,0:T(8,128)S(1)}, u32[]{:S(2)}, u32[]{:S(2)}) %collective-permute-start.7) | collective-permute-done | bytes 331808 | tf_op jit(solution)/shard_map/ppermute | solution.py:23
  55.9 3.2 %collective-permute-start.10 = (f32[56,256]{1,0:T(8,128)S(1)}, f32[56,256]{1,0:T(8,128)S(1)}, u32[]{:S(2)}, u32[]{:S(2)}) collective-permute-start(f32[56,256]{1,0:T(8,128)S(1)} %get-tuple-element.53), channel_id=1, source_target_pairs={{0,1},{1,0},{2,3},{3,2},{4,5},{5,4},{6,7},{7,6},{8,9},{9,8},{10,11... | collective-permute-start | bytes 172040 | tf_op jit(solution)/shard_map/ppermute | solution.py:23
  60.0 2.7 %collective-permute-start.11 = (f32[56,256]{1,0:T(8,128)S(1)}, f32[56,256]{1,0:T(8,128)S(1)}, u32[]{:S(2)}, u32[]{:S(2)}) collective-permute-start(f32[56,256]{1,0:T(8,128)S(1)} %add.21.refs_3_), channel_id=1, source_target_pairs={{0,2},{1,3},{2,0},{3,1},{4,6},{5,7},{6,4},{7,5},{8,10},{9,11},{10,... | collective-permute-start | bytes 172040 | tf_op jit(solution)/shard_map/ppermute | solution.py:23
  62.6 2.1 %collective-permute-done.11.refs_4_ = f32[56,256]{1,0:T(8,128)S(1)} collective-permute-done((f32[56,256]{1,0:T(8,128)S(1)}, f32[56,256]{1,0:T(8,128)S(1)}, u32[]{:S(2)}, u32[]{:S(2)}) %collective-permute-start.11) | collective-permute-done | bytes 57376 | tf_op jit(solution)/shard_map/ppermute | solution.py:23
  64.7 1.0 update0.2
  65.9 2.6 %collective-permute-start.17 = (f32[56,3456]{1,0:T(8,128)S(1)}, f32[56,3456]{1,0:T(8,128)S(1)}, u32[]{:S(2)}, u32[]{:S(2)}) collective-permute-start(f32[56,3456]{1,0:T(8,128)S(1)} %get-tuple-element.62.refs_1_), channel_id=1, source_target_pairs={{0,12},{4,0},{8,4},{12,8},{1,13},{5,1},{9,5},{13,9},{2,14},{6,2},{... | collective-permute-start | bytes 2322440 | tf_op jit(solution)/shard_map/ppermute | solution.py:23
  69.2 2.6 %collective-permute-start.14 = (f32[64,256]{1,0:T(8,128)S(1)}, f32[64,256]{1,0:T(8,128)S(1)}, u32[]{:S(2)}, u32[]{:S(2)}) collective-permute-start(f32[64,256]{1,0:T(8,128)S(1)} %get-tuple-element.60), channel_id=1, source_target_pairs={{0,1},{1,0},{2,3},{3,2},{4,5},{5,4},{6,7},{7,6},{8,9},{9,8},{10,11... | collective-permute-start | bytes 196616 | tf_op jit(solution)/shard_map/ppermute | solution.py:23
  72.7 1.9 %collective-permute-start.15 = (f32[64,256]{1,0:T(8,128)S(1)}, f32[64,256]{1,0:T(8,128)S(1)}, u32[]{:S(2)}, u32[]{:S(2)}) collective-permute-start(f32[64,256]{1,0:T(8,128)S(1)} %add.22.refs_3_), channel_id=1, source_target_pairs={{0,2},{1,3},{2,0},{3,1},{4,6},{5,7},{6,4},{7,5},{8,10},{9,11},{10,... | collective-permute-start | bytes 196616 | tf_op jit(solution)/shard_map/ppermute | solution.py:23
  74.6 2.8 %collective-permute-done.15.refs_4_ = f32[64,256]{1,0:T(8,128)S(1)} collective-permute-done((f32[64,256]{1,0:T(8,128)S(1)}, f32[64,256]{1,0:T(8,128)S(1)}, u32[]{:S(2)}, u32[]{:S(2)}) %collective-permute-start.15) | collective-permute-done | bytes 65568 | tf_op jit(solution)/shard_map/ppermute | solution.py:23
  77.4 6.1 %collective-permute-done.17.refs_3_ = f32[56,3456]{1,0:T(8,128)S(1)} collective-permute-done((f32[56,3456]{1,0:T(8,128)S(1)}, f32[56,3456]{1,0:T(8,128)S(1)}, u32[]{:S(2)}, u32[]{:S(2)}) %collective-permute-start.17) | collective-permute-done | bytes 774176 | tf_op jit(solution)/shard_map/ppermute | solution.py:23
  83.5 3.1 %collective-permute-done.16.refs_2_ = f32[56,3456]{1,0:T(8,128)S(1)} collective-permute-done((f32[56,3456]{1,0:T(8,128)S(1)}, f32[56,3456]{1,0:T(8,128)S(1)}, u32[]{:S(2)}, u32[]{:S(2)}) %collective-permute-start.16) | collective-permute-done | bytes 774176 | tf_op jit(solution)/shard_map/ppermute | solution.py:23
  87.3 2.8 %collective-permute-start.18 = (f32[56,256]{1,0:T(8,128)S(1)}, f32[56,256]{1,0:T(8,128)S(1)}, u32[]{:S(2)}, u32[]{:S(2)}) collective-permute-start(f32[56,256]{1,0:T(8,128)S(1)} %get-tuple-element.64), channel_id=1, source_target_pairs={{0,1},{1,0},{2,3},{3,2},{4,5},{5,4},{6,7},{7,6},{8,9},{9,8},{10,11... | collective-permute-start | bytes 172040 | tf_op jit(solution)/shard_map/ppermute | solution.py:23
  91.1 2.8 %collective-permute-start.19 = (f32[56,256]{1,0:T(8,128)S(1)}, f32[56,256]{1,0:T(8,128)S(1)}, u32[]{:S(2)}, u32[]{:S(2)}) collective-permute-start(f32[56,256]{1,0:T(8,128)S(1)} %add.23.refs_3_), channel_id=1, source_target_pairs={{0,2},{1,3},{2,0},{3,1},{4,6},{5,7},{6,4},{7,5},{8,10},{9,11},{10,... | collective-permute-start | bytes 172040 | tf_op jit(solution)/shard_map/ppermute | solution.py:23
  93.8 2.6 %update1.2 = (f32[1,1,120,3456]{3,2,1,0:T(8,128)}, f32[1,1,120,3456]{3,2,1,0:T(8,128)}, f32[1,1,120,3456]{3,2,1,0:T(8,128)}, f32[1,1]{1,0:T(1,128)}) custom-call(bf16[1,1,2,256,3456]{4,3,2,1,0:T(8,128)(2,1)S(1)} %load.1.refs_0_, f32[1,1,2,120,256]{4,3,2,1,0:T(8,128)S(1)} %copy-done.2, f32[64,3456]{1,0:T(8,128)S(1)} %get-tuple-element.68.refs_2_, ...), custom_call_target="tpu_custom_call" | custom-call | flops 226492416 | bytes 1048576 | tf_op jit(solution)/shard_map/update1/pallas_call | solution.py:288
  96.4 2.5 %update1.3 = (f32[1,1,120,3456]{3,2,1,0:T(8,128)}, f32[1,1,120,3456]{3,2,1,0:T(8,128)}, f32[1,1,120,3456]{3,2,1,0:T(8,128)}, f32[1,1]{1,0:T(1,128)}) custom-call(bf16[1,1,2,256,3456]{4,3,2,1,0:T(8,128)(2,1)S(1)} %load.1.refs_0_, f32[1,1,2,120,256]{4,3,2,1,0:T(8,128)S(1)} %copy-done.2, ...), custom_call_target="tpu_custom_call", output_to_operand_aliasing={{0}: (8, {}), {1}: (9, {}), {2}: (10, {})} | custom-call | flops 198180864 | bytes 1048576 | tf_op jit(solution)/shard_map/update1/pallas_call | solution.py:288
  (31 shorter events, 5.9 us)
Async XLA Ops:
  2.5 11.0 %collective-permute-start.2 = (f32[109,8,128]{2,1,0:T(8,128)S(1)}, f32[109,8,128]{2,1,0:T(8,128)S(1)}, u32[]{:S(2)}, u32[]{:S(2)}) collective-permute-start(f32[109,8,128]{2,1,0:T(8,128)S(1)} %get-tuple-element.45.refs_1_), channel_id=1, source_target_pairs={{0,16},{16,0},{32,48},{48,32},{64,80},{80,64},{96,112},{112,96},{1... | collective-permute-start | bytes 1339400 | tf_op jit(solution)/shard_map/ppermute | solution.py:23
  4.8 14.1 %collective-permute-start = (f32[32,3456]{1,0:T(8,128)S(1)}, f32[32,3456]{1,0:T(8,128)S(1)}, u32[]{:S(2)}, u32[]{:S(2)}) collective-permute-start(f32[32,3456]{1,0:T(8,128)S(1)} %get-tuple-element.43.refs_4_), channel_id=1, source_target_pairs={{0,224},{16,48},{32,0},{48,80},{64,32},{80,112},{96,64},{112,144},... | collective-permute-start | bytes 1327112 | tf_op jit(solution)/shard_map/ppermute | solution.py:23
  13.5 16.8 %collective-permute-start.3 = (f32[109,8,128]{2,1,0:T(8,128)S(1)}, f32[109,8,128]{2,1,0:T(8,128)S(1)}, u32[]{:S(2)}, u32[]{:S(2)}) collective-permute-start(f32[109,8,128]{2,1,0:T(8,128)S(1)} %collective-permute-done.2.refs_2_), channel_id=1, source_target_pairs={{0,32},{16,240},{32,64},{48,16},{64,96},{80,48},{96,128},{112,80},... | collective-permute-start | bytes 1339400 | tf_op jit(solution)/shard_map/ppermute | solution.py:23
  18.9 11.4 %collective-permute-start.4 = (f32[32,3456]{1,0:T(8,128)S(1)}, f32[32,3456]{1,0:T(8,128)S(1)}, u32[]{:S(2)}, u32[]{:S(2)}) collective-permute-start(f32[32,3456]{1,0:T(8,128)S(1)} %add.18), channel_id=1, source_target_pairs={{0,16},{16,0},{32,48},{48,32},{64,80},{80,64},{96,112},{112,96},{1... | collective-permute-start | bytes 1327112 | tf_op jit(solution)/shard_map/ppermute | solution.py:23
  21.6 20.4 %copy-start = (f32[1,1,120,3456]{3,2,1,0:T(8,128)S(1)}, f32[1,1,120,3456]{3,2,1,0:T(8,128)}, u32[]{:S(2)}) copy-start(f32[1,1,120,3456]{3,2,1,0:T(8,128)} %param.10) | copy-start | bytes 4976644
  21.6 20.4 %copy-start.1 = (f32[1,1,120,3456]{3,2,1,0:T(8,128)S(1)}, f32[1,1,120,3456]{3,2,1,0:T(8,128)}, u32[]{:S(2)}) copy-start(f32[1,1,120,3456]{3,2,1,0:T(8,128)} %param.11) | copy-start | bytes 4976644
  21.6 20.4 %copy-start.2 = (f32[1,1,2,120,256]{4,3,2,1,0:T(8,128)S(1)}, f32[1,1,2,120,256]{4,3,2,1,0:T(8,128)}, u32[]{:S(2)}) copy-start(f32[1,1,2,120,256]{4,3,2,1,0:T(8,128)} %refs_1_.7) | copy-start | bytes 737284
  21.6 17.6 %collective-permute-start.8 = (f32[32,3456]{1,0:T(8,128)S(1)}, f32[32,3456]{1,0:T(8,128)S(1)}, u32[]{:S(2)}, u32[]{:S(2)}) collective-permute-start(f32[32,3456]{1,0:T(8,128)S(1)} %get-tuple-element.51.refs_4_), channel_id=1, source_target_pairs={{0,224},{16,48},{32,0},{48,80},{64,32},{80,112},{96,64},{112,144},... | collective-permute-start | bytes 1327112 | tf_op jit(solution)/shard_map/ppermute | solution.py:23
  22.5 16.7 %collective-permute-start.1 = (f32[24,3456]{1,0:T(8,128)S(1)}, f32[24,3456]{1,0:T(8,128)S(1)}, u32[]{:S(2)}, u32[]{:S(2)}) collective-permute-start(f32[24,3456]{1,0:T(8,128)S(1)} %get-tuple-element.44.refs_1_), channel_id=1, source_target_pairs={{0,16},{16,0},{32,48},{48,32},{64,80},{80,64},{96,112},{112,96},{1... | collective-permute-start | bytes 995336 | tf_op jit(solution)/shard_map/ppermute | solution.py:23
  31.0 5.5 %collective-permute-start.5 = (f32[64,256]{1,0:T(8,128)S(1)}, f32[64,256]{1,0:T(8,128)S(1)}, u32[]{:S(2)}, u32[]{:S(2)}) collective-permute-start(f32[64,256]{1,0:T(8,128)S(1)} %get-tuple-element.47), channel_id=1, source_target_pairs={{0,1},{1,0},{2,3},{3,2},{4,5},{5,4},{6,7},{7,6},{8,9},{9,8},{10,11... | collective-permute-start | bytes 196616 | tf_op jit(solution)/shard_map/ppermute | solution.py:23
  36.5 5.5 %collective-permute-start.6 = (f32[64,256]{1,0:T(8,128)S(1)}, f32[64,256]{1,0:T(8,128)S(1)}, u32[]{:S(2)}, u32[]{:S(2)}) collective-permute-start(f32[64,256]{1,0:T(8,128)S(1)} %add.19.refs_3_), channel_id=1, source_target_pairs={{0,2},{1,3},{2,0},{3,1},{4,6},{5,7},{6,4},{7,5},{8,10},{9,11},{10,... | collective-permute-start | bytes 196616 | tf_op jit(solution)/shard_map/ppermute | solution.py:23
  43.0 22.7 %collective-permute-start.13 = (f32[217,8,128]{2,1,0:T(8,128)S(1)}, f32[217,8,128]{2,1,0:T(8,128)S(1)}, u32[]{:S(2)}, u32[]{:S(2)}) collective-permute-start(f32[217,8,128]{2,1,0:T(8,128)S(1)} %get-tuple-element.59.refs_1_), channel_id=1, source_target_pairs={{0,12},{4,0},{8,4},{12,8},{1,13},{5,1},{9,5},{13,9},{2,14},{6,2},{... | collective-permute-start | bytes 2666504 | tf_op jit(solution)/shard_map/ppermute | solution.py:23
  45.6 20.3 %collective-permute-start.12 = (f32[217,8,128]{2,1,0:T(8,128)S(1)}, f32[217,8,128]{2,1,0:T(8,128)S(1)}, u32[]{:S(2)}, u32[]{:S(2)}) collective-permute-start(f32[217,8,128]{2,1,0:T(8,128)S(1)} %get-tuple-element.59.refs_1_), channel_id=1, source_target_pairs={{0,4},{4,8},{8,12},{12,0},{1,5},{5,9},{9,13},{13,1},{2,6},{6,10},{... | collective-permute-start | bytes 2666504 | tf_op jit(solution)/shard_map/ppermute | solution.py:23
  45.6 9.6 %collective-permute-start.9 = (f32[32,3456]{1,0:T(8,128)S(1)}, f32[32,3456]{1,0:T(8,128)S(1)}, u32[]{:S(2)}, u32[]{:S(2)}) collective-permute-start(f32[32,3456]{1,0:T(8,128)S(1)} %add.20), channel_id=1, source_target_pairs={{0,16},{16,0},{32,48},{48,32},{64,80},{80,64},{96,112},{112,96},{1... | collective-permute-start | bytes 1327112 | tf_op jit(solution)/shard_map/ppermute | solution.py:23
  46.7 8.4 %collective-permute-start.7 = (f32[24,3456]{1,0:T(8,128)S(1)}, f32[24,3456]{1,0:T(8,128)S(1)}, u32[]{:S(2)}, u32[]{:S(2)}) collective-permute-start(f32[24,3456]{1,0:T(8,128)S(1)} %collective-permute-done.1.refs_2_), channel_id=1, source_target_pairs={{0,32},{16,240},{32,64},{48,16},{64,96},{80,48},{96,128},{112,80},... | collective-permute-start | bytes 995336 | tf_op jit(solution)/shard_map/ppermute | solution.py:23
  55.9 4.1 %collective-permute-start.10 = (f32[56,256]{1,0:T(8,128)S(1)}, f32[56,256]{1,0:T(8,128)S(1)}, u32[]{:S(2)}, u32[]{:S(2)}) collective-permute-start(f32[56,256]{1,0:T(8,128)S(1)} %get-tuple-element.53), channel_id=1, source_target_pairs={{0,1},{1,0},{2,3},{3,2},{4,5},{5,4},{6,7},{7,6},{8,9},{9,8},{10,11... | collective-permute-start | bytes 172040 | tf_op jit(solution)/shard_map/ppermute | solution.py:23
  60.0 4.8 %collective-permute-start.11 = (f32[56,256]{1,0:T(8,128)S(1)}, f32[56,256]{1,0:T(8,128)S(1)}, u32[]{:S(2)}, u32[]{:S(2)}) collective-permute-start(f32[56,256]{1,0:T(8,128)S(1)} %add.21.refs_3_), channel_id=1, source_target_pairs={{0,2},{1,3},{2,0},{3,1},{4,6},{5,7},{6,4},{7,5},{8,10},{9,11},{10,... | collective-permute-start | bytes 172040 | tf_op jit(solution)/shard_map/ppermute | solution.py:23
  65.9 17.6 %collective-permute-start.17 = (f32[56,3456]{1,0:T(8,128)S(1)}, f32[56,3456]{1,0:T(8,128)S(1)}, u32[]{:S(2)}, u32[]{:S(2)}) collective-permute-start(f32[56,3456]{1,0:T(8,128)S(1)} %get-tuple-element.62.refs_1_), channel_id=1, source_target_pairs={{0,12},{4,0},{8,4},{12,8},{1,13},{5,1},{9,5},{13,9},{2,14},{6,2},{... | collective-permute-start | bytes 2322440 | tf_op jit(solution)/shard_map/ppermute | solution.py:23
  68.5 18.2 %collective-permute-start.16 = (f32[56,3456]{1,0:T(8,128)S(1)}, f32[56,3456]{1,0:T(8,128)S(1)}, u32[]{:S(2)}, u32[]{:S(2)}) collective-permute-start(f32[56,3456]{1,0:T(8,128)S(1)} %get-tuple-element.62.refs_1_), channel_id=1, source_target_pairs={{0,4},{4,8},{8,12},{12,0},{1,5},{5,9},{9,13},{13,1},{2,6},{6,10},{... | collective-permute-start | bytes 2322440 | tf_op jit(solution)/shard_map/ppermute | solution.py:23
  69.2 3.5 %collective-permute-start.14 = (f32[64,256]{1,0:T(8,128)S(1)}, f32[64,256]{1,0:T(8,128)S(1)}, u32[]{:S(2)}, u32[]{:S(2)}) collective-permute-start(f32[64,256]{1,0:T(8,128)S(1)} %get-tuple-element.60), channel_id=1, source_target_pairs={{0,1},{1,0},{2,3},{3,2},{4,5},{5,4},{6,7},{7,6},{8,9},{9,8},{10,11... | collective-permute-start | bytes 196616 | tf_op jit(solution)/shard_map/ppermute | solution.py:23
  72.7 4.7 %collective-permute-start.15 = (f32[64,256]{1,0:T(8,128)S(1)}, f32[64,256]{1,0:T(8,128)S(1)}, u32[]{:S(2)}, u32[]{:S(2)}) collective-permute-start(f32[64,256]{1,0:T(8,128)S(1)} %add.22.refs_3_), channel_id=1, source_target_pairs={{0,2},{1,3},{2,0},{3,1},{4,6},{5,7},{6,4},{7,5},{8,10},{9,11},{10,... | collective-permute-start | bytes 196616 | tf_op jit(solution)/shard_map/ppermute | solution.py:23
  87.3 3.7 %collective-permute-start.18 = (f32[56,256]{1,0:T(8,128)S(1)}, f32[56,256]{1,0:T(8,128)S(1)}, u32[]{:S(2)}, u32[]{:S(2)}) collective-permute-start(f32[56,256]{1,0:T(8,128)S(1)} %get-tuple-element.64), channel_id=1, source_target_pairs={{0,1},{1,0},{2,3},{3,2},{4,5},{5,4},{6,7},{7,6},{8,9},{9,8},{10,11... | collective-permute-start | bytes 172040 | tf_op jit(solution)/shard_map/ppermute | solution.py:23
  91.1 5.4 %collective-permute-start.19 = (f32[56,256]{1,0:T(8,128)S(1)}, f32[56,256]{1,0:T(8,128)S(1)}, u32[]{:S(2)}, u32[]{:S(2)}) collective-permute-start(f32[56,256]{1,0:T(8,128)S(1)} %add.23.refs_3_), channel_id=1, source_target_pairs={{0,2},{1,3},{2,0},{3,1},{4,6},{5,7},{6,4},{7,5},{8,10},{9,11},{10,... | collective-permute-start | bytes 172040 | tf_op jit(solution)/shard_map/ppermute | solution.py:23

commit v3 on v2

--- a/solution.py
+++ b/solution.py
@@ -13,9 +13,11 @@
 LEARN_RATE = 0.05
 EPSILON = 1e-08
 
-GROUPS = ((32, 32), (24, 32))
-BATCHES = ((0,), (1,))
+GROUPS = ((24, 24), (16, 24), (16, 16))
+BATCHES = ((0, 1), (2,))
 TILE = 384
+COST = 120
+RUN = 1152
 LANE_TILES = 27
 
 
@@ -239,16 +241,20 @@
 def last_kernel(row, pieces, n_operands, n_aliased, *refs):
     outs = refs[n_operands + n_aliased : n_operands + n_aliased + 3]
     weight_ref, held, sems = refs[-3:]
+    n_rows, width = held.shape[1:]
     copies = []
     weight_ref[...] = refs[5][0:1, 0:1] * (1.0 / 3.0)
 
-    def store(done, count, start, width, blocks):
-        lanes = pl.ds(start, width)
-        for which, (ref, block) in enumerate(zip(outs, blocks)):
-            held[which, pl.ds(done, count), lanes] = block
+    def store(done, count, start, size, blocks):
+        for which, block in enumerate(blocks):
+            held[which, pl.ds(done, count), pl.ds(start, size)] = block
+        if done + count < n_rows or (start + size) % RUN != 0:
+            return
+        lanes = pl.ds(start + size - RUN, RUN)
+        for which, ref in enumerate(outs):
             copy = pltpu.make_async_copy(
-                held.at[which, pl.ds(done, count), lanes],
-                ref.at[0, 0, pl.ds(row + done, count), lanes],
+                held.at[which, :, lanes],
+                ref.at[0, 0, pl.ds(row, n_rows), lanes],
                 sems.at[len(copies)],
             )
             copy.start()
@@ -260,7 +266,7 @@
 
 
 def update_cost(n_rows, tokens, width):
-    return pl.CostEstimate(flops=4 * n_rows * tokens * width, bytes_accessed=1 << 20, transcendentals=n_rows * width)
+    return pl.CostEstimate(flops=COST * n_rows * tokens * width, bytes_accessed=1 << 20, transcendentals=n_rows * width)
 
 
 def update_middle(row, operands, packed):
@@ -292,7 +298,7 @@
         out_shape=[jax.ShapeDtypeStruct(whole_shape, jnp.float32)] * 3 + [jax.ShapeDtypeStruct((1, 1), jnp.float32)],
         scratch_shapes=[
             pltpu.VMEM((3, n_rows, width), jnp.float32),
-            pltpu.SemaphoreType.DMA((3 * len(tiles(width)) * len(pieces),)),
+            pltpu.SemaphoreType.DMA((3 * width // RUN,)),
         ],
         input_output_aliases={len(operands) + which: which for which in range(len(previous))},
         compiler_params=pltpu.CompilerParams(vmem_limit_bytes=24 * 1024 * 1024),
@@ -321,7 +327,8 @@
     rows = []
     row = 0
     for group in GROUPS:
-        own.append(cut(numerator, weight, row, group, row == 0))
+        pieces = cut(numerator, weight, row, [count for count in group if count > 0], row == 0)
+        own.append(pieces if group[0] > 0 else (None, *pieces))
         rows.append(row)
         row += sum(group)
     inputs = load(inputs)
@@ -329,28 +336,29 @@
     results = []
     across = send(own[0][0], "rx", partner)
     along = send(own[0][1], "rx", into)
-    earlier = (inputs, own[1][0])
+    earlier = (inputs, *[group[1] for group in own[1:]])
     for g, (own_a, own_b) in enumerate(own):
+        if g > 0:
+            earlier = (mine,) if across is None else (across, mine)
         pair_sum = after(own_b, *earlier) + along
-        across_now = after(across, *earlier)
+        summed = send(pair_sum, "rx", partner)
+        count_a, count_b = GROUPS[g]
+        operands = (own_b, summed)
+        terms = ((count_b, ((0, 0), (1, 0))),)
+        if own_a is not None:
+            across_now = after(across, pair_sum)
+            operands += (own_a, across_now, send(across_now, "rx", out_of))
+            terms = ((count_a, ((2, 0), (3, 0), (4, 0))), *terms)
         if g + 1 < len(GROUPS):
             next_a, next_b = own[g + 1]
             along = send(after(next_b, pair_sum), "rx", into)
-            across = send(after(next_a, pair_sum), "rx", partner)
-        count_a, count_b = GROUPS[g]
-        total, pred, *tile = predict(
-            0,
-            inputs,
-            (own_a, across_now, send(across_now, "rx", out_of), own_b, send(pair_sum, "rx", partner)),
-            ((count_a, ((0, 0), (1, 0), (2, 0))), (count_b, ((3, 0), (4, 0)))),
-            (0, 1, 2) if g == 0 else (),
-        )
+            across = None if next_a is None else send(after(next_a, summed), "rx", partner)
+        total, pred, *tile = predict(0, inputs, operands, terms, (2, 3, 4) if g == 0 else ())
         if g == 0:
             (row_sum,) = tile
         mine, other = summed_over_ma(pred)
-        earlier = (other,)
         if g + 1 < len(GROUPS):
-            total = after(total, along, across)
+            total = after(total, along, *([] if across is None else [across]))
         values, first_mid, second_mid = update_middle(
             rows[g], (inputs, targets, total, mine, other, row_sum, first, second), g == 0
         )

time: 99.3 us -> 91.2 us (0.918)
  waiting for transfers between devices: 39.5 us -> 25.5 us
  starting transfers between devices: 43.6 us -> 47.6 us
  Pallas kernels: 14.3 us -> 16.1 us
    ppermute x20 -> x28, waiting for transfers between devices: 39.5 us -> 25.5 us  [send(): lax.ppermute(block, axis, [(i, target(i)) for i in range(lax.axis_size(ax...]
    ppermute x20 -> x28, starting transfers between devices: 43.6 us -> 47.6 us  [send(): lax.ppermute(block, axis, [(i, target(i)) for i in range(lax.axis_size(ax...]
    pallas_call x2 -> x3, Pallas kernels: 2.39 us -> 3.36 us  [cut(): pl.pallas_call(functools.partial(cut_kernel, row, counts, packed), in_spe...]
    pallas_call x4 -> x5, Pallas kernels: 2.81 us -> 3.6 us  [predict(): pl.pallas_call(functools.partial(predict_kernel, round_number, terms, n_r...]
    pallas_call x2 -> x3, Pallas kernels: 1.98 us -> 2.12 us  [update_middle(): pl.pallas_call(functools.partial(middle_kernel, row, ((n_rows, 0, row),),...]
  transfers between devices with their start and end apart: 20 -> 28, of which waited for: 14 -> 17; matrix products, arithmetic and copies ran while one was open for 0% -> 0% of each run, Pallas kernels for 9% -> 13%
where the time goes in v3:
time: 91.2 us; the launch traced here: 91 us
  starting transfers between devices  47.6 us (52%)
  waiting for transfers between devices  25.5 us (28%)
  Pallas kernels  16.1 us (18%)
  between operations  1.61 us (2%)
    ppermute x28, starting transfers between devices, send(): lax.ppermute(block, axis, [(i, target(i)) for i in range(lax.axis_size(ax...  47.6 us
    ppermute x28, waiting for transfers between devices, send(): lax.ppermute(block, axis, [(i, target(i)) for i in range(lax.axis_size(ax...  25.5 us
    pallas_call x2, Pallas kernels, update_last(): pl.pallas_call(functools.partial(last_kernel, row, pieces, len(operands),...  5.01 us
    pallas_call x5, Pallas kernels, predict(): pl.pallas_call(functools.partial(predict_kernel, round_number, terms, n_r...  3.6 us
    pallas_call x3, Pallas kernels, cut(): pl.pallas_call(functools.partial(cut_kernel, row, counts, packed), in_spe...  3.36 us
    pallas_call x3, Pallas kernels, update_middle(): pl.pallas_call(functools.partial(middle_kernel, row, ((n_rows, 0, row),),...  2.12 us
    pallas_call x1, Pallas kernels, load(): pl.pallas_call(load_kernel, in_specs=[pl.BlockSpec(memory_space=pltpu.HBM...  2.01 us
  transfers between devices with their start and end apart: 28, of which 17 were waited for; matrix products, arithmetic and copies ran while one was open for 0% of the time, Pallas kernels for 13%

profile of v3, /device:TPU:1, one launch (start us, length us, event | category | flops | bytes accessed | tf_op | source)
XLA Modules:
  0.0 91.0 jit_solution(15516541904913336964)
XLA Ops:
  1.3 1.2 %cut.5 = (f32[82,8,128]{2,1,0:T(8,128)S(1)}, f32[24,3456]{1,0:T(8,128)S(1)}) custom-call(f32[1,1,120,3456]{3,2,1,0:T(8,128)} %numerator_ref.5, f32[1,1]{1,0:T(1,128)S(6)} %copy.16.weight_ref), custom_call_target="tpu_custom_call" | custom-call | bytes 1048576 | tf_op jit(solution)/shard_map/cut/pallas_call | solution.py:171
  2.5 6.5 %collective-permute-start = (f32[24,3456]{1,0:T(8,128)S(1)}, f32[24,3456]{1,0:T(8,128)S(1)}, u32[]{:S(2)}, u32[]{:S(2)}) collective-permute-start(f32[24,3456]{1,0:T(8,128)S(1)} %get-tuple-element.60.refs_1_), channel_id=1, source_target_pairs={{0,224},{16,48},{32,0},{48,80},{64,32},{80,112},{96,64},{112,144},... | collective-permute-start | bytes 995336 | tf_op jit(solution)/shard_map/ppermute | solution.py:25
  10.0 1.1 %cut.4 = (f32[16,3456]{1,0:T(8,128)S(1)}, f32[24,3456]{1,0:T(8,128)S(1)}) custom-call(f32[1,1,120,3456]{3,2,1,0:T(8,128)} %numerator_ref.5, f32[1,1]{1,0:T(1,128)S(6)} %copy.16.weight_ref), custom_call_target="tpu_custom_call" | custom-call | bytes 1048576 | tf_op jit(solution)/shard_map/cut/pallas_call | solution.py:171
  11.1 2.0 %load.1.refs_0_ = bf16[1,1,2,256,3456]{4,3,2,1,0:T(8,128)(2,1)S(1)} custom-call(bf16[1,1,2,256,3456]{4,3,2,1,0:T(8,128)(2,1)} %inputs_ref.1), custom_call_target="tpu_custom_call" | custom-call | bytes 4194304 | tf_op jit(solution)/shard_map/load/pallas_call | solution.py:190
  13.2 2.3 %collective-permute-done = f32[24,3456]{1,0:T(8,128)S(1)} collective-permute-done((f32[24,3456]{1,0:T(8,128)S(1)}, f32[24,3456]{1,0:T(8,128)S(1)}, u32[]{:S(2)}, u32[]{:S(2)}) %collective-permute-start) | collective-permute-done | bytes 331808 | tf_op jit(solution)/shard_map/ppermute | solution.py:25
  15.5 2.4 %collective-permute-start.1 = (f32[24,3456]{1,0:T(8,128)S(1)}, f32[24,3456]{1,0:T(8,128)S(1)}, u32[]{:S(2)}, u32[]{:S(2)}) collective-permute-start(f32[24,3456]{1,0:T(8,128)S(1)} %add.24), channel_id=1, source_target_pairs={{0,16},{16,0},{32,48},{48,32},{64,80},{80,64},{96,112},{112,96},{1... | collective-permute-start | bytes 995336 | tf_op jit(solution)/shard_map/ppermute | solution.py:25
  17.9 2.7 %collective-permute-start.6 = (f32[24,3456]{1,0:T(8,128)S(1)}, f32[24,3456]{1,0:T(8,128)S(1)}, u32[]{:S(2)}, u32[]{:S(2)}) collective-permute-start(f32[24,3456]{1,0:T(8,128)S(1)} %get-tuple-element.66.refs_1_), channel_id=1, source_target_pairs={{0,224},{16,48},{32,0},{48,80},{64,32},{80,112},{96,64},{112,144},... | collective-permute-start | bytes 995336 | tf_op jit(solution)/shard_map/ppermute | solution.py:25
  20.6 4.2 %collective-permute-done.1.refs_2_ = f32[24,3456]{1,0:T(8,128)S(1)} collective-permute-done((f32[24,3456]{1,0:T(8,128)S(1)}, f32[24,3456]{1,0:T(8,128)S(1)}, u32[]{:S(2)}, u32[]{:S(2)}) %collective-permute-start.1) | collective-permute-done | bytes 331808 | tf_op jit(solution)/shard_map/ppermute | solution.py:25
  24.8 1.2 %collective-permute-start.2 = (f32[16,3456]{1,0:T(8,128)S(1)}, f32[16,3456]{1,0:T(8,128)S(1)}, u32[]{:S(2)}, u32[]{:S(2)}) collective-permute-start(f32[16,3456]{1,0:T(8,128)S(1)} %get-tuple-element.61.refs_3_), channel_id=1, source_target_pairs={{0,16},{16,0},{32,48},{48,32},{64,80},{80,64},{96,112},{112,96},{1... | collective-permute-start | bytes 663560 | tf_op jit(solution)/shard_map/ppermute | solution.py:25
  27.7 2.5 %collective-permute-start.5 = (f32[48,256]{1,0:T(8,128)S(1)}, f32[48,256]{1,0:T(8,128)S(1)}, u32[]{:S(2)}, u32[]{:S(2)}) collective-permute-start(f32[48,256]{1,0:T(8,128)S(1)} %get-tuple-element.64), channel_id=1, source_target_pairs={{0,1},{1,0},{2,3},{3,2},{4,5},{5,4},{6,7},{7,6},{8,9},{9,8},{10,11... | collective-permute-start | bytes 147464 | tf_op jit(solution)/shard_map/ppermute | solution.py:25
  31.1 2.7 %collective-permute-start.16 = (f32[48,256]{1,0:T(8,128)S(1)}, f32[48,256]{1,0:T(8,128)S(1)}, u32[]{:S(2)}, u32[]{:S(2)}) collective-permute-start(f32[48,256]{1,0:T(8,128)S(1)} %add.25.refs_3_), channel_id=1, source_target_pairs={{0,2},{1,3},{2,0},{3,1},{4,6},{5,7},{6,4},{7,5},{8,10},{9,11},{10,... | collective-permute-start | bytes 147464 | tf_op jit(solution)/shard_map/ppermute | solution.py:25
  34.0 1.6 %collective-permute-done.16.refs_4_ = f32[48,256]{1,0:T(8,128)S(1)} collective-permute-done((f32[48,256]{1,0:T(8,128)S(1)}, f32[48,256]{1,0:T(8,128)S(1)}, u32[]{:S(2)}, u32[]{:S(2)}) %collective-permute-start.16) | collective-permute-done | bytes 49184 | tf_op jit(solution)/shard_map/ppermute | solution.py:25
  36.4 2.6 %collective-permute-start.18 = (f32[163,8,128]{2,1,0:T(8,128)S(1)}, f32[163,8,128]{2,1,0:T(8,128)S(1)}, u32[]{:S(2)}, u32[]{:S(2)}) collective-permute-start(f32[163,8,128]{2,1,0:T(8,128)S(1)} %get-tuple-element.80.refs_1_), channel_id=1, source_target_pairs={{0,12},{4,0},{8,4},{12,8},{1,13},{5,1},{9,5},{13,9},{2,14},{6,2},{... | collective-permute-start | bytes 2002952 | tf_op jit(solution)/shard_map/ppermute | solution.py:25
  39.0 1.1 %collective-permute-start.11 = (f32[16,3456]{1,0:T(8,128)S(1)}, f32[16,3456]{1,0:T(8,128)S(1)}, u32[]{:S(2)}, u32[]{:S(2)}) collective-permute-start(f32[16,3456]{1,0:T(8,128)S(1)} %get-tuple-element.71.refs_1_), channel_id=1, source_target_pairs={{0,224},{16,48},{32,0},{48,80},{64,32},{80,112},{96,64},{112,144},... | collective-permute-start | bytes 663560 | tf_op jit(solution)/shard_map/ppermute | solution.py:25
  40.1 2.5 %collective-permute-done.7.refs_2_ = f32[24,3456]{1,0:T(8,128)S(1)} collective-permute-done((f32[24,3456]{1,0:T(8,128)S(1)}, f32[24,3456]{1,0:T(8,128)S(1)}, u32[]{:S(2)}, u32[]{:S(2)}) %collective-permute-start.7) | collective-permute-done | bytes 331808 | tf_op jit(solution)/shard_map/ppermute | solution.py:25
  42.6 1.2 %collective-permute-start.8 = (f32[16,3456]{1,0:T(8,128)S(1)}, f32[16,3456]{1,0:T(8,128)S(1)}, u32[]{:S(2)}, u32[]{:S(2)}) collective-permute-start(f32[16,3456]{1,0:T(8,128)S(1)} %get-tuple-element.67.refs_3_), channel_id=1, source_target_pairs={{0,16},{16,0},{32,48},{48,32},{64,80},{80,64},{96,112},{112,96},{1... | collective-permute-start | bytes 663560 | tf_op jit(solution)/shard_map/ppermute | solution.py:25
  44.5 1.6 %collective-permute-start.10 = (f32[40,256]{1,0:T(8,128)S(1)}, f32[40,256]{1,0:T(8,128)S(1)}, u32[]{:S(2)}, u32[]{:S(2)}) collective-permute-start(f32[40,256]{1,0:T(8,128)S(1)} %get-tuple-element.69), channel_id=1, source_target_pairs={{0,1},{1,0},{2,3},{3,2},{4,5},{5,4},{6,7},{7,6},{8,9},{9,8},{10,11... | collective-permute-start | bytes 122888 | tf_op jit(solution)/shard_map/ppermute | solution.py:25
  48.0 1.6 %collective-permute-start.12 = (f32[16,3456]{1,0:T(8,128)S(1)}, f32[16,3456]{1,0:T(8,128)S(1)}, u32[]{:S(2)}, u32[]{:S(2)}) collective-permute-start(f32[16,3456]{1,0:T(8,128)S(1)} %add.28), channel_id=1, source_target_pairs={{0,16},{16,0},{32,48},{48,32},{64,80},{80,64},{96,112},{112,96},{1... | collective-permute-start | bytes 663560 | tf_op jit(solution)/shard_map/ppermute | solution.py:25
  49.6 1.7 %collective-permute-done.19.refs_4_ = f32[40,256]{1,0:T(8,128)S(1)} collective-permute-done((f32[40,256]{1,0:T(8,128)S(1)}, f32[40,256]{1,0:T(8,128)S(1)}, u32[]{:S(2)}, u32[]{:S(2)}) %collective-permute-start.19) | collective-permute-done | bytes 40992 | tf_op jit(solution)/shard_map/ppermute | solution.py:25
  52.1 2.3 %collective-permute-done.17.refs_2_ = f32[163,8,128]{2,1,0:T(8,128)S(1)} collective-permute-done((f32[163,8,128]{2,1,0:T(8,128)S(1)}, f32[163,8,128]{2,1,0:T(8,128)S(1)}, u32[]{:S(2)}, u32[]{:S(2)}) %collective-permute-start.17) | collective-permute-done | bytes 667680 | tf_op jit(solution)/shard_map/ppermute | solution.py:25
  54.6 1.2 %collective-permute-start.20 = (f32[40,3456]{1,0:T(8,128)S(1)}, f32[40,3456]{1,0:T(8,128)S(1)}, u32[]{:S(2)}, u32[]{:S(2)}) collective-permute-start(f32[40,3456]{1,0:T(8,128)S(1)} %get-tuple-element.85.refs_4_), channel_id=1, source_target_pairs={{0,4},{4,8},{8,12},{12,0},{1,5},{5,9},{9,13},{13,1},{2,6},{6,10},{... | collective-permute-start | bytes 1658888 | tf_op jit(solution)/shard_map/ppermute | solution.py:25
  56.6 3.8 %collective-permute-start.14 = (f32[32,256]{1,0:T(8,128)S(1)}, f32[32,256]{1,0:T(8,128)S(1)}, u32[]{:S(2)}, u32[]{:S(2)}) collective-permute-start(f32[32,256]{1,0:T(8,128)S(1)} %get-tuple-element.74), channel_id=1, source_target_pairs={{0,1},{1,0},{2,3},{3,2},{4,5},{5,4},{6,7},{7,6},{8,9},{9,8},{10,11... | collective-permute-start | bytes 98312 | tf_op jit(solution)/shard_map/ppermute | solution.py:25
  61.3 2.6 %collective-permute-start.15 = (f32[32,256]{1,0:T(8,128)S(1)}, f32[32,256]{1,0:T(8,128)S(1)}, u32[]{:S(2)}, u32[]{:S(2)}) collective-permute-start(f32[32,256]{1,0:T(8,128)S(1)} %add.29.refs_3_), channel_id=1, source_target_pairs={{0,2},{1,3},{2,0},{3,1},{4,6},{5,7},{6,4},{7,5},{8,10},{9,11},{10,... | collective-permute-start | bytes 98312 | tf_op jit(solution)/shard_map/ppermute | solution.py:25
  63.9 1.6 %collective-permute-done.15.refs_4_ = f32[32,256]{1,0:T(8,128)S(1)} collective-permute-done((f32[32,256]{1,0:T(8,128)S(1)}, f32[32,256]{1,0:T(8,128)S(1)}, u32[]{:S(2)}, u32[]{:S(2)}) %collective-permute-start.15) | collective-permute-done | bytes 32800 | tf_op jit(solution)/shard_map/ppermute | solution.py:25
  66.6 2.1 %collective-permute-start.25 = (f32[32,3456]{1,0:T(8,128)S(1)}, f32[32,3456]{1,0:T(8,128)S(1)}, u32[]{:S(2)}, u32[]{:S(2)}) collective-permute-start(f32[32,3456]{1,0:T(8,128)S(1)} %get-tuple-element.88.refs_1_), channel_id=1, source_target_pairs={{0,12},{4,0},{8,4},{12,8},{1,13},{5,1},{9,5},{13,9},{2,14},{6,2},{... | collective-permute-start | bytes 1327112 | tf_op jit(solution)/shard_map/ppermute | solution.py:25
  69.6 4.2 %collective-permute-start.22 = (f32[88,256]{1,0:T(8,128)S(1)}, f32[88,256]{1,0:T(8,128)S(1)}, u32[]{:S(2)}, u32[]{:S(2)}) collective-permute-start(f32[88,256]{1,0:T(8,128)S(1)} %get-tuple-element.86), channel_id=1, source_target_pairs={{0,1},{1,0},{2,3},{3,2},{4,5},{5,4},{6,7},{7,6},{8,9},{9,8},{10,11... | collective-permute-start | bytes 270344 | tf_op jit(solution)/shard_map/ppermute | solution.py:25
  74.7 2.7 %collective-permute-start.23 = (f32[88,256]{1,0:T(8,128)S(1)}, f32[88,256]{1,0:T(8,128)S(1)}, u32[]{:S(2)}, u32[]{:S(2)}) collective-permute-start(f32[88,256]{1,0:T(8,128)S(1)} %add.30.refs_3_), channel_id=1, source_target_pairs={{0,2},{1,3},{2,0},{3,1},{4,6},{5,7},{6,4},{7,5},{8,10},{9,11},{10,... | collective-permute-start | bytes 270344 | tf_op jit(solution)/shard_map/ppermute | solution.py:25
  77.4 2.7 %collective-permute-done.23.refs_4_ = f32[88,256]{1,0:T(8,128)S(1)} collective-permute-done((f32[88,256]{1,0:T(8,128)S(1)}, f32[88,256]{1,0:T(8,128)S(1)}, u32[]{:S(2)}, u32[]{:S(2)}) %collective-permute-start.23) | collective-permute-done | bytes 90144 | tf_op jit(solution)/shard_map/ppermute | solution.py:25
  80.9 2.4 %collective-permute-start.26 = (f32[32,256]{1,0:T(8,128)S(1)}, f32[32,256]{1,0:T(8,128)S(1)}, u32[]{:S(2)}, u32[]{:S(2)}) collective-permute-start(f32[32,256]{1,0:T(8,128)S(1)} %get-tuple-element.90), channel_id=1, source_target_pairs={{0,1},{1,0},{2,3},{3,2},{4,5},{5,4},{6,7},{7,6},{8,9},{9,8},{10,11... | collective-permute-start | bytes 98312 | tf_op jit(solution)/shard_map/ppermute | solution.py:25
  84.1 1.7 %collective-permute-start.27 = (f32[32,256]{1,0:T(8,128)S(1)}, f32[32,256]{1,0:T(8,128)S(1)}, u32[]{:S(2)}, u32[]{:S(2)}) collective-permute-start(f32[32,256]{1,0:T(8,128)S(1)} %add.31.refs_3_), channel_id=1, source_target_pairs={{0,2},{1,3},{2,0},{3,1},{4,6},{5,7},{6,4},{7,5},{8,10},{9,11},{10,... | collective-permute-start | bytes 98312 | tf_op jit(solution)/shard_map/ppermute | solution.py:25
  85.8 3.0 %update1.2 = (f32[1,1,120,3456]{3,2,1,0:T(8,128)}, f32[1,1,120,3456]{3,2,1,0:T(8,128)}, f32[1,1,120,3456]{3,2,1,0:T(8,128)}, f32[1,1]{1,0:T(1,128)}) custom-call(bf16[1,1,2,256,3456]{4,3,2,1,0:T(8,128)(2,1)S(1)} %load.1.refs_0_, f32[1,1,2,120,256]{4,3,2,1,0:T(8,128)S(1)} %copy-done.2, f32[88,3456]{1,0:T(8,128)S(1)} %get-tuple-element.94.refs_2_, ...), custom_call_target="tpu_custom_call" | custom-call | flops 9342812160 | bytes 1048576 | tf_op jit(solution)/shard_map/update1/pallas_call | solution.py:294
  88.9 2.0 %update1.3 = (f32[1,1,120,3456]{3,2,1,0:T(8,128)}, f32[1,1,120,3456]{3,2,1,0:T(8,128)}, f32[1,1,120,3456]{3,2,1,0:T(8,128)}, f32[1,1]{1,0:T(1,128)}) custom-call(bf16[1,1,2,256,3456]{4,3,2,1,0:T(8,128)(2,1)S(1)} %load.1.refs_0_, f32[1,1,2,120,256]{4,3,2,1,0:T(8,128)S(1)} %copy-done.2, ...), custom_call_target="tpu_custom_call", output_to_operand_aliasing={{0}: (8, {}), {1}: (9, {}), {2}: (10, {})} | custom-call | flops 3397386240 | bytes 1048576 | tf_op jit(solution)/shard_map/update1/pallas_call | solution.py:294
  (52 shorter events, 14.4 us)
Async XLA Ops:
  2.5 12.9 %collective-permute-start = (f32[24,3456]{1,0:T(8,128)S(1)}, f32[24,3456]{1,0:T(8,128)S(1)}, u32[]{:S(2)}, u32[]{:S(2)}) collective-permute-start(f32[24,3456]{1,0:T(8,128)S(1)} %get-tuple-element.60.refs_1_), channel_id=1, source_target_pairs={{0,224},{16,48},{32,0},{48,80},{64,32},{80,112},{96,64},{112,144},... | collective-permute-start | bytes 995336 | tf_op jit(solution)/shard_map/ppermute | solution.py:25
  9.0 8.9 %collective-permute-start.3 = (f32[82,8,128]{2,1,0:T(8,128)S(1)}, f32[82,8,128]{2,1,0:T(8,128)S(1)}, u32[]{:S(2)}, u32[]{:S(2)}) collective-permute-start(f32[82,8,128]{2,1,0:T(8,128)S(1)} %get-tuple-element.62.refs_3_), channel_id=1, source_target_pairs={{0,16},{16,0},{32,48},{48,32},{64,80},{80,64},{96,112},{112,96},{1... | collective-permute-start | bytes 1007624 | tf_op jit(solution)/shard_map/ppermute | solution.py:25
  15.5 9.3 %collective-permute-start.1 = (f32[24,3456]{1,0:T(8,128)S(1)}, f32[24,3456]{1,0:T(8,128)S(1)}, u32[]{:S(2)}, u32[]{:S(2)}) collective-permute-start(f32[24,3456]{1,0:T(8,128)S(1)} %add.24), channel_id=1, source_target_pairs={{0,16},{16,0},{32,48},{48,32},{64,80},{80,64},{96,112},{112,96},{1... | collective-permute-start | bytes 995336 | tf_op jit(solution)/shard_map/ppermute | solution.py:25
  17.9 9.1 %collective-permute-start.4 = (f32[82,8,128]{2,1,0:T(8,128)S(1)}, f32[82,8,128]{2,1,0:T(8,128)S(1)}, u32[]{:S(2)}, u32[]{:S(2)}) collective-permute-start(f32[82,8,128]{2,1,0:T(8,128)S(1)} %collective-permute-done.3.refs_4_), channel_id=1, source_target_pairs={{0,32},{16,240},{32,64},{48,16},{64,96},{80,48},{96,128},{112,80},... | collective-permute-start | bytes 1007624 | tf_op jit(solution)/shard_map/ppermute | solution.py:25
  17.9 15.9 %collective-permute-start.6 = (f32[24,3456]{1,0:T(8,128)S(1)}, f32[24,3456]{1,0:T(8,128)S(1)}, u32[]{:S(2)}, u32[]{:S(2)}) collective-permute-start(f32[24,3456]{1,0:T(8,128)S(1)} %get-tuple-element.66.refs_1_), channel_id=1, source_target_pairs={{0,224},{16,48},{32,0},{48,80},{64,32},{80,112},{96,64},{112,144},... | collective-permute-start | bytes 995336 | tf_op jit(solution)/shard_map/ppermute | solution.py:25
  24.8 10.8 %copy-start = (f32[1,1,120,3456]{3,2,1,0:T(8,128)S(1)}, f32[1,1,120,3456]{3,2,1,0:T(8,128)}, u32[]{:S(2)}) copy-start(f32[1,1,120,3456]{3,2,1,0:T(8,128)} %param.10) | copy-start | bytes 4976644
  24.8 10.8 %copy-start.1 = (f32[1,1,120,3456]{3,2,1,0:T(8,128)S(1)}, f32[1,1,120,3456]{3,2,1,0:T(8,128)}, u32[]{:S(2)}) copy-start(f32[1,1,120,3456]{3,2,1,0:T(8,128)} %param.11) | copy-start | bytes 4976644
  24.8 10.8 %copy-start.2 = (f32[1,1,2,120,256]{4,3,2,1,0:T(8,128)S(1)}, f32[1,1,2,120,256]{4,3,2,1,0:T(8,128)}, u32[]{:S(2)}) copy-start(f32[1,1,2,120,256]{4,3,2,1,0:T(8,128)} %refs_1_.9) | copy-start | bytes 737284
  24.8 9.0 %collective-permute-start.2 = (f32[16,3456]{1,0:T(8,128)S(1)}, f32[16,3456]{1,0:T(8,128)S(1)}, u32[]{:S(2)}, u32[]{:S(2)}) collective-permute-start(f32[16,3456]{1,0:T(8,128)S(1)} %get-tuple-element.61.refs_3_), channel_id=1, source_target_pairs={{0,16},{16,0},{32,48},{48,32},{64,80},{80,64},{96,112},{112,96},{1... | collective-permute-start | bytes 663560 | tf_op jit(solution)/shard_map/ppermute | solution.py:25
  27.7 3.4 %collective-permute-start.5 = (f32[48,256]{1,0:T(8,128)S(1)}, f32[48,256]{1,0:T(8,128)S(1)}, u32[]{:S(2)}, u32[]{:S(2)}) collective-permute-start(f32[48,256]{1,0:T(8,128)S(1)} %get-tuple-element.64), channel_id=1, source_target_pairs={{0,1},{1,0},{2,3},{3,2},{4,5},{5,4},{6,7},{7,6},{8,9},{9,8},{10,11... | collective-permute-start | bytes 147464 | tf_op jit(solution)/shard_map/ppermute | solution.py:25
  31.1 4.5 %collective-permute-start.16 = (f32[48,256]{1,0:T(8,128)S(1)}, f32[48,256]{1,0:T(8,128)S(1)}, u32[]{:S(2)}, u32[]{:S(2)}) collective-permute-start(f32[48,256]{1,0:T(8,128)S(1)} %add.25.refs_3_), channel_id=1, source_target_pairs={{0,2},{1,3},{2,0},{3,1},{4,6},{5,7},{6,4},{7,5},{8,10},{9,11},{10,... | collective-permute-start | bytes 147464 | tf_op jit(solution)/shard_map/ppermute | solution.py:25
  33.8 8.7 %collective-permute-start.7 = (f32[24,3456]{1,0:T(8,128)S(1)}, f32[24,3456]{1,0:T(8,128)S(1)}, u32[]{:S(2)}, u32[]{:S(2)}) collective-permute-start(f32[24,3456]{1,0:T(8,128)S(1)} %add.26), channel_id=1, source_target_pairs={{0,16},{16,0},{32,48},{48,32},{64,80},{80,64},{96,112},{112,96},{1... | collective-permute-start | bytes 995336 | tf_op jit(solution)/shard_map/ppermute | solution.py:25
  33.9 9.9 %collective-permute-start.9 = (f32[16,3456]{1,0:T(8,128)S(1)}, f32[16,3456]{1,0:T(8,128)S(1)}, u32[]{:S(2)}, u32[]{:S(2)}) collective-permute-start(f32[16,3456]{1,0:T(8,128)S(1)} %collective-permute-done.2.refs_4_), channel_id=1, source_target_pairs={{0,32},{16,240},{32,64},{48,16},{64,96},{80,48},{96,128},{112,80},... | collective-permute-start | bytes 663560 | tf_op jit(solution)/shard_map/ppermute | solution.py:25
  36.4 15.6 %collective-permute-start.18 = (f32[163,8,128]{2,1,0:T(8,128)S(1)}, f32[163,8,128]{2,1,0:T(8,128)S(1)}, u32[]{:S(2)}, u32[]{:S(2)}) collective-permute-start(f32[163,8,128]{2,1,0:T(8,128)S(1)} %get-tuple-element.80.refs_1_), channel_id=1, source_target_pairs={{0,12},{4,0},{8,4},{12,8},{1,13},{5,1},{9,5},{13,9},{2,14},{6,2},{... | collective-permute-start | bytes 2002952 | tf_op jit(solution)/shard_map/ppermute | solution.py:25
  39.0 15.4 %collective-permute-start.17 = (f32[163,8,128]{2,1,0:T(8,128)S(1)}, f32[163,8,128]{2,1,0:T(8,128)S(1)}, u32[]{:S(2)}, u32[]{:S(2)}) collective-permute-start(f32[163,8,128]{2,1,0:T(8,128)S(1)} %get-tuple-element.80.refs_1_), channel_id=1, source_target_pairs={{0,4},{4,8},{8,12},{12,0},{1,5},{5,9},{9,13},{13,1},{2,6},{6,10},{... | collective-permute-start | bytes 2002952 | tf_op jit(solution)/shard_map/ppermute | solution.py:25
  39.0 8.3 %collective-permute-start.11 = (f32[16,3456]{1,0:T(8,128)S(1)}, f32[16,3456]{1,0:T(8,128)S(1)}, u32[]{:S(2)}, u32[]{:S(2)}) collective-permute-start(f32[16,3456]{1,0:T(8,128)S(1)} %get-tuple-element.71.refs_1_), channel_id=1, source_target_pairs={{0,224},{16,48},{32,0},{48,80},{64,32},{80,112},{96,64},{112,144},... | collective-permute-start | bytes 663560 | tf_op jit(solution)/shard_map/ppermute | solution.py:25
  42.6 5.4 %collective-permute-start.8 = (f32[16,3456]{1,0:T(8,128)S(1)}, f32[16,3456]{1,0:T(8,128)S(1)}, u32[]{:S(2)}, u32[]{:S(2)}) collective-permute-start(f32[16,3456]{1,0:T(8,128)S(1)} %get-tuple-element.67.refs_3_), channel_id=1, source_target_pairs={{0,16},{16,0},{32,48},{48,32},{64,80},{80,64},{96,112},{112,96},{1... | collective-permute-start | bytes 663560 | tf_op jit(solution)/shard_map/ppermute | solution.py:25
  44.5 2.5 %collective-permute-start.10 = (f32[40,256]{1,0:T(8,128)S(1)}, f32[40,256]{1,0:T(8,128)S(1)}, u32[]{:S(2)}, u32[]{:S(2)}) collective-permute-start(f32[40,256]{1,0:T(8,128)S(1)} %get-tuple-element.69), channel_id=1, source_target_pairs={{0,1},{1,0},{2,3},{3,2},{4,5},{5,4},{6,7},{7,6},{8,9},{9,8},{10,11... | collective-permute-start | bytes 122888 | tf_op jit(solution)/shard_map/ppermute | solution.py:25
  47.0 4.4 %collective-permute-start.19 = (f32[40,256]{1,0:T(8,128)S(1)}, f32[40,256]{1,0:T(8,128)S(1)}, u32[]{:S(2)}, u32[]{:S(2)}) collective-permute-start(f32[40,256]{1,0:T(8,128)S(1)} %add.27.refs_3_), channel_id=1, source_target_pairs={{0,2},{1,3},{2,0},{3,1},{4,6},{5,7},{6,4},{7,5},{8,10},{9,11},{10,... | collective-permute-start | bytes 122888 | tf_op jit(solution)/shard_map/ppermute | solution.py:25
  48.0 7.9 %collective-permute-start.12 = (f32[16,3456]{1,0:T(8,128)S(1)}, f32[16,3456]{1,0:T(8,128)S(1)}, u32[]{:S(2)}, u32[]{:S(2)}) collective-permute-start(f32[16,3456]{1,0:T(8,128)S(1)} %add.28), channel_id=1, source_target_pairs={{0,16},{16,0},{32,48},{48,32},{64,80},{80,64},{96,112},{112,96},{1... | collective-permute-start | bytes 663560 | tf_op jit(solution)/shard_map/ppermute | solution.py:25
  49.6 6.3 %collective-permute-start.13 = (f32[16,3456]{1,0:T(8,128)S(1)}, f32[16,3456]{1,0:T(8,128)S(1)}, u32[]{:S(2)}, u32[]{:S(2)}) collective-permute-start(f32[16,3456]{1,0:T(8,128)S(1)} %collective-permute-done.8.refs_4_), channel_id=1, source_target_pairs={{0,32},{16,240},{32,64},{48,16},{64,96},{80,48},{96,128},{112,80},... | collective-permute-start | bytes 663560 | tf_op jit(solution)/shard_map/ppermute | solution.py:25
  54.4 11.8 %collective-permute-start.21 = (f32[40,3456]{1,0:T(8,128)S(1)}, f32[40,3456]{1,0:T(8,128)S(1)}, u32[]{:S(2)}, u32[]{:S(2)}) collective-permute-start(f32[40,3456]{1,0:T(8,128)S(1)} %get-tuple-element.85.refs_4_), channel_id=1, source_target_pairs={{0,12},{4,0},{8,4},{12,8},{1,13},{5,1},{9,5},{13,9},{2,14},{6,2},{... | collective-permute-start | bytes 1658888 | tf_op jit(solution)/shard_map/ppermute | solution.py:25
  54.6 12.0 %collective-permute-start.20 = (f32[40,3456]{1,0:T(8,128)S(1)}, f32[40,3456]{1,0:T(8,128)S(1)}, u32[]{:S(2)}, u32[]{:S(2)}) collective-permute-start(f32[40,3456]{1,0:T(8,128)S(1)} %get-tuple-element.85.refs_4_), channel_id=1, source_target_pairs={{0,4},{4,8},{8,12},{12,0},{1,5},{5,9},{9,13},{13,1},{2,6},{6,10},{... | collective-permute-start | bytes 1658888 | tf_op jit(solution)/shard_map/ppermute | solution.py:25
  56.6 4.7 %collective-permute-start.14 = (f32[32,256]{1,0:T(8,128)S(1)}, f32[32,256]{1,0:T(8,128)S(1)}, u32[]{:S(2)}, u32[]{:S(2)}) collective-permute-start(f32[32,256]{1,0:T(8,128)S(1)} %get-tuple-element.74), channel_id=1, source_target_pairs={{0,1},{1,0},{2,3},{3,2},{4,5},{5,4},{6,7},{7,6},{8,9},{9,8},{10,11... | collective-permute-start | bytes 98312 | tf_op jit(solution)/shard_map/ppermute | solution.py:25
  61.3 4.3 %collective-permute-start.15 = (f32[32,256]{1,0:T(8,128)S(1)}, f32[32,256]{1,0:T(8,128)S(1)}, u32[]{:S(2)}, u32[]{:S(2)}) collective-permute-start(f32[32,256]{1,0:T(8,128)S(1)} %add.29.refs_3_), channel_id=1, source_target_pairs={{0,2},{1,3},{2,0},{3,1},{4,6},{5,7},{6,4},{7,5},{8,10},{9,11},{10,... | collective-permute-start | bytes 98312 | tf_op jit(solution)/shard_map/ppermute | solution.py:25
  66.6 13.5 %collective-permute-start.25 = (f32[32,3456]{1,0:T(8,128)S(1)}, f32[32,3456]{1,0:T(8,128)S(1)}, u32[]{:S(2)}, u32[]{:S(2)}) collective-permute-start(f32[32,3456]{1,0:T(8,128)S(1)} %get-tuple-element.88.refs_1_), channel_id=1, source_target_pairs={{0,12},{4,0},{8,4},{12,8},{1,13},{5,1},{9,5},{13,9},{2,14},{6,2},{... | collective-permute-start | bytes 1327112 | tf_op jit(solution)/shard_map/ppermute | solution.py:25
  68.7 11.5 %collective-permute-start.24 = (f32[32,3456]{1,0:T(8,128)S(1)}, f32[32,3456]{1,0:T(8,128)S(1)}, u32[]{:S(2)}, u32[]{:S(2)}) collective-permute-start(f32[32,3456]{1,0:T(8,128)S(1)} %get-tuple-element.88.refs_1_), channel_id=1, source_target_pairs={{0,4},{4,8},{8,12},{12,0},{1,5},{5,9},{9,13},{13,1},{2,6},{6,10},{... | collective-permute-start | bytes 1327112 | tf_op jit(solution)/shard_map/ppermute | solution.py:25
  69.6 5.1 %collective-permute-start.22 = (f32[88,256]{1,0:T(8,128)S(1)}, f32[88,256]{1,0:T(8,128)S(1)}, u32[]{:S(2)}, u32[]{:S(2)}) collective-permute-start(f32[88,256]{1,0:T(8,128)S(1)} %get-tuple-element.86), channel_id=1, source_target_pairs={{0,1},{1,0},{2,3},{3,2},{4,5},{5,4},{6,7},{7,6},{8,9},{9,8},{10,11... | collective-permute-start | bytes 270344 | tf_op jit(solution)/shard_map/ppermute | solution.py:25
  74.7 5.4 %collective-permute-start.23 = (f32[88,256]{1,0:T(8,128)S(1)}, f32[88,256]{1,0:T(8,128)S(1)}, u32[]{:S(2)}, u32[]{:S(2)}) collective-permute-start(f32[88,256]{1,0:T(8,128)S(1)} %add.30.refs_3_), channel_id=1, source_target_pairs={{0,2},{1,3},{2,0},{3,1},{4,6},{5,7},{6,4},{7,5},{8,10},{9,11},{10,... | collective-permute-start | bytes 270344 | tf_op jit(solution)/shard_map/ppermute | solution.py:25
  80.9 3.3 %collective-permute-start.26 = (f32[32,256]{1,0:T(8,128)S(1)}, f32[32,256]{1,0:T(8,128)S(1)}, u32[]{:S(2)}, u32[]{:S(2)}) collective-permute-start(f32[32,256]{1,0:T(8,128)S(1)} %get-tuple-element.90), channel_id=1, source_target_pairs={{0,1},{1,0},{2,3},{3,2},{4,5},{5,4},{6,7},{7,6},{8,9},{9,8},{10,11... | collective-permute-start | bytes 98312 | tf_op jit(solution)/shard_map/ppermute | solution.py:25
  84.1 4.7 %collective-permute-start.27 = (f32[32,256]{1,0:T(8,128)S(1)}, f32[32,256]{1,0:T(8,128)S(1)}, u32[]{:S(2)}, u32[]{:S(2)}) collective-permute-start(f32[32,256]{1,0:T(8,128)S(1)} %add.31.refs_3_), channel_id=1, source_target_pairs={{0,2},{1,3},{2,0},{3,1},{4,6},{5,7},{6,4},{7,5},{8,10},{9,11},{10,... | collective-permute-start | bytes 98312 | tf_op jit(solution)/shard_map/ppermute | solution.py:25

commit v4 on v3

--- a/solution.py
+++ b/solution.py
@@ -200,12 +200,16 @@
 
 
 def update_tiles(round_number, row, pieces, refs, store):
-    inputs_ref, targets_ref, total_ref, mine_ref, other_ref, scale_ref, *moments = refs
-    n_rows, tokens = mine_ref.shape
+    inputs_ref, targets_ref, total_ref, scale_ref, *rest = refs
+    moments, preds = rest[: 2 * len(pieces)], rest[2 * len(pieces) :]
+    n_rows, tokens = preds[0].shape
+    predicted = preds[0][...]
+    for ref in preds[1:]:
+        predicted = predicted + ref[...]
     scale = jnp.concatenate([scale_ref[0:1, :]] * (TILE // 128), axis=1)
     inverse = 1.0 / scale
     scale = scale * (1.0 / 3.0)
-    residual = (mine_ref[...] + other_ref[...]) * inverse[:, :tokens]
+    residual = predicted * inverse[:, :tokens]
     residual = two_parts(residual - targets_ref[0, 0, round_number, pl.ds(row, n_rows), :])
     for start, width in tiles(total_ref.shape[1]):
         lanes = pl.ds(start, width)
@@ -235,7 +239,7 @@
 
     update_tiles(0, row, pieces, refs[:n_operands], store)
     if len(outs[0].shape) == 3:
-        outs[0][outs[0].shape[0] - 1] = refs[5][...]
+        outs[0][outs[0].shape[0] - 1] = refs[3][...]
 
 
 def last_kernel(row, pieces, n_operands, n_aliased, *refs):
@@ -243,7 +247,7 @@
     weight_ref, held, sems = refs[-3:]
     n_rows, width = held.shape[1:]
     copies = []
-    weight_ref[...] = refs[5][0:1, 0:1] * (1.0 / 3.0)
+    weight_ref[...] = refs[3][0:1, 0:1] * (1.0 / 3.0)
 
     def store(done, count, start, size, blocks):
         for which, block in enumerate(blocks):
@@ -310,6 +314,10 @@
 def summed_over_ma(pred):
     pair = pred + send(pred, "ma", lambda i: i ^ 1)
     return pair, send(pair, "ma", lambda i: i ^ 2)
+
+
+def gathered_over_ma(pred):
+    return (pred, *[send(pred, "ma", functools.partial(lambda turn, i: i ^ turn, turn)) for turn in (3, 2, 1)])
 
 
 def neighbours(block, axis):
@@ -360,7 +368,7 @@
         if g + 1 < len(GROUPS):
             total = after(total, along, *([] if across is None else [across]))
         values, first_mid, second_mid = update_middle(
-            rows[g], (inputs, targets, total, mine, other, row_sum, first, second), g == 0
+            rows[g], (inputs, targets, total, row_sum, first, second, mine, other), g == 0
         )
         ready = after(values, *results[-1][1:3]) if g > 0 else values
         results.append((values, *neighbours(ready, "ry"), first_mid, second_mid))
@@ -377,12 +385,13 @@
         total, pred, *tile = predict(1, inputs, tuple(operands), tuple(terms), (0, 1, 2) if not outs else ())
         if not outs:
             (column_sum,) = tile
-        mine, other = summed_over_ma(pred)
+        preds = gathered_over_ma(pred) if outs else summed_over_ma(pred)
+        other = preds[-1]
         moments = [block for g in batch for block in results[g][3:]]
         outs = update_last(
             rows[batch[0]],
             tuple((sum(GROUPS[g]), which, 0) for which, g in enumerate(batch)),
-            (inputs, targets, total, mine, other, column_sum, *moments),
+            (inputs, targets, total, column_sum, *moments, *preds),
             numerator.shape,
             outs[:3],
         )

time: 91.2 us -> 92.1 us (level)
  starting transfers between devices: 47.6 us -> 49.1 us
    ppermute x28 -> x29, starting transfers between devices: 47.6 us -> 49.1 us  [send(): lax.ppermute(block, axis, [(i, target(i)) for i in range(lax.axis_size(ax...]
    ppermute x28 -> x29, waiting for transfers between devices: 25.5 us -> 24.9 us  [send(): lax.ppermute(block, axis, [(i, target(i)) for i in range(lax.axis_size(ax...]
  transfers between devices with their start and end apart: 28 -> 29, of which waited for: 17 -> 17; matrix products, arithmetic and copies ran while one was open for 0% -> 0% of each run, Pallas kernels for 13% -> 13%
where the time goes in v4:
time: 92.1 us; the launch traced here: 91.9 us
  starting transfers between devices  49.1 us (53%)
  waiting for transfers between devices  24.9 us (27%)
  Pallas kernels  16.1 us (17%)
  between operations  1.61 us (2%)
    ppermute x29, starting transfers between devices, send(): lax.ppermute(block, axis, [(i, target(i)) for i in range(lax.axis_size(ax...  49.1 us
    ppermute x29, waiting for transfers between devices, send(): lax.ppermute(block, axis, [(i, target(i)) for i in range(lax.axis_size(ax...  24.9 us
    pallas_call x2, Pallas kernels, update_last(): pl.pallas_call(functools.partial(last_kernel, row, pieces, len(operands),...  5.01 us
    pallas_call x5, Pallas kernels, predict(): pl.pallas_call(functools.partial(predict_kernel, round_number, terms, n_r...  3.61 us
    pallas_call x3, Pallas kernels, cut(): pl.pallas_call(functools.partial(cut_kernel, row, counts, packed), in_spe...  3.36 us
    pallas_call x3, Pallas kernels, update_middle(): pl.pallas_call(functools.partial(middle_kernel, row, ((n_rows, 0, row),),...  2.11 us
    pallas_call x1, Pallas kernels, load(): pl.pallas_call(load_kernel, in_specs=[pl.BlockSpec(memory_space=pltpu.HBM...  2.01 us
  transfers between devices with their start and end apart: 29, of which 17 were waited for; matrix products, arithmetic and copies ran while one was open for 0% of the time, Pallas kernels for 13%

profile of v4, /device:TPU:1, one launch (start us, length us, event | category | flops | bytes accessed | tf_op | source)
XLA Modules:
  0.0 91.9 jit_solution(13897102454307459497)
XLA Ops:
  1.3 1.2 %cut.5 = (f32[82,8,128]{2,1,0:T(8,128)S(1)}, f32[24,3456]{1,0:T(8,128)S(1)}) custom-call(f32[1,1,120,3456]{3,2,1,0:T(8,128)} %numerator_ref.5, f32[1,1]{1,0:T(1,128)S(6)} %copy.16.weight_ref), custom_call_target="tpu_custom_call" | custom-call | bytes 1048576 | tf_op jit(solution)/shard_map/cut/pallas_call | solution.py:171
  2.5 6.5 %collective-permute-start = (f32[24,3456]{1,0:T(8,128)S(1)}, f32[24,3456]{1,0:T(8,128)S(1)}, u32[]{:S(2)}, u32[]{:S(2)}) collective-permute-start(f32[24,3456]{1,0:T(8,128)S(1)} %get-tuple-element.60.refs_1_), channel_id=1, source_target_pairs={{0,224},{16,48},{32,0},{48,80},{64,32},{80,112},{96,64},{112,144},... | collective-permute-start | bytes 995336 | tf_op jit(solution)/shard_map/ppermute | solution.py:25
  10.0 1.1 %cut.4 = (f32[16,3456]{1,0:T(8,128)S(1)}, f32[24,3456]{1,0:T(8,128)S(1)}) custom-call(f32[1,1,120,3456]{3,2,1,0:T(8,128)} %numerator_ref.5, f32[1,1]{1,0:T(1,128)S(6)} %copy.16.weight_ref), custom_call_target="tpu_custom_call" | custom-call | bytes 1048576 | tf_op jit(solution)/shard_map/cut/pallas_call | solution.py:171
  11.1 2.0 %load.1.refs_0_ = bf16[1,1,2,256,3456]{4,3,2,1,0:T(8,128)(2,1)S(1)} custom-call(bf16[1,1,2,256,3456]{4,3,2,1,0:T(8,128)(2,1)} %inputs_ref.1), custom_call_target="tpu_custom_call" | custom-call | bytes 4194304 | tf_op jit(solution)/shard_map/load/pallas_call | solution.py:190
  13.2 2.3 %collective-permute-done = f32[24,3456]{1,0:T(8,128)S(1)} collective-permute-done((f32[24,3456]{1,0:T(8,128)S(1)}, f32[24,3456]{1,0:T(8,128)S(1)}, u32[]{:S(2)}, u32[]{:S(2)}) %collective-permute-start) | collective-permute-done | bytes 331808 | tf_op jit(solution)/shard_map/ppermute | solution.py:25
  15.5 2.4 %collective-permute-start.1 = (f32[24,3456]{1,0:T(8,128)S(1)}, f32[24,3456]{1,0:T(8,128)S(1)}, u32[]{:S(2)}, u32[]{:S(2)}) collective-permute-start(f32[24,3456]{1,0:T(8,128)S(1)} %add.21), channel_id=1, source_target_pairs={{0,16},{16,0},{32,48},{48,32},{64,80},{80,64},{96,112},{112,96},{1... | collective-permute-start | bytes 995336 | tf_op jit(solution)/shard_map/ppermute | solution.py:25
  17.9 2.7 %collective-permute-start.6 = (f32[24,3456]{1,0:T(8,128)S(1)}, f32[24,3456]{1,0:T(8,128)S(1)}, u32[]{:S(2)}, u32[]{:S(2)}) collective-permute-start(f32[24,3456]{1,0:T(8,128)S(1)} %get-tuple-element.66.refs_1_), channel_id=1, source_target_pairs={{0,224},{16,48},{32,0},{48,80},{64,32},{80,112},{96,64},{112,144},... | collective-permute-start | bytes 995336 | tf_op jit(solution)/shard_map/ppermute | solution.py:25
  20.6 4.2 %collective-permute-done.1.refs_2_ = f32[24,3456]{1,0:T(8,128)S(1)} collective-permute-done((f32[24,3456]{1,0:T(8,128)S(1)}, f32[24,3456]{1,0:T(8,128)S(1)}, u32[]{:S(2)}, u32[]{:S(2)}) %collective-permute-start.1) | collective-permute-done | bytes 331808 | tf_op jit(solution)/shard_map/ppermute | solution.py:25
  24.8 1.2 %collective-permute-start.2 = (f32[16,3456]{1,0:T(8,128)S(1)}, f32[16,3456]{1,0:T(8,128)S(1)}, u32[]{:S(2)}, u32[]{:S(2)}) collective-permute-start(f32[16,3456]{1,0:T(8,128)S(1)} %get-tuple-element.61.refs_3_), channel_id=1, source_target_pairs={{0,16},{16,0},{32,48},{48,32},{64,80},{80,64},{96,112},{112,96},{1... | collective-permute-start | bytes 663560 | tf_op jit(solution)/shard_map/ppermute | solution.py:25
  27.7 2.5 %collective-permute-start.5 = (f32[48,256]{1,0:T(8,128)S(1)}, f32[48,256]{1,0:T(8,128)S(1)}, u32[]{:S(2)}, u32[]{:S(2)}) collective-permute-start(f32[48,256]{1,0:T(8,128)S(1)} %get-tuple-element.64), channel_id=1, source_target_pairs={{0,1},{1,0},{2,3},{3,2},{4,5},{5,4},{6,7},{7,6},{8,9},{9,8},{10,11... | collective-permute-start | bytes 147464 | tf_op jit(solution)/shard_map/ppermute | solution.py:25
  31.1 2.7 %collective-permute-start.16 = (f32[48,256]{1,0:T(8,128)S(1)}, f32[48,256]{1,0:T(8,128)S(1)}, u32[]{:S(2)}, u32[]{:S(2)}) collective-permute-start(f32[48,256]{1,0:T(8,128)S(1)} %add.22.refs_6_), channel_id=1, source_target_pairs={{0,2},{1,3},{2,0},{3,1},{4,6},{5,7},{6,4},{7,5},{8,10},{9,11},{10,... | collective-permute-start | bytes 147464 | tf_op jit(solution)/shard_map/ppermute | solution.py:25
  34.0 1.6 %collective-permute-done.16.refs_7_ = f32[48,256]{1,0:T(8,128)S(1)} collective-permute-done((f32[48,256]{1,0:T(8,128)S(1)}, f32[48,256]{1,0:T(8,128)S(1)}, u32[]{:S(2)}, u32[]{:S(2)}) %collective-permute-start.16) | collective-permute-done | bytes 49184 | tf_op jit(solution)/shard_map/ppermute | solution.py:25
  36.4 2.6 %collective-permute-start.18 = (f32[163,8,128]{2,1,0:T(8,128)S(1)}, f32[163,8,128]{2,1,0:T(8,128)S(1)}, u32[]{:S(2)}, u32[]{:S(2)}) collective-permute-start(f32[163,8,128]{2,1,0:T(8,128)S(1)} %get-tuple-element.80.refs_1_), channel_id=1, source_target_pairs={{0,12},{4,0},{8,4},{12,8},{1,13},{5,1},{9,5},{13,9},{2,14},{6,2},{... | collective-permute-start | bytes 2002952 | tf_op jit(solution)/shard_map/ppermute | solution.py:25
  40.1 2.5 %collective-permute-done.7.refs_2_ = f32[24,3456]{1,0:T(8,128)S(1)} collective-permute-done((f32[24,3456]{1,0:T(8,128)S(1)}, f32[24,3456]{1,0:T(8,128)S(1)}, u32[]{:S(2)}, u32[]{:S(2)}) %collective-permute-start.7) | collective-permute-done | bytes 331808 | tf_op jit(solution)/shard_map/ppermute | solution.py:25
  42.6 1.2 %collective-permute-start.8 = (f32[16,3456]{1,0:T(8,128)S(1)}, f32[16,3456]{1,0:T(8,128)S(1)}, u32[]{:S(2)}, u32[]{:S(2)}) collective-permute-start(f32[16,3456]{1,0:T(8,128)S(1)} %get-tuple-element.67.refs_3_), channel_id=1, source_target_pairs={{0,16},{16,0},{32,48},{48,32},{64,80},{80,64},{96,112},{112,96},{1... | collective-permute-start | bytes 663560 | tf_op jit(solution)/shard_map/ppermute | solution.py:25
  44.5 1.6 %collective-permute-start.10 = (f32[40,256]{1,0:T(8,128)S(1)}, f32[40,256]{1,0:T(8,128)S(1)}, u32[]{:S(2)}, u32[]{:S(2)}) collective-permute-start(f32[40,256]{1,0:T(8,128)S(1)} %get-tuple-element.69), channel_id=1, source_target_pairs={{0,1},{1,0},{2,3},{3,2},{4,5},{5,4},{6,7},{7,6},{8,9},{9,8},{10,11... | collective-permute-start | bytes 122888 | tf_op jit(solution)/shard_map/ppermute | solution.py:25
  48.0 1.6 %collective-permute-start.12 = (f32[16,3456]{1,0:T(8,128)S(1)}, f32[16,3456]{1,0:T(8,128)S(1)}, u32[]{:S(2)}, u32[]{:S(2)}) collective-permute-start(f32[16,3456]{1,0:T(8,128)S(1)} %add.25), channel_id=1, source_target_pairs={{0,16},{16,0},{32,48},{48,32},{64,80},{80,64},{96,112},{112,96},{1... | collective-permute-start | bytes 663560 | tf_op jit(solution)/shard_map/ppermute | solution.py:25
  49.6 1.7 %collective-permute-done.19.refs_7_ = f32[40,256]{1,0:T(8,128)S(1)} collective-permute-done((f32[40,256]{1,0:T(8,128)S(1)}, f32[40,256]{1,0:T(8,128)S(1)}, u32[]{:S(2)}, u32[]{:S(2)}) %collective-permute-start.19) | collective-permute-done | bytes 40992 | tf_op jit(solution)/shard_map/ppermute | solution.py:25
  52.1 2.3 %collective-permute-done.17.refs_2_ = f32[163,8,128]{2,1,0:T(8,128)S(1)} collective-permute-done((f32[163,8,128]{2,1,0:T(8,128)S(1)}, f32[163,8,128]{2,1,0:T(8,128)S(1)}, u32[]{:S(2)}, u32[]{:S(2)}) %collective-permute-start.17) | collective-permute-done | bytes 667680 | tf_op jit(solution)/shard_map/ppermute | solution.py:25
  54.6 1.2 %collective-permute-start.20 = (f32[40,3456]{1,0:T(8,128)S(1)}, f32[40,3456]{1,0:T(8,128)S(1)}, u32[]{:S(2)}, u32[]{:S(2)}) collective-permute-start(f32[40,3456]{1,0:T(8,128)S(1)} %get-tuple-element.85.refs_4_), channel_id=1, source_target_pairs={{0,4},{4,8},{8,12},{12,0},{1,5},{5,9},{9,13},{13,1},{2,6},{6,10},{... | collective-permute-start | bytes 1658888 | tf_op jit(solution)/shard_map/ppermute | solution.py:25
  56.6 3.8 %collective-permute-start.14 = (f32[32,256]{1,0:T(8,128)S(1)}, f32[32,256]{1,0:T(8,128)S(1)}, u32[]{:S(2)}, u32[]{:S(2)}) collective-permute-start(f32[32,256]{1,0:T(8,128)S(1)} %get-tuple-element.75), channel_id=1, source_target_pairs={{0,1},{1,0},{2,3},{3,2},{4,5},{5,4},{6,7},{7,6},{8,9},{9,8},{10,11... | collective-permute-start | bytes 98312 | tf_op jit(solution)/shard_map/ppermute | solution.py:25
  61.3 2.6 %collective-permute-start.15 = (f32[32,256]{1,0:T(8,128)S(1)}, f32[32,256]{1,0:T(8,128)S(1)}, u32[]{:S(2)}, u32[]{:S(2)}) collective-permute-start(f32[32,256]{1,0:T(8,128)S(1)} %add.26.refs_6_), channel_id=1, source_target_pairs={{0,2},{1,3},{2,0},{3,1},{4,6},{5,7},{6,4},{7,5},{8,10},{9,11},{10,... | collective-permute-start | bytes 98312 | tf_op jit(solution)/shard_map/ppermute | solution.py:25
  63.9 1.6 %collective-permute-done.15.refs_7_ = f32[32,256]{1,0:T(8,128)S(1)} collective-permute-done((f32[32,256]{1,0:T(8,128)S(1)}, f32[32,256]{1,0:T(8,128)S(1)}, u32[]{:S(2)}, u32[]{:S(2)}) %collective-permute-start.15) | collective-permute-done | bytes 32800 | tf_op jit(solution)/shard_map/ppermute | solution.py:25
  66.6 2.1 %collective-permute-start.25 = (f32[32,3456]{1,0:T(8,128)S(1)}, f32[32,3456]{1,0:T(8,128)S(1)}, u32[]{:S(2)}, u32[]{:S(2)}) collective-permute-start(f32[32,3456]{1,0:T(8,128)S(1)} %get-tuple-element.88.refs_1_), channel_id=1, source_target_pairs={{0,12},{4,0},{8,4},{12,8},{1,13},{5,1},{9,5},{13,9},{2,14},{6,2},{... | collective-permute-start | bytes 1327112 | tf_op jit(solution)/shard_map/ppermute | solution.py:25
  69.6 4.2 %collective-permute-start.22 = (f32[88,256]{1,0:T(8,128)S(1)}, f32[88,256]{1,0:T(8,128)S(1)}, u32[]{:S(2)}, u32[]{:S(2)}) collective-permute-start(f32[88,256]{1,0:T(8,128)S(1)} %get-tuple-element.86), channel_id=1, source_target_pairs={{0,1},{1,0},{2,3},{3,2},{4,5},{5,4},{6,7},{7,6},{8,9},{9,8},{10,11... | collective-permute-start | bytes 270344 | tf_op jit(solution)/shard_map/ppermute | solution.py:25
  74.7 2.7 %collective-permute-start.23 = (f32[88,256]{1,0:T(8,128)S(1)}, f32[88,256]{1,0:T(8,128)S(1)}, u32[]{:S(2)}, u32[]{:S(2)}) collective-permute-start(f32[88,256]{1,0:T(8,128)S(1)} %add.27.refs_8_), channel_id=1, source_target_pairs={{0,2},{1,3},{2,0},{3,1},{4,6},{5,7},{6,4},{7,5},{8,10},{9,11},{10,... | collective-permute-start | bytes 270344 | tf_op jit(solution)/shard_map/ppermute | solution.py:25
  77.4 2.7 %collective-permute-done.23.refs_9_ = f32[88,256]{1,0:T(8,128)S(1)} collective-permute-done((f32[88,256]{1,0:T(8,128)S(1)}, f32[88,256]{1,0:T(8,128)S(1)}, u32[]{:S(2)}, u32[]{:S(2)}) %collective-permute-start.23) | collective-permute-done | bytes 90144 | tf_op jit(solution)/shard_map/ppermute | solution.py:25
  80.9 2.4 %collective-permute-start.28 = (f32[32,256]{1,0:T(8,128)S(1)}, f32[32,256]{1,0:T(8,128)S(1)}, u32[]{:S(2)}, u32[]{:S(2)}) collective-permute-start(f32[32,256]{1,0:T(8,128)S(1)} %get-tuple-element.93.refs_6_), channel_id=1, source_target_pairs={{0,1},{1,0},{2,3},{3,2},{4,5},{5,4},{6,7},{7,6},{8,9},{9,8},{10,11... | collective-permute-start | bytes 98312 | tf_op jit(solution)/shard_map/ppermute | solution.py:25
  83.3 1.7 %collective-permute-start.27 = (f32[32,256]{1,0:T(8,128)S(1)}, f32[32,256]{1,0:T(8,128)S(1)}, u32[]{:S(2)}, u32[]{:S(2)}) collective-permute-start(f32[32,256]{1,0:T(8,128)S(1)} %get-tuple-element.93.refs_6_), channel_id=1, source_target_pairs={{0,2},{1,3},{2,0},{3,1},{4,6},{5,7},{6,4},{7,5},{8,10},{9,11},{10,... | collective-permute-start | bytes 98312 | tf_op jit(solution)/shard_map/ppermute | solution.py:25
  84.9 1.6 %collective-permute-start.26 = (f32[32,256]{1,0:T(8,128)S(1)}, f32[32,256]{1,0:T(8,128)S(1)}, u32[]{:S(2)}, u32[]{:S(2)}) collective-permute-start(f32[32,256]{1,0:T(8,128)S(1)} %get-tuple-element.93.refs_6_), channel_id=1, source_target_pairs={{0,3},{1,2},{2,1},{3,0},{4,7},{5,6},{6,5},{7,4},{8,11},{9,10},{10,... | collective-permute-start | bytes 98312 | tf_op jit(solution)/shard_map/ppermute | solution.py:25
  86.5 3.0 %update1.2 = (f32[1,1,120,3456]{3,2,1,0:T(8,128)}, f32[1,1,120,3456]{3,2,1,0:T(8,128)}, f32[1,1,120,3456]{3,2,1,0:T(8,128)}, f32[1,1]{1,0:T(1,128)}) custom-call(bf16[1,1,2,256,3456]{4,3,2,1,0:T(8,128)(2,1)S(1)} %load.1.refs_0_, f32[1,1,2,120,256]{4,3,2,1,0:T(8,128)S(1)} %copy-done.2, f32[88,3456]{1,0:T(8,128)S(1)} %get-tuple-element.94.refs_2_, ...), custom_call_target="tpu_custom_call" | custom-call | flops 9342812160 | bytes 1048576 | tf_op jit(solution)/shard_map/update1/pallas_call | solution.py:298
  89.8 2.0 %update1.3 = (f32[1,1,120,3456]{3,2,1,0:T(8,128)}, f32[1,1,120,3456]{3,2,1,0:T(8,128)}, f32[1,1,120,3456]{3,2,1,0:T(8,128)}, f32[1,1]{1,0:T(1,128)}) custom-call(bf16[1,1,2,256,3456]{4,3,2,1,0:T(8,128)(2,1)S(1)} %load.1.refs_0_, f32[1,1,2,120,256]{4,3,2,1,0:T(8,128)S(1)} %copy-done.2, ...), custom_call_target="tpu_custom_call", output_to_operand_aliasing={{0}: (10, {}), {1}: (11, {}), {2}: (12, {})} | custom-call | flops 3397386240 | bytes 1048576 | tf_op jit(solution)/shard_map/update1/pallas_call | solution.py:298
  (53 shorter events, 14.9 us)
Async XLA Ops:
  2.5 12.9 %collective-permute-start = (f32[24,3456]{1,0:T(8,128)S(1)}, f32[24,3456]{1,0:T(8,128)S(1)}, u32[]{:S(2)}, u32[]{:S(2)}) collective-permute-start(f32[24,3456]{1,0:T(8,128)S(1)} %get-tuple-element.60.refs_1_), channel_id=1, source_target_pairs={{0,224},{16,48},{32,0},{48,80},{64,32},{80,112},{96,64},{112,144},... | collective-permute-start | bytes 995336 | tf_op jit(solution)/shard_map/ppermute | solution.py:25
  9.0 8.9 %collective-permute-start.3 = (f32[82,8,128]{2,1,0:T(8,128)S(1)}, f32[82,8,128]{2,1,0:T(8,128)S(1)}, u32[]{:S(2)}, u32[]{:S(2)}) collective-permute-start(f32[82,8,128]{2,1,0:T(8,128)S(1)} %get-tuple-element.62.refs_3_), channel_id=1, source_target_pairs={{0,16},{16,0},{32,48},{48,32},{64,80},{80,64},{96,112},{112,96},{1... | collective-permute-start | bytes 1007624 | tf_op jit(solution)/shard_map/ppermute | solution.py:25
  15.5 9.3 %collective-permute-start.1 = (f32[24,3456]{1,0:T(8,128)S(1)}, f32[24,3456]{1,0:T(8,128)S(1)}, u32[]{:S(2)}, u32[]{:S(2)}) collective-permute-start(f32[24,3456]{1,0:T(8,128)S(1)} %add.21), channel_id=1, source_target_pairs={{0,16},{16,0},{32,48},{48,32},{64,80},{80,64},{96,112},{112,96},{1... | collective-permute-start | bytes 995336 | tf_op jit(solution)/shard_map/ppermute | solution.py:25
  17.9 9.1 %collective-permute-start.4 = (f32[82,8,128]{2,1,0:T(8,128)S(1)}, f32[82,8,128]{2,1,0:T(8,128)S(1)}, u32[]{:S(2)}, u32[]{:S(2)}) collective-permute-start(f32[82,8,128]{2,1,0:T(8,128)S(1)} %collective-permute-done.3.refs_4_), channel_id=1, source_target_pairs={{0,32},{16,240},{32,64},{48,16},{64,96},{80,48},{96,128},{112,80},... | collective-permute-start | bytes 1007624 | tf_op jit(solution)/shard_map/ppermute | solution.py:25
  17.9 15.9 %collective-permute-start.6 = (f32[24,3456]{1,0:T(8,128)S(1)}, f32[24,3456]{1,0:T(8,128)S(1)}, u32[]{:S(2)}, u32[]{:S(2)}) collective-permute-start(f32[24,3456]{1,0:T(8,128)S(1)} %get-tuple-element.66.refs_1_), channel_id=1, source_target_pairs={{0,224},{16,48},{32,0},{48,80},{64,32},{80,112},{96,64},{112,144},... | collective-permute-start | bytes 995336 | tf_op jit(solution)/shard_map/ppermute | solution.py:25
  24.8 10.8 %copy-start = (f32[1,1,120,3456]{3,2,1,0:T(8,128)S(1)}, f32[1,1,120,3456]{3,2,1,0:T(8,128)}, u32[]{:S(2)}) copy-start(f32[1,1,120,3456]{3,2,1,0:T(8,128)} %param.10) | copy-start | bytes 4976644
  24.8 10.8 %copy-start.1 = (f32[1,1,120,3456]{3,2,1,0:T(8,128)S(1)}, f32[1,1,120,3456]{3,2,1,0:T(8,128)}, u32[]{:S(2)}) copy-start(f32[1,1,120,3456]{3,2,1,0:T(8,128)} %param.11) | copy-start | bytes 4976644
  24.8 10.8 %copy-start.2 = (f32[1,1,2,120,256]{4,3,2,1,0:T(8,128)S(1)}, f32[1,1,2,120,256]{4,3,2,1,0:T(8,128)}, u32[]{:S(2)}) copy-start(f32[1,1,2,120,256]{4,3,2,1,0:T(8,128)} %refs_1_.9) | copy-start | bytes 737284
  24.8 9.0 %collective-permute-start.2 = (f32[16,3456]{1,0:T(8,128)S(1)}, f32[16,3456]{1,0:T(8,128)S(1)}, u32[]{:S(2)}, u32[]{:S(2)}) collective-permute-start(f32[16,3456]{1,0:T(8,128)S(1)} %get-tuple-element.61.refs_3_), channel_id=1, source_target_pairs={{0,16},{16,0},{32,48},{48,32},{64,80},{80,64},{96,112},{112,96},{1... | collective-permute-start | bytes 663560 | tf_op jit(solution)/shard_map/ppermute | solution.py:25
  27.7 3.4 %collective-permute-start.5 = (f32[48,256]{1,0:T(8,128)S(1)}, f32[48,256]{1,0:T(8,128)S(1)}, u32[]{:S(2)}, u32[]{:S(2)}) collective-permute-start(f32[48,256]{1,0:T(8,128)S(1)} %get-tuple-element.64), channel_id=1, source_target_pairs={{0,1},{1,0},{2,3},{3,2},{4,5},{5,4},{6,7},{7,6},{8,9},{9,8},{10,11... | collective-permute-start | bytes 147464 | tf_op jit(solution)/shard_map/ppermute | solution.py:25
  31.1 4.5 %collective-permute-start.16 = (f32[48,256]{1,0:T(8,128)S(1)}, f32[48,256]{1,0:T(8,128)S(1)}, u32[]{:S(2)}, u32[]{:S(2)}) collective-permute-start(f32[48,256]{1,0:T(8,128)S(1)} %add.22.refs_6_), channel_id=1, source_target_pairs={{0,2},{1,3},{2,0},{3,1},{4,6},{5,7},{6,4},{7,5},{8,10},{9,11},{10,... | collective-permute-start | bytes 147464 | tf_op jit(solution)/shard_map/ppermute | solution.py:25
  33.8 8.7 %collective-permute-start.7 = (f32[24,3456]{1,0:T(8,128)S(1)}, f32[24,3456]{1,0:T(8,128)S(1)}, u32[]{:S(2)}, u32[]{:S(2)}) collective-permute-start(f32[24,3456]{1,0:T(8,128)S(1)} %add.23), channel_id=1, source_target_pairs={{0,16},{16,0},{32,48},{48,32},{64,80},{80,64},{96,112},{112,96},{1... | collective-permute-start | bytes 995336 | tf_op jit(solution)/shard_map/ppermute | solution.py:25
  33.9 9.9 %collective-permute-start.9 = (f32[16,3456]{1,0:T(8,128)S(1)}, f32[16,3456]{1,0:T(8,128)S(1)}, u32[]{:S(2)}, u32[]{:S(2)}) collective-permute-start(f32[16,3456]{1,0:T(8,128)S(1)} %collective-permute-done.2.refs_4_), channel_id=1, source_target_pairs={{0,32},{16,240},{32,64},{48,16},{64,96},{80,48},{96,128},{112,80},... | collective-permute-start | bytes 663560 | tf_op jit(solution)/shard_map/ppermute | solution.py:25
  36.4 15.6 %collective-permute-start.18 = (f32[163,8,128]{2,1,0:T(8,128)S(1)}, f32[163,8,128]{2,1,0:T(8,128)S(1)}, u32[]{:S(2)}, u32[]{:S(2)}) collective-permute-start(f32[163,8,128]{2,1,0:T(8,128)S(1)} %get-tuple-element.80.refs_1_), channel_id=1, source_target_pairs={{0,12},{4,0},{8,4},{12,8},{1,13},{5,1},{9,5},{13,9},{2,14},{6,2},{... | collective-permute-start | bytes 2002952 | tf_op jit(solution)/shard_map/ppermute | solution.py:25
  39.0 15.4 %collective-permute-start.17 = (f32[163,8,128]{2,1,0:T(8,128)S(1)}, f32[163,8,128]{2,1,0:T(8,128)S(1)}, u32[]{:S(2)}, u32[]{:S(2)}) collective-permute-start(f32[163,8,128]{2,1,0:T(8,128)S(1)} %get-tuple-element.80.refs_1_), channel_id=1, source_target_pairs={{0,4},{4,8},{8,12},{12,0},{1,5},{5,9},{9,13},{13,1},{2,6},{6,10},{... | collective-permute-start | bytes 2002952 | tf_op jit(solution)/shard_map/ppermute | solution.py:25
  39.0 8.3 %collective-permute-start.11 = (f32[16,3456]{1,0:T(8,128)S(1)}, f32[16,3456]{1,0:T(8,128)S(1)}, u32[]{:S(2)}, u32[]{:S(2)}) collective-permute-start(f32[16,3456]{1,0:T(8,128)S(1)} %get-tuple-element.71.refs_1_), channel_id=1, source_target_pairs={{0,224},{16,48},{32,0},{48,80},{64,32},{80,112},{96,64},{112,144},... | collective-permute-start | bytes 663560 | tf_op jit(solution)/shard_map/ppermute | solution.py:25
  42.6 5.4 %collective-permute-start.8 = (f32[16,3456]{1,0:T(8,128)S(1)}, f32[16,3456]{1,0:T(8,128)S(1)}, u32[]{:S(2)}, u32[]{:S(2)}) collective-permute-start(f32[16,3456]{1,0:T(8,128)S(1)} %get-tuple-element.67.refs_3_), channel_id=1, source_target_pairs={{0,16},{16,0},{32,48},{48,32},{64,80},{80,64},{96,112},{112,96},{1... | collective-permute-start | bytes 663560 | tf_op jit(solution)/shard_map/ppermute | solution.py:25
  44.5 2.5 %collective-permute-start.10 = (f32[40,256]{1,0:T(8,128)S(1)}, f32[40,256]{1,0:T(8,128)S(1)}, u32[]{:S(2)}, u32[]{:S(2)}) collective-permute-start(f32[40,256]{1,0:T(8,128)S(1)} %get-tuple-element.69), channel_id=1, source_target_pairs={{0,1},{1,0},{2,3},{3,2},{4,5},{5,4},{6,7},{7,6},{8,9},{9,8},{10,11... | collective-permute-start | bytes 122888 | tf_op jit(solution)/shard_map/ppermute | solution.py:25
  47.0 4.4 %collective-permute-start.19 = (f32[40,256]{1,0:T(8,128)S(1)}, f32[40,256]{1,0:T(8,128)S(1)}, u32[]{:S(2)}, u32[]{:S(2)}) collective-permute-start(f32[40,256]{1,0:T(8,128)S(1)} %add.24.refs_6_), channel_id=1, source_target_pairs={{0,2},{1,3},{2,0},{3,1},{4,6},{5,7},{6,4},{7,5},{8,10},{9,11},{10,... | collective-permute-start | bytes 122888 | tf_op jit(solution)/shard_map/ppermute | solution.py:25
  48.0 7.9 %collective-permute-start.12 = (f32[16,3456]{1,0:T(8,128)S(1)}, f32[16,3456]{1,0:T(8,128)S(1)}, u32[]{:S(2)}, u32[]{:S(2)}) collective-permute-start(f32[16,3456]{1,0:T(8,128)S(1)} %add.25), channel_id=1, source_target_pairs={{0,16},{16,0},{32,48},{48,32},{64,80},{80,64},{96,112},{112,96},{1... | collective-permute-start | bytes 663560 | tf_op jit(solution)/shard_map/ppermute | solution.py:25
  49.6 6.3 %collective-permute-start.13 = (f32[16,3456]{1,0:T(8,128)S(1)}, f32[16,3456]{1,0:T(8,128)S(1)}, u32[]{:S(2)}, u32[]{:S(2)}) collective-permute-start(f32[16,3456]{1,0:T(8,128)S(1)} %collective-permute-done.8.refs_4_), channel_id=1, source_target_pairs={{0,32},{16,240},{32,64},{48,16},{64,96},{80,48},{96,128},{112,80},... | collective-permute-start | bytes 663560 | tf_op jit(solution)/shard_map/ppermute | solution.py:25
  54.4 11.8 %collective-permute-start.21 = (f32[40,3456]{1,0:T(8,128)S(1)}, f32[40,3456]{1,0:T(8,128)S(1)}, u32[]{:S(2)}, u32[]{:S(2)}) collective-permute-start(f32[40,3456]{1,0:T(8,128)S(1)} %get-tuple-element.85.refs_4_), channel_id=1, source_target_pairs={{0,12},{4,0},{8,4},{12,8},{1,13},{5,1},{9,5},{13,9},{2,14},{6,2},{... | collective-permute-start | bytes 1658888 | tf_op jit(solution)/shard_map/ppermute | solution.py:25
  54.6 12.0 %collective-permute-start.20 = (f32[40,3456]{1,0:T(8,128)S(1)}, f32[40,3456]{1,0:T(8,128)S(1)}, u32[]{:S(2)}, u32[]{:S(2)}) collective-permute-start(f32[40,3456]{1,0:T(8,128)S(1)} %get-tuple-element.85.refs_4_), channel_id=1, source_target_pairs={{0,4},{4,8},{8,12},{12,0},{1,5},{5,9},{9,13},{13,1},{2,6},{6,10},{... | collective-permute-start | bytes 1658888 | tf_op jit(solution)/shard_map/ppermute | solution.py:25
  56.6 4.7 %collective-permute-start.14 = (f32[32,256]{1,0:T(8,128)S(1)}, f32[32,256]{1,0:T(8,128)S(1)}, u32[]{:S(2)}, u32[]{:S(2)}) collective-permute-start(f32[32,256]{1,0:T(8,128)S(1)} %get-tuple-element.75), channel_id=1, source_target_pairs={{0,1},{1,0},{2,3},{3,2},{4,5},{5,4},{6,7},{7,6},{8,9},{9,8},{10,11... | collective-permute-start | bytes 98312 | tf_op jit(solution)/shard_map/ppermute | solution.py:25
  61.3 4.3 %collective-permute-start.15 = (f32[32,256]{1,0:T(8,128)S(1)}, f32[32,256]{1,0:T(8,128)S(1)}, u32[]{:S(2)}, u32[]{:S(2)}) collective-permute-start(f32[32,256]{1,0:T(8,128)S(1)} %add.26.refs_6_), channel_id=1, source_target_pairs={{0,2},{1,3},{2,0},{3,1},{4,6},{5,7},{6,4},{7,5},{8,10},{9,11},{10,... | collective-permute-start | bytes 98312 | tf_op jit(solution)/shard_map/ppermute | solution.py:25
  66.6 13.5 %collective-permute-start.25 = (f32[32,3456]{1,0:T(8,128)S(1)}, f32[32,3456]{1,0:T(8,128)S(1)}, u32[]{:S(2)}, u32[]{:S(2)}) collective-permute-start(f32[32,3456]{1,0:T(8,128)S(1)} %get-tuple-element.88.refs_1_), channel_id=1, source_target_pairs={{0,12},{4,0},{8,4},{12,8},{1,13},{5,1},{9,5},{13,9},{2,14},{6,2},{... | collective-permute-start | bytes 1327112 | tf_op jit(solution)/shard_map/ppermute | solution.py:25
  68.7 11.5 %collective-permute-start.24 = (f32[32,3456]{1,0:T(8,128)S(1)}, f32[32,3456]{1,0:T(8,128)S(1)}, u32[]{:S(2)}, u32[]{:S(2)}) collective-permute-start(f32[32,3456]{1,0:T(8,128)S(1)} %get-tuple-element.88.refs_1_), channel_id=1, source_target_pairs={{0,4},{4,8},{8,12},{12,0},{1,5},{5,9},{9,13},{13,1},{2,6},{6,10},{... | collective-permute-start | bytes 1327112 | tf_op jit(solution)/shard_map/ppermute | solution.py:25
  69.6 5.1 %collective-permute-start.22 = (f32[88,256]{1,0:T(8,128)S(1)}, f32[88,256]{1,0:T(8,128)S(1)}, u32[]{:S(2)}, u32[]{:S(2)}) collective-permute-start(f32[88,256]{1,0:T(8,128)S(1)} %get-tuple-element.86), channel_id=1, source_target_pairs={{0,1},{1,0},{2,3},{3,2},{4,5},{5,4},{6,7},{7,6},{8,9},{9,8},{10,11... | collective-permute-start | bytes 270344 | tf_op jit(solution)/shard_map/ppermute | solution.py:25
  74.7 5.4 %collective-permute-start.23 = (f32[88,256]{1,0:T(8,128)S(1)}, f32[88,256]{1,0:T(8,128)S(1)}, u32[]{:S(2)}, u32[]{:S(2)}) collective-permute-start(f32[88,256]{1,0:T(8,128)S(1)} %add.27.refs_8_), channel_id=1, source_target_pairs={{0,2},{1,3},{2,0},{3,1},{4,6},{5,7},{6,4},{7,5},{8,10},{9,11},{10,... | collective-permute-start | bytes 270344 | tf_op jit(solution)/shard_map/ppermute | solution.py:25
  80.9 8.7 %collective-permute-start.28 = (f32[32,256]{1,0:T(8,128)S(1)}, f32[32,256]{1,0:T(8,128)S(1)}, u32[]{:S(2)}, u32[]{:S(2)}) collective-permute-start(f32[32,256]{1,0:T(8,128)S(1)} %get-tuple-element.93.refs_6_), channel_id=1, source_target_pairs={{0,1},{1,0},{2,3},{3,2},{4,5},{5,4},{6,7},{7,6},{8,9},{9,8},{10,11... | collective-permute-start | bytes 98312 | tf_op jit(solution)/shard_map/ppermute | solution.py:25
  83.3 6.3 %collective-permute-start.27 = (f32[32,256]{1,0:T(8,128)S(1)}, f32[32,256]{1,0:T(8,128)S(1)}, u32[]{:S(2)}, u32[]{:S(2)}) collective-permute-start(f32[32,256]{1,0:T(8,128)S(1)} %get-tuple-element.93.refs_6_), channel_id=1, source_target_pairs={{0,2},{1,3},{2,0},{3,1},{4,6},{5,7},{6,4},{7,5},{8,10},{9,11},{10,... | collective-permute-start | bytes 98312 | tf_op jit(solution)/shard_map/ppermute | solution.py:25
  84.9 4.9 %collective-permute-start.26 = (f32[32,256]{1,0:T(8,128)S(1)}, f32[32,256]{1,0:T(8,128)S(1)}, u32[]{:S(2)}, u32[]{:S(2)}) collective-permute-start(f32[32,256]{1,0:T(8,128)S(1)} %get-tuple-element.93.refs_6_), channel_id=1, source_target_pairs={{0,3},{1,2},{2,1},{3,0},{4,7},{5,6},{6,5},{7,4},{8,11},{9,10},{10,... | collective-permute-start | bytes 98312 | tf_op jit(solution)/shard_map/ppermute | solution.py:25

commit v5 on v4

--- a/solution.py
+++ b/solution.py
@@ -320,9 +320,12 @@
     return (pred, *[send(pred, "ma", functools.partial(lambda turn, i: i ^ turn, turn)) for turn in (3, 2, 1)])
 
 
-def neighbours(block, axis):
-    count = lax.axis_size(axis)
-    return send(block, axis, lambda i: (i + 1) % count), send(block, axis, lambda i: (i - 1) % count)
+def upward(i):
+    return (i + 1) % lax.axis_size("ry")
+
+
+def downward(i):
+    return (i - 1) % lax.axis_size("ry")
 
 
 def local(numerator, weight, inputs, targets, first_moment, second_moment):
@@ -370,8 +373,9 @@
         values, first_mid, second_mid = update_middle(
             rows[g], (inputs, targets, total, row_sum, first, second, mine, other), g == 0
         )
-        ready = after(values, *results[-1][1:3]) if g > 0 else values
-        results.append((values, *neighbours(ready, "ry"), first_mid, second_mid))
+        came = [after(values, earlier_one) for earlier_one in results[-1][1:3]] if g > 0 else [values] * 2
+        sides = (send(block, "ry", turn) for block, turn in zip(came, (upward, downward)))
+        results.append((values, *sides, first_mid, second_mid))
 
     outs = ()
     for batch in BATCHES:

time: 92.1 us -> 92.1 us (level)
  transfers between devices with their start and end apart: 29 -> 29, of which waited for: 17 -> 16; matrix products, arithmetic and copies ran while one was open for 0% -> 0% of each run, Pallas kernels for 13% -> 13%
where the time goes in v5:
time: 92.1 us; the launch traced here: 91.9 us
  starting transfers between devices  48.3 us (52%)
  waiting for transfers between devices  25.8 us (28%)
  Pallas kernels  16.1 us (17%)
  between operations  1.61 us (2%)
    ppermute x29, starting transfers between devices, send(): lax.ppermute(block, axis, [(i, target(i)) for i in range(lax.axis_size(ax...  48.3 us
    ppermute x29, waiting for transfers between devices, send(): lax.ppermute(block, axis, [(i, target(i)) for i in range(lax.axis_size(ax...  25.8 us
    pallas_call x2, Pallas kernels, update_last(): pl.pallas_call(functools.partial(last_kernel, row, pieces, len(operands),...  5.01 us
    pallas_call x5, Pallas kernels, predict(): pl.pallas_call(functools.partial(predict_kernel, round_number, terms, n_r...  3.61 us
    pallas_call x3, Pallas kernels, cut(): pl.pallas_call(functools.partial(cut_kernel, row, counts, packed), in_spe...  3.36 us
    pallas_call x3, Pallas kernels, update_middle(): pl.pallas_call(functools.partial(middle_kernel, row, ((n_rows, 0, row),),...  2.11 us
    pallas_call x1, Pallas kernels, load(): pl.pallas_call(load_kernel, in_specs=[pl.BlockSpec(memory_space=pltpu.HBM...  2.01 us
  transfers between devices with their start and end apart: 29, of which 16 were waited for; matrix products, arithmetic and copies ran while one was open for 0% of the time, Pallas kernels for 13%

profile of v5, /device:TPU:1, one launch (start us, length us, event | category | flops | bytes accessed | tf_op | source)
XLA Modules:
  0.0 91.9 jit_solution(6129241021978540659)
XLA Ops:
  1.3 1.2 %cut.5 = (f32[82,8,128]{2,1,0:T(8,128)S(1)}, f32[24,3456]{1,0:T(8,128)S(1)}) custom-call(f32[1,1,120,3456]{3,2,1,0:T(8,128)} %numerator_ref.5, f32[1,1]{1,0:T(1,128)S(6)} %copy.16.weight_ref), custom_call_target="tpu_custom_call" | custom-call | bytes 1048576 | tf_op jit(solution)/shard_map/cut/pallas_call | solution.py:171
  2.5 6.5 %collective-permute-start = (f32[24,3456]{1,0:T(8,128)S(1)}, f32[24,3456]{1,0:T(8,128)S(1)}, u32[]{:S(2)}, u32[]{:S(2)}) collective-permute-start(f32[24,3456]{1,0:T(8,128)S(1)} %get-tuple-element.62.refs_1_), channel_id=1, source_target_pairs={{0,224},{16,48},{32,0},{48,80},{64,32},{80,112},{96,64},{112,144},... | collective-permute-start | bytes 995336 | tf_op jit(solution)/shard_map/ppermute | solution.py:25
  10.0 1.1 %cut.4 = (f32[16,3456]{1,0:T(8,128)S(1)}, f32[24,3456]{1,0:T(8,128)S(1)}) custom-call(f32[1,1,120,3456]{3,2,1,0:T(8,128)} %numerator_ref.5, f32[1,1]{1,0:T(1,128)S(6)} %copy.16.weight_ref), custom_call_target="tpu_custom_call" | custom-call | bytes 1048576 | tf_op jit(solution)/shard_map/cut/pallas_call | solution.py:171
  11.1 2.0 %load.1.refs_0_ = bf16[1,1,2,256,3456]{4,3,2,1,0:T(8,128)(2,1)S(1)} custom-call(bf16[1,1,2,256,3456]{4,3,2,1,0:T(8,128)(2,1)} %inputs_ref.1), custom_call_target="tpu_custom_call" | custom-call | bytes 4194304 | tf_op jit(solution)/shard_map/load/pallas_call | solution.py:190
  13.2 2.3 %collective-permute-done = f32[24,3456]{1,0:T(8,128)S(1)} collective-permute-done((f32[24,3456]{1,0:T(8,128)S(1)}, f32[24,3456]{1,0:T(8,128)S(1)}, u32[]{:S(2)}, u32[]{:S(2)}) %collective-permute-start) | collective-permute-done | bytes 331808 | tf_op jit(solution)/shard_map/ppermute | solution.py:25
  15.5 2.4 %collective-permute-start.1 = (f32[24,3456]{1,0:T(8,128)S(1)}, f32[24,3456]{1,0:T(8,128)S(1)}, u32[]{:S(2)}, u32[]{:S(2)}) collective-permute-start(f32[24,3456]{1,0:T(8,128)S(1)} %add.21), channel_id=1, source_target_pairs={{0,16},{16,0},{32,48},{48,32},{64,80},{80,64},{96,112},{112,96},{1... | collective-permute-start | bytes 995336 | tf_op jit(solution)/shard_map/ppermute | solution.py:25
  17.9 2.7 %collective-permute-start.6 = (f32[24,3456]{1,0:T(8,128)S(1)}, f32[24,3456]{1,0:T(8,128)S(1)}, u32[]{:S(2)}, u32[]{:S(2)}) collective-permute-start(f32[24,3456]{1,0:T(8,128)S(1)} %get-tuple-element.68.refs_1_), channel_id=1, source_target_pairs={{0,224},{16,48},{32,0},{48,80},{64,32},{80,112},{96,64},{112,144},... | collective-permute-start | bytes 995336 | tf_op jit(solution)/shard_map/ppermute | solution.py:25
  20.6 4.2 %collective-permute-done.1.refs_2_ = f32[24,3456]{1,0:T(8,128)S(1)} collective-permute-done((f32[24,3456]{1,0:T(8,128)S(1)}, f32[24,3456]{1,0:T(8,128)S(1)}, u32[]{:S(2)}, u32[]{:S(2)}) %collective-permute-start.1) | collective-permute-done | bytes 331808 | tf_op jit(solution)/shard_map/ppermute | solution.py:25
  24.8 1.2 %collective-permute-start.2 = (f32[16,3456]{1,0:T(8,128)S(1)}, f32[16,3456]{1,0:T(8,128)S(1)}, u32[]{:S(2)}, u32[]{:S(2)}) collective-permute-start(f32[16,3456]{1,0:T(8,128)S(1)} %get-tuple-element.63.refs_3_), channel_id=1, source_target_pairs={{0,16},{16,0},{32,48},{48,32},{64,80},{80,64},{96,112},{112,96},{1... | collective-permute-start | bytes 663560 | tf_op jit(solution)/shard_map/ppermute | solution.py:25
  27.7 2.5 %collective-permute-start.5 = (f32[48,256]{1,0:T(8,128)S(1)}, f32[48,256]{1,0:T(8,128)S(1)}, u32[]{:S(2)}, u32[]{:S(2)}) collective-permute-start(f32[48,256]{1,0:T(8,128)S(1)} %get-tuple-element.66), channel_id=1, source_target_pairs={{0,1},{1,0},{2,3},{3,2},{4,5},{5,4},{6,7},{7,6},{8,9},{9,8},{10,11... | collective-permute-start | bytes 147464 | tf_op jit(solution)/shard_map/ppermute | solution.py:25
  31.1 2.7 %collective-permute-start.16 = (f32[48,256]{1,0:T(8,128)S(1)}, f32[48,256]{1,0:T(8,128)S(1)}, u32[]{:S(2)}, u32[]{:S(2)}) collective-permute-start(f32[48,256]{1,0:T(8,128)S(1)} %add.22.refs_6_), channel_id=1, source_target_pairs={{0,2},{1,3},{2,0},{3,1},{4,6},{5,7},{6,4},{7,5},{8,10},{9,11},{10,... | collective-permute-start | bytes 147464 | tf_op jit(solution)/shard_map/ppermute | solution.py:25
  34.0 1.6 %collective-permute-done.16.refs_7_ = f32[48,256]{1,0:T(8,128)S(1)} collective-permute-done((f32[48,256]{1,0:T(8,128)S(1)}, f32[48,256]{1,0:T(8,128)S(1)}, u32[]{:S(2)}, u32[]{:S(2)}) %collective-permute-start.16) | collective-permute-done | bytes 49184 | tf_op jit(solution)/shard_map/ppermute | solution.py:25
  36.4 2.6 %collective-permute-start.18 = (f32[163,8,128]{2,1,0:T(8,128)S(1)}, f32[163,8,128]{2,1,0:T(8,128)S(1)}, u32[]{:S(2)}, u32[]{:S(2)}) collective-permute-start(f32[163,8,128]{2,1,0:T(8,128)S(1)} %get-tuple-element.82.refs_1_), channel_id=1, source_target_pairs={{0,12},{4,0},{8,4},{12,8},{1,13},{5,1},{9,5},{13,9},{2,14},{6,2},{... | collective-permute-start | bytes 2002952 | tf_op jit(solution)/shard_map/ppermute | solution.py:25
  39.0 1.1 %collective-permute-start.11 = (f32[16,3456]{1,0:T(8,128)S(1)}, f32[16,3456]{1,0:T(8,128)S(1)}, u32[]{:S(2)}, u32[]{:S(2)}) collective-permute-start(f32[16,3456]{1,0:T(8,128)S(1)} %get-tuple-element.73.refs_1_), channel_id=1, source_target_pairs={{0,224},{16,48},{32,0},{48,80},{64,32},{80,112},{96,64},{112,144},... | collective-permute-start | bytes 663560 | tf_op jit(solution)/shard_map/ppermute | solution.py:25
  40.1 2.5 %collective-permute-done.7.refs_2_ = f32[24,3456]{1,0:T(8,128)S(1)} collective-permute-done((f32[24,3456]{1,0:T(8,128)S(1)}, f32[24,3456]{1,0:T(8,128)S(1)}, u32[]{:S(2)}, u32[]{:S(2)}) %collective-permute-start.7) | collective-permute-done | bytes 331808 | tf_op jit(solution)/shard_map/ppermute | solution.py:25
  42.6 1.2 %collective-permute-start.8 = (f32[16,3456]{1,0:T(8,128)S(1)}, f32[16,3456]{1,0:T(8,128)S(1)}, u32[]{:S(2)}, u32[]{:S(2)}) collective-permute-start(f32[16,3456]{1,0:T(8,128)S(1)} %get-tuple-element.69.refs_3_), channel_id=1, source_target_pairs={{0,16},{16,0},{32,48},{48,32},{64,80},{80,64},{96,112},{112,96},{1... | collective-permute-start | bytes 663560 | tf_op jit(solution)/shard_map/ppermute | solution.py:25
  44.5 1.6 %collective-permute-start.10 = (f32[40,256]{1,0:T(8,128)S(1)}, f32[40,256]{1,0:T(8,128)S(1)}, u32[]{:S(2)}, u32[]{:S(2)}) collective-permute-start(f32[40,256]{1,0:T(8,128)S(1)} %get-tuple-element.71), channel_id=1, source_target_pairs={{0,1},{1,0},{2,3},{3,2},{4,5},{5,4},{6,7},{7,6},{8,9},{9,8},{10,11... | collective-permute-start | bytes 122888 | tf_op jit(solution)/shard_map/ppermute | solution.py:25
  48.0 1.6 %collective-permute-start.12 = (f32[16,3456]{1,0:T(8,128)S(1)}, f32[16,3456]{1,0:T(8,128)S(1)}, u32[]{:S(2)}, u32[]{:S(2)}) collective-permute-start(f32[16,3456]{1,0:T(8,128)S(1)} %add.25), channel_id=1, source_target_pairs={{0,16},{16,0},{32,48},{48,32},{64,80},{80,64},{96,112},{112,96},{1... | collective-permute-start | bytes 663560 | tf_op jit(solution)/shard_map/ppermute | solution.py:25
  49.6 1.7 %collective-permute-done.19.refs_7_ = f32[40,256]{1,0:T(8,128)S(1)} collective-permute-done((f32[40,256]{1,0:T(8,128)S(1)}, f32[40,256]{1,0:T(8,128)S(1)}, u32[]{:S(2)}, u32[]{:S(2)}) %collective-permute-start.19) | collective-permute-done | bytes 40992 | tf_op jit(solution)/shard_map/ppermute | solution.py:25
  52.1 2.6 %collective-permute-start.21 = (f32[40,3456]{1,0:T(8,128)S(1)}, f32[40,3456]{1,0:T(8,128)S(1)}, u32[]{:S(2)}, u32[]{:S(2)}) collective-permute-start(f32[40,3456]{1,0:T(8,128)S(1)} %get-tuple-element.88.refs_4_), channel_id=1, source_target_pairs={{0,12},{4,0},{8,4},{12,8},{1,13},{5,1},{9,5},{13,9},{2,14},{6,2},{... | collective-permute-start | bytes 1658888 | tf_op jit(solution)/shard_map/ppermute | solution.py:25
  54.6 1.3 %collective-permute-done.13.refs_5_ = f32[16,3456]{1,0:T(8,128)S(1)} collective-permute-done((f32[16,3456]{1,0:T(8,128)S(1)}, f32[16,3456]{1,0:T(8,128)S(1)}, u32[]{:S(2)}, u32[]{:S(2)}) %collective-permute-start.13) | collective-permute-done | bytes 221216 | tf_op jit(solution)/shard_map/ppermute | solution.py:25
  56.6 3.8 %collective-permute-start.14 = (f32[32,256]{1,0:T(8,128)S(1)}, f32[32,256]{1,0:T(8,128)S(1)}, u32[]{:S(2)}, u32[]{:S(2)}) collective-permute-start(f32[32,256]{1,0:T(8,128)S(1)} %get-tuple-element.77), channel_id=1, source_target_pairs={{0,1},{1,0},{2,3},{3,2},{4,5},{5,4},{6,7},{7,6},{8,9},{9,8},{10,11... | collective-permute-start | bytes 98312 | tf_op jit(solution)/shard_map/ppermute | solution.py:25
  62.2 3.4 %collective-permute-done.15.refs_7_ = f32[32,256]{1,0:T(8,128)S(1)} collective-permute-done((f32[32,256]{1,0:T(8,128)S(1)}, f32[32,256]{1,0:T(8,128)S(1)}, u32[]{:S(2)}, u32[]{:S(2)}) %collective-permute-start.15) | collective-permute-done | bytes 32800 | tf_op jit(solution)/shard_map/ppermute | solution.py:25
  66.1 2.6 %collective-permute-start.25 = (f32[32,3456]{1,0:T(8,128)S(1)}, f32[32,3456]{1,0:T(8,128)S(1)}, u32[]{:S(2)}, u32[]{:S(2)}) collective-permute-start(f32[32,3456]{1,0:T(8,128)S(1)} %get-tuple-element.92.refs_1_), channel_id=1, source_target_pairs={{0,12},{4,0},{8,4},{12,8},{1,13},{5,1},{9,5},{13,9},{2,14},{6,2},{... | collective-permute-start | bytes 1327112 | tf_op jit(solution)/shard_map/ppermute | solution.py:25
  69.6 2.5 %collective-permute-start.22 = (f32[88,256]{1,0:T(8,128)S(1)}, f32[88,256]{1,0:T(8,128)S(1)}, u32[]{:S(2)}, u32[]{:S(2)}) collective-permute-start(f32[88,256]{1,0:T(8,128)S(1)} %get-tuple-element.89), channel_id=1, source_target_pairs={{0,1},{1,0},{2,3},{3,2},{4,5},{5,4},{6,7},{7,6},{8,9},{9,8},{10,11... | collective-permute-start | bytes 270344 | tf_op jit(solution)/shard_map/ppermute | solution.py:25
  73.0 2.7 %collective-permute-start.23 = (f32[88,256]{1,0:T(8,128)S(1)}, f32[88,256]{1,0:T(8,128)S(1)}, u32[]{:S(2)}, u32[]{:S(2)}) collective-permute-start(f32[88,256]{1,0:T(8,128)S(1)} %add.27.refs_8_), channel_id=1, source_target_pairs={{0,2},{1,3},{2,0},{3,1},{4,6},{5,7},{6,4},{7,5},{8,10},{9,11},{10,... | collective-permute-start | bytes 270344 | tf_op jit(solution)/shard_map/ppermute | solution.py:25
  75.7 2.7 %collective-permute-done.23.refs_9_ = f32[88,256]{1,0:T(8,128)S(1)} collective-permute-done((f32[88,256]{1,0:T(8,128)S(1)}, f32[88,256]{1,0:T(8,128)S(1)}, u32[]{:S(2)}, u32[]{:S(2)}) %collective-permute-start.23) | collective-permute-done | bytes 90144 | tf_op jit(solution)/shard_map/ppermute | solution.py:25
  79.9 3.4 %collective-permute-start.28 = (f32[32,256]{1,0:T(8,128)S(1)}, f32[32,256]{1,0:T(8,128)S(1)}, u32[]{:S(2)}, u32[]{:S(2)}) collective-permute-start(f32[32,256]{1,0:T(8,128)S(1)} %get-tuple-element.97.refs_6_), channel_id=1, source_target_pairs={{0,1},{1,0},{2,3},{3,2},{4,5},{5,4},{6,7},{7,6},{8,9},{9,8},{10,11... | collective-permute-start | bytes 98312 | tf_op jit(solution)/shard_map/ppermute | solution.py:25
  83.3 1.7 %collective-permute-start.27 = (f32[32,256]{1,0:T(8,128)S(1)}, f32[32,256]{1,0:T(8,128)S(1)}, u32[]{:S(2)}, u32[]{:S(2)}) collective-permute-start(f32[32,256]{1,0:T(8,128)S(1)} %get-tuple-element.97.refs_6_), channel_id=1, source_target_pairs={{0,2},{1,3},{2,0},{3,1},{4,6},{5,7},{6,4},{7,5},{8,10},{9,11},{10,... | collective-permute-start | bytes 98312 | tf_op jit(solution)/shard_map/ppermute | solution.py:25
  84.9 1.6 %collective-permute-start.26 = (f32[32,256]{1,0:T(8,128)S(1)}, f32[32,256]{1,0:T(8,128)S(1)}, u32[]{:S(2)}, u32[]{:S(2)}) collective-permute-start(f32[32,256]{1,0:T(8,128)S(1)} %get-tuple-element.97.refs_6_), channel_id=1, source_target_pairs={{0,3},{1,2},{2,1},{3,0},{4,7},{5,6},{6,5},{7,4},{8,11},{9,10},{10,... | collective-permute-start | bytes 98312 | tf_op jit(solution)/shard_map/ppermute | solution.py:25
  86.5 3.0 %update1.2 = (f32[1,1,120,3456]{3,2,1,0:T(8,128)}, f32[1,1,120,3456]{3,2,1,0:T(8,128)}, f32[1,1,120,3456]{3,2,1,0:T(8,128)}, f32[1,1]{1,0:T(1,128)}) custom-call(bf16[1,1,2,256,3456]{4,3,2,1,0:T(8,128)(2,1)S(1)} %load.1.refs_0_, f32[1,1,2,120,256]{4,3,2,1,0:T(8,128)S(1)} %copy-done.2, f32[88,3456]{1,0:T(8,128)S(1)} %get-tuple-element.98.refs_2_, ...), custom_call_target="tpu_custom_call" | custom-call | flops 9342812160 | bytes 1048576 | tf_op jit(solution)/shard_map/update1/pallas_call | solution.py:298
  89.8 2.0 %update1.3 = (f32[1,1,120,3456]{3,2,1,0:T(8,128)}, f32[1,1,120,3456]{3,2,1,0:T(8,128)}, f32[1,1,120,3456]{3,2,1,0:T(8,128)}, f32[1,1]{1,0:T(1,128)}) custom-call(bf16[1,1,2,256,3456]{4,3,2,1,0:T(8,128)(2,1)S(1)} %load.1.refs_0_, f32[1,1,2,120,256]{4,3,2,1,0:T(8,128)S(1)} %copy-done.2, ...), custom_call_target="tpu_custom_call", output_to_operand_aliasing={{0}: (10, {}), {1}: (11, {}), {2}: (12, {})} | custom-call | flops 3397386240 | bytes 1048576 | tf_op jit(solution)/shard_map/update1/pallas_call | solution.py:298
  (53 shorter events, 14.6 us)
Async XLA Ops:
  2.5 12.9 %collective-permute-start = (f32[24,3456]{1,0:T(8,128)S(1)}, f32[24,3456]{1,0:T(8,128)S(1)}, u32[]{:S(2)}, u32[]{:S(2)}) collective-permute-start(f32[24,3456]{1,0:T(8,128)S(1)} %get-tuple-element.62.refs_1_), channel_id=1, source_target_pairs={{0,224},{16,48},{32,0},{48,80},{64,32},{80,112},{96,64},{112,144},... | collective-permute-start | bytes 995336 | tf_op jit(solution)/shard_map/ppermute | solution.py:25
  9.0 8.9 %collective-permute-start.3 = (f32[82,8,128]{2,1,0:T(8,128)S(1)}, f32[82,8,128]{2,1,0:T(8,128)S(1)}, u32[]{:S(2)}, u32[]{:S(2)}) collective-permute-start(f32[82,8,128]{2,1,0:T(8,128)S(1)} %get-tuple-element.64.refs_3_), channel_id=1, source_target_pairs={{0,16},{16,0},{32,48},{48,32},{64,80},{80,64},{96,112},{112,96},{1... | collective-permute-start | bytes 1007624 | tf_op jit(solution)/shard_map/ppermute | solution.py:25
  15.5 9.3 %collective-permute-start.1 = (f32[24,3456]{1,0:T(8,128)S(1)}, f32[24,3456]{1,0:T(8,128)S(1)}, u32[]{:S(2)}, u32[]{:S(2)}) collective-permute-start(f32[24,3456]{1,0:T(8,128)S(1)} %add.21), channel_id=1, source_target_pairs={{0,16},{16,0},{32,48},{48,32},{64,80},{80,64},{96,112},{112,96},{1... | collective-permute-start | bytes 995336 | tf_op jit(solution)/shard_map/ppermute | solution.py:25
  17.9 9.1 %collective-permute-start.4 = (f32[82,8,128]{2,1,0:T(8,128)S(1)}, f32[82,8,128]{2,1,0:T(8,128)S(1)}, u32[]{:S(2)}, u32[]{:S(2)}) collective-permute-start(f32[82,8,128]{2,1,0:T(8,128)S(1)} %collective-permute-done.3.refs_4_), channel_id=1, source_target_pairs={{0,32},{16,240},{32,64},{48,16},{64,96},{80,48},{96,128},{112,80},... | collective-permute-start | bytes 1007624 | tf_op jit(solution)/shard_map/ppermute | solution.py:25
  17.9 15.9 %collective-permute-start.6 = (f32[24,3456]{1,0:T(8,128)S(1)}, f32[24,3456]{1,0:T(8,128)S(1)}, u32[]{:S(2)}, u32[]{:S(2)}) collective-permute-start(f32[24,3456]{1,0:T(8,128)S(1)} %get-tuple-element.68.refs_1_), channel_id=1, source_target_pairs={{0,224},{16,48},{32,0},{48,80},{64,32},{80,112},{96,64},{112,144},... | collective-permute-start | bytes 995336 | tf_op jit(solution)/shard_map/ppermute | solution.py:25
  24.8 10.8 %copy-start = (f32[1,1,120,3456]{3,2,1,0:T(8,128)S(1)}, f32[1,1,120,3456]{3,2,1,0:T(8,128)}, u32[]{:S(2)}) copy-start(f32[1,1,120,3456]{3,2,1,0:T(8,128)} %param.10) | copy-start | bytes 4976644
  24.8 10.8 %copy-start.1 = (f32[1,1,120,3456]{3,2,1,0:T(8,128)S(1)}, f32[1,1,120,3456]{3,2,1,0:T(8,128)}, u32[]{:S(2)}) copy-start(f32[1,1,120,3456]{3,2,1,0:T(8,128)} %param.11) | copy-start | bytes 4976644
  24.8 10.8 %copy-start.2 = (f32[1,1,2,120,256]{4,3,2,1,0:T(8,128)S(1)}, f32[1,1,2,120,256]{4,3,2,1,0:T(8,128)}, u32[]{:S(2)}) copy-start(f32[1,1,2,120,256]{4,3,2,1,0:T(8,128)} %refs_1_.9) | copy-start | bytes 737284
  24.8 9.0 %collective-permute-start.2 = (f32[16,3456]{1,0:T(8,128)S(1)}, f32[16,3456]{1,0:T(8,128)S(1)}, u32[]{:S(2)}, u32[]{:S(2)}) collective-permute-start(f32[16,3456]{1,0:T(8,128)S(1)} %get-tuple-element.63.refs_3_), channel_id=1, source_target_pairs={{0,16},{16,0},{32,48},{48,32},{64,80},{80,64},{96,112},{112,96},{1... | collective-permute-start | bytes 663560 | tf_op jit(solution)/shard_map/ppermute | solution.py:25
  27.7 3.4 %collective-permute-start.5 = (f32[48,256]{1,0:T(8,128)S(1)}, f32[48,256]{1,0:T(8,128)S(1)}, u32[]{:S(2)}, u32[]{:S(2)}) collective-permute-start(f32[48,256]{1,0:T(8,128)S(1)} %get-tuple-element.66), channel_id=1, source_target_pairs={{0,1},{1,0},{2,3},{3,2},{4,5},{5,4},{6,7},{7,6},{8,9},{9,8},{10,11... | collective-permute-start | bytes 147464 | tf_op jit(solution)/shard_map/ppermute | solution.py:25
  31.1 4.5 %collective-permute-start.16 = (f32[48,256]{1,0:T(8,128)S(1)}, f32[48,256]{1,0:T(8,128)S(1)}, u32[]{:S(2)}, u32[]{:S(2)}) collective-permute-start(f32[48,256]{1,0:T(8,128)S(1)} %add.22.refs_6_), channel_id=1, source_target_pairs={{0,2},{1,3},{2,0},{3,1},{4,6},{5,7},{6,4},{7,5},{8,10},{9,11},{10,... | collective-permute-start | bytes 147464 | tf_op jit(solution)/shard_map/ppermute | solution.py:25
  33.8 8.7 %collective-permute-start.7 = (f32[24,3456]{1,0:T(8,128)S(1)}, f32[24,3456]{1,0:T(8,128)S(1)}, u32[]{:S(2)}, u32[]{:S(2)}) collective-permute-start(f32[24,3456]{1,0:T(8,128)S(1)} %add.23), channel_id=1, source_target_pairs={{0,16},{16,0},{32,48},{48,32},{64,80},{80,64},{96,112},{112,96},{1... | collective-permute-start | bytes 995336 | tf_op jit(solution)/shard_map/ppermute | solution.py:25
  33.9 9.9 %collective-permute-start.9 = (f32[16,3456]{1,0:T(8,128)S(1)}, f32[16,3456]{1,0:T(8,128)S(1)}, u32[]{:S(2)}, u32[]{:S(2)}) collective-permute-start(f32[16,3456]{1,0:T(8,128)S(1)} %collective-permute-done.2.refs_4_), channel_id=1, source_target_pairs={{0,32},{16,240},{32,64},{48,16},{64,96},{80,48},{96,128},{112,80},... | collective-permute-start | bytes 663560 | tf_op jit(solution)/shard_map/ppermute | solution.py:25
  36.4 15.6 %collective-permute-start.18 = (f32[163,8,128]{2,1,0:T(8,128)S(1)}, f32[163,8,128]{2,1,0:T(8,128)S(1)}, u32[]{:S(2)}, u32[]{:S(2)}) collective-permute-start(f32[163,8,128]{2,1,0:T(8,128)S(1)} %get-tuple-element.82.refs_1_), channel_id=1, source_target_pairs={{0,12},{4,0},{8,4},{12,8},{1,13},{5,1},{9,5},{13,9},{2,14},{6,2},{... | collective-permute-start | bytes 2002952 | tf_op jit(solution)/shard_map/ppermute | solution.py:25
  39.0 15.7 %collective-permute-start.17 = (f32[163,8,128]{2,1,0:T(8,128)S(1)}, f32[163,8,128]{2,1,0:T(8,128)S(1)}, u32[]{:S(2)}, u32[]{:S(2)}) collective-permute-start(f32[163,8,128]{2,1,0:T(8,128)S(1)} %get-tuple-element.82.refs_1_), channel_id=1, source_target_pairs={{0,4},{4,8},{8,12},{12,0},{1,5},{5,9},{9,13},{13,1},{2,6},{6,10},{... | collective-permute-start | bytes 2002952 | tf_op jit(solution)/shard_map/ppermute | solution.py:25
  39.0 8.3 %collective-permute-start.11 = (f32[16,3456]{1,0:T(8,128)S(1)}, f32[16,3456]{1,0:T(8,128)S(1)}, u32[]{:S(2)}, u32[]{:S(2)}) collective-permute-start(f32[16,3456]{1,0:T(8,128)S(1)} %get-tuple-element.73.refs_1_), channel_id=1, source_target_pairs={{0,224},{16,48},{32,0},{48,80},{64,32},{80,112},{96,64},{112,144},... | collective-permute-start | bytes 663560 | tf_op jit(solution)/shard_map/ppermute | solution.py:25
  42.6 5.4 %collective-permute-start.8 = (f32[16,3456]{1,0:T(8,128)S(1)}, f32[16,3456]{1,0:T(8,128)S(1)}, u32[]{:S(2)}, u32[]{:S(2)}) collective-permute-start(f32[16,3456]{1,0:T(8,128)S(1)} %get-tuple-element.69.refs_3_), channel_id=1, source_target_pairs={{0,16},{16,0},{32,48},{48,32},{64,80},{80,64},{96,112},{112,96},{1... | collective-permute-start | bytes 663560 | tf_op jit(solution)/shard_map/ppermute | solution.py:25
  44.5 2.5 %collective-permute-start.10 = (f32[40,256]{1,0:T(8,128)S(1)}, f32[40,256]{1,0:T(8,128)S(1)}, u32[]{:S(2)}, u32[]{:S(2)}) collective-permute-start(f32[40,256]{1,0:T(8,128)S(1)} %get-tuple-element.71), channel_id=1, source_target_pairs={{0,1},{1,0},{2,3},{3,2},{4,5},{5,4},{6,7},{7,6},{8,9},{9,8},{10,11... | collective-permute-start | bytes 122888 | tf_op jit(solution)/shard_map/ppermute | solution.py:25
  47.0 4.4 %collective-permute-start.19 = (f32[40,256]{1,0:T(8,128)S(1)}, f32[40,256]{1,0:T(8,128)S(1)}, u32[]{:S(2)}, u32[]{:S(2)}) collective-permute-start(f32[40,256]{1,0:T(8,128)S(1)} %add.24.refs_6_), channel_id=1, source_target_pairs={{0,2},{1,3},{2,0},{3,1},{4,6},{5,7},{6,4},{7,5},{8,10},{9,11},{10,... | collective-permute-start | bytes 122888 | tf_op jit(solution)/shard_map/ppermute | solution.py:25
  48.0 7.9 %collective-permute-start.12 = (f32[16,3456]{1,0:T(8,128)S(1)}, f32[16,3456]{1,0:T(8,128)S(1)}, u32[]{:S(2)}, u32[]{:S(2)}) collective-permute-start(f32[16,3456]{1,0:T(8,128)S(1)} %add.25), channel_id=1, source_target_pairs={{0,16},{16,0},{32,48},{48,32},{64,80},{80,64},{96,112},{112,96},{1... | collective-permute-start | bytes 663560 | tf_op jit(solution)/shard_map/ppermute | solution.py:25
  49.6 6.3 %collective-permute-start.13 = (f32[16,3456]{1,0:T(8,128)S(1)}, f32[16,3456]{1,0:T(8,128)S(1)}, u32[]{:S(2)}, u32[]{:S(2)}) collective-permute-start(f32[16,3456]{1,0:T(8,128)S(1)} %collective-permute-done.8.refs_4_), channel_id=1, source_target_pairs={{0,32},{16,240},{32,64},{48,16},{64,96},{80,48},{96,128},{112,80},... | collective-permute-start | bytes 663560 | tf_op jit(solution)/shard_map/ppermute | solution.py:25
  52.1 14.1 %collective-permute-start.21 = (f32[40,3456]{1,0:T(8,128)S(1)}, f32[40,3456]{1,0:T(8,128)S(1)}, u32[]{:S(2)}, u32[]{:S(2)}) collective-permute-start(f32[40,3456]{1,0:T(8,128)S(1)} %get-tuple-element.88.refs_4_), channel_id=1, source_target_pairs={{0,12},{4,0},{8,4},{12,8},{1,13},{5,1},{9,5},{13,9},{2,14},{6,2},{... | collective-permute-start | bytes 1658888 | tf_op jit(solution)/shard_map/ppermute | solution.py:25
  54.6 14.1 %collective-permute-start.20 = (f32[40,3456]{1,0:T(8,128)S(1)}, f32[40,3456]{1,0:T(8,128)S(1)}, u32[]{:S(2)}, u32[]{:S(2)}) collective-permute-start(f32[40,3456]{1,0:T(8,128)S(1)} %get-tuple-element.88.refs_4_), channel_id=1, source_target_pairs={{0,4},{4,8},{8,12},{12,0},{1,5},{5,9},{9,13},{13,1},{2,6},{6,10},{... | collective-permute-start | bytes 1658888 | tf_op jit(solution)/shard_map/ppermute | solution.py:25
  56.6 4.7 %collective-permute-start.14 = (f32[32,256]{1,0:T(8,128)S(1)}, f32[32,256]{1,0:T(8,128)S(1)}, u32[]{:S(2)}, u32[]{:S(2)}) collective-permute-start(f32[32,256]{1,0:T(8,128)S(1)} %get-tuple-element.77), channel_id=1, source_target_pairs={{0,1},{1,0},{2,3},{3,2},{4,5},{5,4},{6,7},{7,6},{8,9},{9,8},{10,11... | collective-permute-start | bytes 98312 | tf_op jit(solution)/shard_map/ppermute | solution.py:25
  61.3 4.3 %collective-permute-start.15 = (f32[32,256]{1,0:T(8,128)S(1)}, f32[32,256]{1,0:T(8,128)S(1)}, u32[]{:S(2)}, u32[]{:S(2)}) collective-permute-start(f32[32,256]{1,0:T(8,128)S(1)} %add.26.refs_6_), channel_id=1, source_target_pairs={{0,2},{1,3},{2,0},{3,1},{4,6},{5,7},{6,4},{7,5},{8,10},{9,11},{10,... | collective-permute-start | bytes 98312 | tf_op jit(solution)/shard_map/ppermute | solution.py:25
  66.1 12.3 %collective-permute-start.25 = (f32[32,3456]{1,0:T(8,128)S(1)}, f32[32,3456]{1,0:T(8,128)S(1)}, u32[]{:S(2)}, u32[]{:S(2)}) collective-permute-start(f32[32,3456]{1,0:T(8,128)S(1)} %get-tuple-element.92.refs_1_), channel_id=1, source_target_pairs={{0,12},{4,0},{8,4},{12,8},{1,13},{5,1},{9,5},{13,9},{2,14},{6,2},{... | collective-permute-start | bytes 1327112 | tf_op jit(solution)/shard_map/ppermute | solution.py:25
  68.7 10.5 %collective-permute-start.24 = (f32[32,3456]{1,0:T(8,128)S(1)}, f32[32,3456]{1,0:T(8,128)S(1)}, u32[]{:S(2)}, u32[]{:S(2)}) collective-permute-start(f32[32,3456]{1,0:T(8,128)S(1)} %get-tuple-element.92.refs_1_), channel_id=1, source_target_pairs={{0,4},{4,8},{8,12},{12,0},{1,5},{5,9},{9,13},{13,1},{2,6},{6,10},{... | collective-permute-start | bytes 1327112 | tf_op jit(solution)/shard_map/ppermute | solution.py:25
  69.6 3.4 %collective-permute-start.22 = (f32[88,256]{1,0:T(8,128)S(1)}, f32[88,256]{1,0:T(8,128)S(1)}, u32[]{:S(2)}, u32[]{:S(2)}) collective-permute-start(f32[88,256]{1,0:T(8,128)S(1)} %get-tuple-element.89), channel_id=1, source_target_pairs={{0,1},{1,0},{2,3},{3,2},{4,5},{5,4},{6,7},{7,6},{8,9},{9,8},{10,11... | collective-permute-start | bytes 270344 | tf_op jit(solution)/shard_map/ppermute | solution.py:25
  73.0 5.4 %collective-permute-start.23 = (f32[88,256]{1,0:T(8,128)S(1)}, f32[88,256]{1,0:T(8,128)S(1)}, u32[]{:S(2)}, u32[]{:S(2)}) collective-permute-start(f32[88,256]{1,0:T(8,128)S(1)} %add.27.refs_8_), channel_id=1, source_target_pairs={{0,2},{1,3},{2,0},{3,1},{4,6},{5,7},{6,4},{7,5},{8,10},{9,11},{10,... | collective-permute-start | bytes 270344 | tf_op jit(solution)/shard_map/ppermute | solution.py:25
  79.9 9.7 %collective-permute-start.28 = (f32[32,256]{1,0:T(8,128)S(1)}, f32[32,256]{1,0:T(8,128)S(1)}, u32[]{:S(2)}, u32[]{:S(2)}) collective-permute-start(f32[32,256]{1,0:T(8,128)S(1)} %get-tuple-element.97.refs_6_), channel_id=1, source_target_pairs={{0,1},{1,0},{2,3},{3,2},{4,5},{5,4},{6,7},{7,6},{8,9},{9,8},{10,11... | collective-permute-start | bytes 98312 | tf_op jit(solution)/shard_map/ppermute | solution.py:25
  83.3 6.3 %collective-permute-start.27 = (f32[32,256]{1,0:T(8,128)S(1)}, f32[32,256]{1,0:T(8,128)S(1)}, u32[]{:S(2)}, u32[]{:S(2)}) collective-permute-start(f32[32,256]{1,0:T(8,128)S(1)} %get-tuple-element.97.refs_6_), channel_id=1, source_target_pairs={{0,2},{1,3},{2,0},{3,1},{4,6},{5,7},{6,4},{7,5},{8,10},{9,11},{10,... | collective-permute-start | bytes 98312 | tf_op jit(solution)/shard_map/ppermute | solution.py:25
  84.9 4.9 %collective-permute-start.26 = (f32[32,256]{1,0:T(8,128)S(1)}, f32[32,256]{1,0:T(8,128)S(1)}, u32[]{:S(2)}, u32[]{:S(2)}) collective-permute-start(f32[32,256]{1,0:T(8,128)S(1)} %get-tuple-element.97.refs_6_), channel_id=1, source_target_pairs={{0,3},{1,2},{2,1},{3,0},{4,7},{5,6},{6,5},{7,4},{8,11},{9,10},{10,... | collective-permute-start | bytes 98312 | tf_op jit(solution)/shard_map/ppermute | solution.py:25

commit v6 on v3

--- a/solution.py
+++ b/solution.py
@@ -14,7 +14,7 @@
 EPSILON = 1e-08
 
 GROUPS = ((24, 24), (16, 24), (16, 16))
-BATCHES = ((0, 1), (2,))
+BATCHES = ((0,), (1, 2))
 TILE = 384
 COST = 120
 RUN = 1152

time: 91.2 us -> 93.2 us (1.022)
  waiting for transfers between devices: 25.5 us -> 30 us
  starting transfers between devices: 47.6 us -> 45.2 us
    ppermute x28, waiting for transfers between devices: 25.5 us -> 30 us  [send(): lax.ppermute(block, axis, [(i, target(i)) for i in range(lax.axis_size(ax...]
    ppermute x28, starting transfers between devices: 47.6 us -> 45.2 us  [send(): lax.ppermute(block, axis, [(i, target(i)) for i in range(lax.axis_size(ax...]
  transfers between devices with their start and end apart: 28 -> 28, of which waited for: 17 -> 17; matrix products, arithmetic and copies ran while one was open for 0% -> 0% of each run, Pallas kernels for 13% -> 12%
where the time goes in v6:
time: 93.2 us; the launch traced here: 93 us
  starting transfers between devices  45.2 us (48%)
  waiting for transfers between devices  30 us (32%)
  Pallas kernels  16 us (17%)
  between operations  1.61 us (2%)
    ppermute x28, starting transfers between devices, send(): lax.ppermute(block, axis, [(i, target(i)) for i in range(lax.axis_size(ax...  45.2 us
    ppermute x28, waiting for transfers between devices, send(): lax.ppermute(block, axis, [(i, target(i)) for i in range(lax.axis_size(ax...  30 us
    pallas_call x2, Pallas kernels, update_last(): pl.pallas_call(functools.partial(last_kernel, row, pieces, len(operands),...  5.06 us
    pallas_call x5, Pallas kernels, predict(): pl.pallas_call(functools.partial(predict_kernel, round_number, terms, n_r...  3.5 us
    pallas_call x3, Pallas kernels, cut(): pl.pallas_call(functools.partial(cut_kernel, row, counts, packed), in_spe...  3.36 us
    pallas_call x3, Pallas kernels, update_middle(): pl.pallas_call(functools.partial(middle_kernel, row, ((n_rows, 0, row),),...  2.11 us
    pallas_call x1, Pallas kernels, load(): pl.pallas_call(load_kernel, in_specs=[pl.BlockSpec(memory_space=pltpu.HBM...  2.01 us
  transfers between devices with their start and end apart: 28, of which 17 were waited for; matrix products, arithmetic and copies ran while one was open for 0% of the time, Pallas kernels for 12%

profile of v6, /device:TPU:1, one launch (start us, length us, event | category | flops | bytes accessed | tf_op | source)
XLA Modules:
  0.0 93.0 jit_solution(9377968046911969273)
XLA Ops:
  1.3 1.2 %cut.4 = (f32[82,8,128]{2,1,0:T(8,128)S(1)}, f32[24,3456]{1,0:T(8,128)S(1)}) custom-call(f32[1,1,120,3456]{3,2,1,0:T(8,128)} %numerator_ref.5, f32[1,1]{1,0:T(1,128)S(6)} %copy.16.weight_ref), custom_call_target="tpu_custom_call" | custom-call | bytes 1048576 | tf_op jit(solution)/shard_map/cut/pallas_call | solution.py:171
  2.5 6.5 %collective-permute-start = (f32[24,3456]{1,0:T(8,128)S(1)}, f32[24,3456]{1,0:T(8,128)S(1)}, u32[]{:S(2)}, u32[]{:S(2)}) collective-permute-start(f32[24,3456]{1,0:T(8,128)S(1)} %get-tuple-element.59.refs_1_), channel_id=1, source_target_pairs={{0,224},{16,48},{32,0},{48,80},{64,32},{80,112},{96,64},{112,144},... | collective-permute-start | bytes 995336 | tf_op jit(solution)/shard_map/ppermute | solution.py:25
  9.0 1.1 %cut.5 = (f32[16,3456]{1,0:T(8,128)S(1)}, f32[16,3456]{1,0:T(8,128)S(1)}) custom-call(f32[1,1,120,3456]{3,2,1,0:T(8,128)} %numerator_ref.5, f32[1,1]{1,0:T(1,128)S(6)} %copy.16.weight_ref), custom_call_target="tpu_custom_call" | custom-call | bytes 1048576 | tf_op jit(solution)/shard_map/cut/pallas_call | solution.py:171
  10.0 1.1 %cut.3 = (f32[16,3456]{1,0:T(8,128)S(1)}, f32[24,3456]{1,0:T(8,128)S(1)}) custom-call(f32[1,1,120,3456]{3,2,1,0:T(8,128)} %numerator_ref.5, f32[1,1]{1,0:T(1,128)S(6)} %copy.16.weight_ref), custom_call_target="tpu_custom_call" | custom-call | bytes 1048576 | tf_op jit(solution)/shard_map/cut/pallas_call | solution.py:171
  11.1 2.0 %load.1.refs_0_ = bf16[1,1,2,256,3456]{4,3,2,1,0:T(8,128)(2,1)S(1)} custom-call(bf16[1,1,2,256,3456]{4,3,2,1,0:T(8,128)(2,1)} %inputs_ref.1), custom_call_target="tpu_custom_call" | custom-call | bytes 4194304 | tf_op jit(solution)/shard_map/load/pallas_call | solution.py:190
  13.2 2.3 %collective-permute-done = f32[24,3456]{1,0:T(8,128)S(1)} collective-permute-done((f32[24,3456]{1,0:T(8,128)S(1)}, f32[24,3456]{1,0:T(8,128)S(1)}, u32[]{:S(2)}, u32[]{:S(2)}) %collective-permute-start) | collective-permute-done | bytes 331808 | tf_op jit(solution)/shard_map/ppermute | solution.py:25
  15.5 2.4 %collective-permute-start.1 = (f32[24,3456]{1,0:T(8,128)S(1)}, f32[24,3456]{1,0:T(8,128)S(1)}, u32[]{:S(2)}, u32[]{:S(2)}) collective-permute-start(f32[24,3456]{1,0:T(8,128)S(1)} %add.24), channel_id=1, source_target_pairs={{0,16},{16,0},{32,48},{48,32},{64,80},{80,64},{96,112},{112,96},{1... | collective-permute-start | bytes 995336 | tf_op jit(solution)/shard_map/ppermute | solution.py:25
  17.9 2.7 %collective-permute-start.6 = (f32[24,3456]{1,0:T(8,128)S(1)}, f32[24,3456]{1,0:T(8,128)S(1)}, u32[]{:S(2)}, u32[]{:S(2)}) collective-permute-start(f32[24,3456]{1,0:T(8,128)S(1)} %get-tuple-element.65.refs_1_), channel_id=1, source_target_pairs={{0,224},{16,48},{32,0},{48,80},{64,32},{80,112},{96,64},{112,144},... | collective-permute-start | bytes 995336 | tf_op jit(solution)/shard_map/ppermute | solution.py:25
  20.6 4.2 %collective-permute-done.1.refs_2_ = f32[24,3456]{1,0:T(8,128)S(1)} collective-permute-done((f32[24,3456]{1,0:T(8,128)S(1)}, f32[24,3456]{1,0:T(8,128)S(1)}, u32[]{:S(2)}, u32[]{:S(2)}) %collective-permute-start.1) | collective-permute-done | bytes 331808 | tf_op jit(solution)/shard_map/ppermute | solution.py:25
  24.8 1.2 %collective-permute-start.2 = (f32[16,3456]{1,0:T(8,128)S(1)}, f32[16,3456]{1,0:T(8,128)S(1)}, u32[]{:S(2)}, u32[]{:S(2)}) collective-permute-start(f32[16,3456]{1,0:T(8,128)S(1)} %get-tuple-element.60.refs_3_), channel_id=1, source_target_pairs={{0,16},{16,0},{32,48},{48,32},{64,80},{80,64},{96,112},{112,96},{1... | collective-permute-start | bytes 663560 | tf_op jit(solution)/shard_map/ppermute | solution.py:25
  27.7 2.5 %collective-permute-start.5 = (f32[48,256]{1,0:T(8,128)S(1)}, f32[48,256]{1,0:T(8,128)S(1)}, u32[]{:S(2)}, u32[]{:S(2)}) collective-permute-start(f32[48,256]{1,0:T(8,128)S(1)} %get-tuple-element.63), channel_id=1, source_target_pairs={{0,1},{1,0},{2,3},{3,2},{4,5},{5,4},{6,7},{7,6},{8,9},{9,8},{10,11... | collective-permute-start | bytes 147464 | tf_op jit(solution)/shard_map/ppermute | solution.py:25
  31.1 2.7 %collective-permute-start.17 = (f32[48,256]{1,0:T(8,128)S(1)}, f32[48,256]{1,0:T(8,128)S(1)}, u32[]{:S(2)}, u32[]{:S(2)}) collective-permute-start(f32[48,256]{1,0:T(8,128)S(1)} %add.25.refs_3_), channel_id=1, source_target_pairs={{0,2},{1,3},{2,0},{3,1},{4,6},{5,7},{6,4},{7,5},{8,10},{9,11},{10,... | collective-permute-start | bytes 147464 | tf_op jit(solution)/shard_map/ppermute | solution.py:25
  34.0 1.6 %collective-permute-done.17.refs_4_ = f32[48,256]{1,0:T(8,128)S(1)} collective-permute-done((f32[48,256]{1,0:T(8,128)S(1)}, f32[48,256]{1,0:T(8,128)S(1)}, u32[]{:S(2)}, u32[]{:S(2)}) %collective-permute-start.17) | collective-permute-done | bytes 49184 | tf_op jit(solution)/shard_map/ppermute | solution.py:25
  36.4 2.6 %collective-permute-start.19 = (f32[163,8,128]{2,1,0:T(8,128)S(1)}, f32[163,8,128]{2,1,0:T(8,128)S(1)}, u32[]{:S(2)}, u32[]{:S(2)}) collective-permute-start(f32[163,8,128]{2,1,0:T(8,128)S(1)} %get-tuple-element.83.refs_1_), channel_id=1, source_target_pairs={{0,12},{4,0},{8,4},{12,8},{1,13},{5,1},{9,5},{13,9},{2,14},{6,2},{... | collective-permute-start | bytes 2002952 | tf_op jit(solution)/shard_map/ppermute | solution.py:25
  39.0 3.6 %collective-permute-done.7.refs_2_ = f32[24,3456]{1,0:T(8,128)S(1)} collective-permute-done((f32[24,3456]{1,0:T(8,128)S(1)}, f32[24,3456]{1,0:T(8,128)S(1)}, u32[]{:S(2)}, u32[]{:S(2)}) %collective-permute-start.7) | collective-permute-done | bytes 331808 | tf_op jit(solution)/shard_map/ppermute | solution.py:25
  42.5 1.2 %collective-permute-start.10 = (f32[16,3456]{1,0:T(8,128)S(1)}, f32[16,3456]{1,0:T(8,128)S(1)}, u32[]{:S(2)}, u32[]{:S(2)}) collective-permute-start(f32[16,3456]{1,0:T(8,128)S(1)} %get-tuple-element.70.refs_3_), channel_id=1, source_target_pairs={{0,16},{16,0},{32,48},{48,32},{64,80},{80,64},{96,112},{112,96},{1... | collective-permute-start | bytes 663560 | tf_op jit(solution)/shard_map/ppermute | solution.py:25
  45.5 2.2 %collective-permute-start.11 = (f32[40,256]{1,0:T(8,128)S(1)}, f32[40,256]{1,0:T(8,128)S(1)}, u32[]{:S(2)}, u32[]{:S(2)}) collective-permute-start(f32[40,256]{1,0:T(8,128)S(1)} %get-tuple-element.72), channel_id=1, source_target_pairs={{0,1},{1,0},{2,3},{3,2},{4,5},{5,4},{6,7},{7,6},{8,9},{9,8},{10,11... | collective-permute-start | bytes 122888 | tf_op jit(solution)/shard_map/ppermute | solution.py:25
  48.5 1.3 %collective-permute-start.12 = (f32[40,256]{1,0:T(8,128)S(1)}, f32[40,256]{1,0:T(8,128)S(1)}, u32[]{:S(2)}, u32[]{:S(2)}) collective-permute-start(f32[40,256]{1,0:T(8,128)S(1)} %add.27.refs_3_), channel_id=1, source_target_pairs={{0,2},{1,3},{2,0},{3,1},{4,6},{5,7},{6,4},{7,5},{8,10},{9,11},{10,... | collective-permute-start | bytes 122888 | tf_op jit(solution)/shard_map/ppermute | solution.py:25
  50.4 2.5 %collective-permute-done.12.refs_4_ = f32[40,256]{1,0:T(8,128)S(1)} collective-permute-done((f32[40,256]{1,0:T(8,128)S(1)}, f32[40,256]{1,0:T(8,128)S(1)}, u32[]{:S(2)}, u32[]{:S(2)}) %collective-permute-start.12) | collective-permute-done | bytes 40992 | tf_op jit(solution)/shard_map/ppermute | solution.py:25
  54.3 1.9 %collective-permute-start.23 = (f32[40,3456]{1,0:T(8,128)S(1)}, f32[40,3456]{1,0:T(8,128)S(1)}, u32[]{:S(2)}, u32[]{:S(2)}) collective-permute-start(f32[40,3456]{1,0:T(8,128)S(1)} %get-tuple-element.86.refs_1_), channel_id=1, source_target_pairs={{0,12},{4,0},{8,4},{12,8},{1,13},{5,1},{9,5},{13,9},{2,14},{6,2},{... | collective-permute-start | bytes 1658888 | tf_op jit(solution)/shard_map/ppermute | solution.py:25
  57.4 4.0 %collective-permute-start.15 = (f32[32,256]{1,0:T(8,128)S(1)}, f32[32,256]{1,0:T(8,128)S(1)}, u32[]{:S(2)}, u32[]{:S(2)}) collective-permute-start(f32[32,256]{1,0:T(8,128)S(1)} %get-tuple-element.78), channel_id=1, source_target_pairs={{0,1},{1,0},{2,3},{3,2},{4,5},{5,4},{6,7},{7,6},{8,9},{9,8},{10,11... | collective-permute-start | bytes 98312 | tf_op jit(solution)/shard_map/ppermute | solution.py:25
  62.2 1.6 %collective-permute-start.16 = (f32[32,256]{1,0:T(8,128)S(1)}, f32[32,256]{1,0:T(8,128)S(1)}, u32[]{:S(2)}, u32[]{:S(2)}) collective-permute-start(f32[32,256]{1,0:T(8,128)S(1)} %add.29.refs_3_), channel_id=1, source_target_pairs={{0,2},{1,3},{2,0},{3,1},{4,6},{5,7},{6,4},{7,5},{8,10},{9,11},{10,... | collective-permute-start | bytes 98312 | tf_op jit(solution)/shard_map/ppermute | solution.py:25
  63.9 2.6 %collective-permute-done.16.refs_4_ = f32[32,256]{1,0:T(8,128)S(1)} collective-permute-done((f32[32,256]{1,0:T(8,128)S(1)}, f32[32,256]{1,0:T(8,128)S(1)}, u32[]{:S(2)}, u32[]{:S(2)}) %collective-permute-start.16) | collective-permute-done | bytes 32800 | tf_op jit(solution)/shard_map/ppermute | solution.py:25
  67.1 2.1 %collective-permute-done.22.refs_2_ = f32[40,3456]{1,0:T(8,128)S(1)} collective-permute-done((f32[40,3456]{1,0:T(8,128)S(1)}, f32[40,3456]{1,0:T(8,128)S(1)}, u32[]{:S(2)}, u32[]{:S(2)}) %collective-permute-start.22) | collective-permute-done | bytes 552992 | tf_op jit(solution)/shard_map/ppermute | solution.py:25
  69.7 1.0 %collective-permute-start.24 = (f32[32,3456]{1,0:T(8,128)S(1)}, f32[32,3456]{1,0:T(8,128)S(1)}, u32[]{:S(2)}, u32[]{:S(2)}) collective-permute-start(f32[32,3456]{1,0:T(8,128)S(1)} %get-tuple-element.88.refs_4_), channel_id=1, source_target_pairs={{0,4},{4,8},{8,12},{12,0},{1,5},{5,9},{9,13},{13,1},{2,6},{6,10},{... | collective-permute-start | bytes 1327112 | tf_op jit(solution)/shard_map/ppermute | solution.py:25
  71.4 3.8 %collective-permute-start.20 = (f32[48,256]{1,0:T(8,128)S(1)}, f32[48,256]{1,0:T(8,128)S(1)}, u32[]{:S(2)}, u32[]{:S(2)}) collective-permute-start(f32[48,256]{1,0:T(8,128)S(1)} %get-tuple-element.84), channel_id=1, source_target_pairs={{0,1},{1,0},{2,3},{3,2},{4,5},{5,4},{6,7},{7,6},{8,9},{9,8},{10,11... | collective-permute-start | bytes 147464 | tf_op jit(solution)/shard_map/ppermute | solution.py:25
  76.1 1.6 %collective-permute-start.21 = (f32[48,256]{1,0:T(8,128)S(1)}, f32[48,256]{1,0:T(8,128)S(1)}, u32[]{:S(2)}, u32[]{:S(2)}) collective-permute-start(f32[48,256]{1,0:T(8,128)S(1)} %add.30.refs_3_), channel_id=1, source_target_pairs={{0,2},{1,3},{2,0},{3,1},{4,6},{5,7},{6,4},{7,5},{8,10},{9,11},{10,... | collective-permute-start | bytes 147464 | tf_op jit(solution)/shard_map/ppermute | solution.py:25
  77.7 2.9 %collective-permute-done.21.refs_4_ = f32[48,256]{1,0:T(8,128)S(1)} collective-permute-done((f32[48,256]{1,0:T(8,128)S(1)}, f32[48,256]{1,0:T(8,128)S(1)}, u32[]{:S(2)}, u32[]{:S(2)}) %collective-permute-start.21) | collective-permute-done | bytes 49184 | tf_op jit(solution)/shard_map/ppermute | solution.py:25
  81.3 3.0 %collective-permute-start.26 = (f32[72,256]{1,0:T(8,128)S(1)}, f32[72,256]{1,0:T(8,128)S(1)}, u32[]{:S(2)}, u32[]{:S(2)}) collective-permute-start(f32[72,256]{1,0:T(8,128)S(1)} %get-tuple-element.90), channel_id=1, source_target_pairs={{0,1},{1,0},{2,3},{3,2},{4,5},{5,4},{6,7},{7,6},{8,9},{9,8},{10,11... | collective-permute-start | bytes 221192 | tf_op jit(solution)/shard_map/ppermute | solution.py:25
  86.2 2.3 %update1.2 = (f32[1,1,120,3456]{3,2,1,0:T(8,128)}, f32[1,1,120,3456]{3,2,1,0:T(8,128)}, f32[1,1,120,3456]{3,2,1,0:T(8,128)}, f32[1,1]{1,0:T(1,128)}) custom-call(bf16[1,1,2,256,3456]{4,3,2,1,0:T(8,128)(2,1)S(1)} %load.1.refs_0_, f32[1,1,2,120,256]{4,3,2,1,0:T(8,128)S(1)} %copy-done.2, f32[48,3456]{1,0:T(8,128)S(1)} %get-tuple-element.96.refs_2_, ...), custom_call_target="tpu_custom_call" | custom-call | flops 5096079360 | bytes 1048576 | tf_op jit(solution)/shard_map/update1/pallas_call | solution.py:294
  88.5 1.5 %collective-permute-done.27.refs_4_ = f32[72,256]{1,0:T(8,128)S(1)} collective-permute-done((f32[72,256]{1,0:T(8,128)S(1)}, f32[72,256]{1,0:T(8,128)S(1)}, u32[]{:S(2)}, u32[]{:S(2)}) %collective-permute-start.27) | collective-permute-done | bytes 73760 | tf_op jit(solution)/shard_map/ppermute | solution.py:25
  90.0 2.8 %update1.3 = (f32[1,1,120,3456]{3,2,1,0:T(8,128)}, f32[1,1,120,3456]{3,2,1,0:T(8,128)}, f32[1,1,120,3456]{3,2,1,0:T(8,128)}, f32[1,1]{1,0:T(1,128)}) custom-call(bf16[1,1,2,256,3456]{4,3,2,1,0:T(8,128)(2,1)S(1)} %load.1.refs_0_, f32[1,1,2,120,256]{4,3,2,1,0:T(8,128)S(1)} %copy-done.2, ...), custom_call_target="tpu_custom_call", output_to_operand_aliasing={{0}: (10, {}), {1}: (11, {}), {2}: (12, {})} | custom-call | flops 7644119040 | bytes 1048576 | tf_op jit(solution)/shard_map/update1/pallas_call | solution.py:294
  (52 shorter events, 15.6 us)
Async XLA Ops:
  2.5 12.9 %collective-permute-start = (f32[24,3456]{1,0:T(8,128)S(1)}, f32[24,3456]{1,0:T(8,128)S(1)}, u32[]{:S(2)}, u32[]{:S(2)}) collective-permute-start(f32[24,3456]{1,0:T(8,128)S(1)} %get-tuple-element.59.refs_1_), channel_id=1, source_target_pairs={{0,224},{16,48},{32,0},{48,80},{64,32},{80,112},{96,64},{112,144},... | collective-permute-start | bytes 995336 | tf_op jit(solution)/shard_map/ppermute | solution.py:25
  9.0 8.9 %collective-permute-start.3 = (f32[82,8,128]{2,1,0:T(8,128)S(1)}, f32[82,8,128]{2,1,0:T(8,128)S(1)}, u32[]{:S(2)}, u32[]{:S(2)}) collective-permute-start(f32[82,8,128]{2,1,0:T(8,128)S(1)} %get-tuple-element.61.refs_3_), channel_id=1, source_target_pairs={{0,16},{16,0},{32,48},{48,32},{64,80},{80,64},{96,112},{112,96},{1... | collective-permute-start | bytes 1007624 | tf_op jit(solution)/shard_map/ppermute | solution.py:25
  15.5 9.3 %collective-permute-start.1 = (f32[24,3456]{1,0:T(8,128)S(1)}, f32[24,3456]{1,0:T(8,128)S(1)}, u32[]{:S(2)}, u32[]{:S(2)}) collective-permute-start(f32[24,3456]{1,0:T(8,128)S(1)} %add.24), channel_id=1, source_target_pairs={{0,16},{16,0},{32,48},{48,32},{64,80},{80,64},{96,112},{112,96},{1... | collective-permute-start | bytes 995336 | tf_op jit(solution)/shard_map/ppermute | solution.py:25
  17.9 9.1 %collective-permute-start.4 = (f32[82,8,128]{2,1,0:T(8,128)S(1)}, f32[82,8,128]{2,1,0:T(8,128)S(1)}, u32[]{:S(2)}, u32[]{:S(2)}) collective-permute-start(f32[82,8,128]{2,1,0:T(8,128)S(1)} %collective-permute-done.3.refs_4_), channel_id=1, source_target_pairs={{0,32},{16,240},{32,64},{48,16},{64,96},{80,48},{96,128},{112,80},... | collective-permute-start | bytes 1007624 | tf_op jit(solution)/shard_map/ppermute | solution.py:25
  17.9 15.8 %collective-permute-start.6 = (f32[24,3456]{1,0:T(8,128)S(1)}, f32[24,3456]{1,0:T(8,128)S(1)}, u32[]{:S(2)}, u32[]{:S(2)}) collective-permute-start(f32[24,3456]{1,0:T(8,128)S(1)} %get-tuple-element.65.refs_1_), channel_id=1, source_target_pairs={{0,224},{16,48},{32,0},{48,80},{64,32},{80,112},{96,64},{112,144},... | collective-permute-start | bytes 995336 | tf_op jit(solution)/shard_map/ppermute | solution.py:25
  24.8 10.8 %copy-start = (f32[1,1,120,3456]{3,2,1,0:T(8,128)S(1)}, f32[1,1,120,3456]{3,2,1,0:T(8,128)}, u32[]{:S(2)}) copy-start(f32[1,1,120,3456]{3,2,1,0:T(8,128)} %param.10) | copy-start | bytes 4976644
  24.8 10.8 %copy-start.1 = (f32[1,1,120,3456]{3,2,1,0:T(8,128)S(1)}, f32[1,1,120,3456]{3,2,1,0:T(8,128)}, u32[]{:S(2)}) copy-start(f32[1,1,120,3456]{3,2,1,0:T(8,128)} %param.11) | copy-start | bytes 4976644
  24.8 10.8 %copy-start.2 = (f32[1,1,2,120,256]{4,3,2,1,0:T(8,128)S(1)}, f32[1,1,2,120,256]{4,3,2,1,0:T(8,128)}, u32[]{:S(2)}) copy-start(f32[1,1,2,120,256]{4,3,2,1,0:T(8,128)} %refs_1_.9) | copy-start | bytes 737284
  24.8 8.9 %collective-permute-start.2 = (f32[16,3456]{1,0:T(8,128)S(1)}, f32[16,3456]{1,0:T(8,128)S(1)}, u32[]{:S(2)}, u32[]{:S(2)}) collective-permute-start(f32[16,3456]{1,0:T(8,128)S(1)} %get-tuple-element.60.refs_3_), channel_id=1, source_target_pairs={{0,16},{16,0},{32,48},{48,32},{64,80},{80,64},{96,112},{112,96},{1... | collective-permute-start | bytes 663560 | tf_op jit(solution)/shard_map/ppermute | solution.py:25
  27.7 3.4 %collective-permute-start.5 = (f32[48,256]{1,0:T(8,128)S(1)}, f32[48,256]{1,0:T(8,128)S(1)}, u32[]{:S(2)}, u32[]{:S(2)}) collective-permute-start(f32[48,256]{1,0:T(8,128)S(1)} %get-tuple-element.63), channel_id=1, source_target_pairs={{0,1},{1,0},{2,3},{3,2},{4,5},{5,4},{6,7},{7,6},{8,9},{9,8},{10,11... | collective-permute-start | bytes 147464 | tf_op jit(solution)/shard_map/ppermute | solution.py:25
  31.1 4.5 %collective-permute-start.17 = (f32[48,256]{1,0:T(8,128)S(1)}, f32[48,256]{1,0:T(8,128)S(1)}, u32[]{:S(2)}, u32[]{:S(2)}) collective-permute-start(f32[48,256]{1,0:T(8,128)S(1)} %add.25.refs_3_), channel_id=1, source_target_pairs={{0,2},{1,3},{2,0},{3,1},{4,6},{5,7},{6,4},{7,5},{8,10},{9,11},{10,... | collective-permute-start | bytes 147464 | tf_op jit(solution)/shard_map/ppermute | solution.py:25
  33.8 8.7 %collective-permute-start.7 = (f32[24,3456]{1,0:T(8,128)S(1)}, f32[24,3456]{1,0:T(8,128)S(1)}, u32[]{:S(2)}, u32[]{:S(2)}) collective-permute-start(f32[24,3456]{1,0:T(8,128)S(1)} %add.26), channel_id=1, source_target_pairs={{0,16},{16,0},{32,48},{48,32},{64,80},{80,64},{96,112},{112,96},{1... | collective-permute-start | bytes 995336 | tf_op jit(solution)/shard_map/ppermute | solution.py:25
  33.9 10.9 %collective-permute-start.8 = (f32[16,3456]{1,0:T(8,128)S(1)}, f32[16,3456]{1,0:T(8,128)S(1)}, u32[]{:S(2)}, u32[]{:S(2)}) collective-permute-start(f32[16,3456]{1,0:T(8,128)S(1)} %collective-permute-done.2.refs_4_), channel_id=1, source_target_pairs={{0,32},{16,240},{32,64},{48,16},{64,96},{80,48},{96,128},{112,80},... | collective-permute-start | bytes 663560 | tf_op jit(solution)/shard_map/ppermute | solution.py:25
  36.4 17.2 %collective-permute-start.19 = (f32[163,8,128]{2,1,0:T(8,128)S(1)}, f32[163,8,128]{2,1,0:T(8,128)S(1)}, u32[]{:S(2)}, u32[]{:S(2)}) collective-permute-start(f32[163,8,128]{2,1,0:T(8,128)S(1)} %get-tuple-element.83.refs_1_), channel_id=1, source_target_pairs={{0,12},{4,0},{8,4},{12,8},{1,13},{5,1},{9,5},{13,9},{2,14},{6,2},{... | collective-permute-start | bytes 2002952 | tf_op jit(solution)/shard_map/ppermute | solution.py:25
  39.0 15.4 %collective-permute-start.18 = (f32[163,8,128]{2,1,0:T(8,128)S(1)}, f32[163,8,128]{2,1,0:T(8,128)S(1)}, u32[]{:S(2)}, u32[]{:S(2)}) collective-permute-start(f32[163,8,128]{2,1,0:T(8,128)S(1)} %get-tuple-element.83.refs_1_), channel_id=1, source_target_pairs={{0,4},{4,8},{8,12},{12,0},{1,5},{5,9},{9,13},{13,1},{2,6},{6,10},{... | collective-permute-start | bytes 2002952 | tf_op jit(solution)/shard_map/ppermute | solution.py:25
  42.5 7.3 %collective-permute-start.10 = (f32[16,3456]{1,0:T(8,128)S(1)}, f32[16,3456]{1,0:T(8,128)S(1)}, u32[]{:S(2)}, u32[]{:S(2)}) collective-permute-start(f32[16,3456]{1,0:T(8,128)S(1)} %get-tuple-element.70.refs_3_), channel_id=1, source_target_pairs={{0,16},{16,0},{32,48},{48,32},{64,80},{80,64},{96,112},{112,96},{1... | collective-permute-start | bytes 663560 | tf_op jit(solution)/shard_map/ppermute | solution.py:25
  43.8 6.0 %collective-permute-start.9 = (f32[16,3456]{1,0:T(8,128)S(1)}, f32[16,3456]{1,0:T(8,128)S(1)}, u32[]{:S(2)}, u32[]{:S(2)}) collective-permute-start(f32[16,3456]{1,0:T(8,128)S(1)} %get-tuple-element.75.refs_1_), channel_id=1, source_target_pairs={{0,224},{16,48},{32,0},{48,80},{64,32},{80,112},{96,64},{112,144},... | collective-permute-start | bytes 663560 | tf_op jit(solution)/shard_map/ppermute | solution.py:25
  45.5 3.1 %collective-permute-start.11 = (f32[40,256]{1,0:T(8,128)S(1)}, f32[40,256]{1,0:T(8,128)S(1)}, u32[]{:S(2)}, u32[]{:S(2)}) collective-permute-start(f32[40,256]{1,0:T(8,128)S(1)} %get-tuple-element.72), channel_id=1, source_target_pairs={{0,1},{1,0},{2,3},{3,2},{4,5},{5,4},{6,7},{7,6},{8,9},{9,8},{10,11... | collective-permute-start | bytes 122888 | tf_op jit(solution)/shard_map/ppermute | solution.py:25
  48.5 4.4 %collective-permute-start.12 = (f32[40,256]{1,0:T(8,128)S(1)}, f32[40,256]{1,0:T(8,128)S(1)}, u32[]{:S(2)}, u32[]{:S(2)}) collective-permute-start(f32[40,256]{1,0:T(8,128)S(1)} %add.27.refs_3_), channel_id=1, source_target_pairs={{0,2},{1,3},{2,0},{3,1},{4,6},{5,7},{6,4},{7,5},{8,10},{9,11},{10,... | collective-permute-start | bytes 122888 | tf_op jit(solution)/shard_map/ppermute | solution.py:25
  49.8 6.9 %collective-permute-start.13 = (f32[16,3456]{1,0:T(8,128)S(1)}, f32[16,3456]{1,0:T(8,128)S(1)}, u32[]{:S(2)}, u32[]{:S(2)}) collective-permute-start(f32[16,3456]{1,0:T(8,128)S(1)} %add.28), channel_id=1, source_target_pairs={{0,16},{16,0},{32,48},{48,32},{64,80},{80,64},{96,112},{112,96},{1... | collective-permute-start | bytes 663560 | tf_op jit(solution)/shard_map/ppermute | solution.py:25
  50.4 6.3 %collective-permute-start.14 = (f32[16,3456]{1,0:T(8,128)S(1)}, f32[16,3456]{1,0:T(8,128)S(1)}, u32[]{:S(2)}, u32[]{:S(2)}) collective-permute-start(f32[16,3456]{1,0:T(8,128)S(1)} %collective-permute-done.10.refs_4_), channel_id=1, source_target_pairs={{0,32},{16,240},{32,64},{48,16},{64,96},{80,48},{96,128},{112,80},... | collective-permute-start | bytes 663560 | tf_op jit(solution)/shard_map/ppermute | solution.py:25
  54.3 12.8 %collective-permute-start.23 = (f32[40,3456]{1,0:T(8,128)S(1)}, f32[40,3456]{1,0:T(8,128)S(1)}, u32[]{:S(2)}, u32[]{:S(2)}) collective-permute-start(f32[40,3456]{1,0:T(8,128)S(1)} %get-tuple-element.86.refs_1_), channel_id=1, source_target_pairs={{0,12},{4,0},{8,4},{12,8},{1,13},{5,1},{9,5},{13,9},{2,14},{6,2},{... | collective-permute-start | bytes 1658888 | tf_op jit(solution)/shard_map/ppermute | solution.py:25
  56.2 13.1 %collective-permute-start.22 = (f32[40,3456]{1,0:T(8,128)S(1)}, f32[40,3456]{1,0:T(8,128)S(1)}, u32[]{:S(2)}, u32[]{:S(2)}) collective-permute-start(f32[40,3456]{1,0:T(8,128)S(1)} %get-tuple-element.86.refs_1_), channel_id=1, source_target_pairs={{0,4},{4,8},{8,12},{12,0},{1,5},{5,9},{9,13},{13,1},{2,6},{6,10},{... | collective-permute-start | bytes 1658888 | tf_op jit(solution)/shard_map/ppermute | solution.py:25
  57.4 4.8 %collective-permute-start.15 = (f32[32,256]{1,0:T(8,128)S(1)}, f32[32,256]{1,0:T(8,128)S(1)}, u32[]{:S(2)}, u32[]{:S(2)}) collective-permute-start(f32[32,256]{1,0:T(8,128)S(1)} %get-tuple-element.78), channel_id=1, source_target_pairs={{0,1},{1,0},{2,3},{3,2},{4,5},{5,4},{6,7},{7,6},{8,9},{9,8},{10,11... | collective-permute-start | bytes 98312 | tf_op jit(solution)/shard_map/ppermute | solution.py:25
  62.2 4.3 %collective-permute-start.16 = (f32[32,256]{1,0:T(8,128)S(1)}, f32[32,256]{1,0:T(8,128)S(1)}, u32[]{:S(2)}, u32[]{:S(2)}) collective-permute-start(f32[32,256]{1,0:T(8,128)S(1)} %add.29.refs_3_), channel_id=1, source_target_pairs={{0,2},{1,3},{2,0},{3,1},{4,6},{5,7},{6,4},{7,5},{8,10},{9,11},{10,... | collective-permute-start | bytes 98312 | tf_op jit(solution)/shard_map/ppermute | solution.py:25
  69.2 11.3 %collective-permute-start.25 = (f32[32,3456]{1,0:T(8,128)S(1)}, f32[32,3456]{1,0:T(8,128)S(1)}, u32[]{:S(2)}, u32[]{:S(2)}) collective-permute-start(f32[32,3456]{1,0:T(8,128)S(1)} %get-tuple-element.88.refs_4_), channel_id=1, source_target_pairs={{0,12},{4,0},{8,4},{12,8},{1,13},{5,1},{9,5},{13,9},{2,14},{6,2},{... | collective-permute-start | bytes 1327112 | tf_op jit(solution)/shard_map/ppermute | solution.py:25
  69.7 10.9 %collective-permute-start.24 = (f32[32,3456]{1,0:T(8,128)S(1)}, f32[32,3456]{1,0:T(8,128)S(1)}, u32[]{:S(2)}, u32[]{:S(2)}) collective-permute-start(f32[32,3456]{1,0:T(8,128)S(1)} %get-tuple-element.88.refs_4_), channel_id=1, source_target_pairs={{0,4},{4,8},{8,12},{12,0},{1,5},{5,9},{9,13},{13,1},{2,6},{6,10},{... | collective-permute-start | bytes 1327112 | tf_op jit(solution)/shard_map/ppermute | solution.py:25
  71.4 4.6 %collective-permute-start.20 = (f32[48,256]{1,0:T(8,128)S(1)}, f32[48,256]{1,0:T(8,128)S(1)}, u32[]{:S(2)}, u32[]{:S(2)}) collective-permute-start(f32[48,256]{1,0:T(8,128)S(1)} %get-tuple-element.84), channel_id=1, source_target_pairs={{0,1},{1,0},{2,3},{3,2},{4,5},{5,4},{6,7},{7,6},{8,9},{9,8},{10,11... | collective-permute-start | bytes 147464 | tf_op jit(solution)/shard_map/ppermute | solution.py:25
  76.1 4.5 %collective-permute-start.21 = (f32[48,256]{1,0:T(8,128)S(1)}, f32[48,256]{1,0:T(8,128)S(1)}, u32[]{:S(2)}, u32[]{:S(2)}) collective-permute-start(f32[48,256]{1,0:T(8,128)S(1)} %add.30.refs_3_), channel_id=1, source_target_pairs={{0,2},{1,3},{2,0},{3,1},{4,6},{5,7},{6,4},{7,5},{8,10},{9,11},{10,... | collective-permute-start | bytes 147464 | tf_op jit(solution)/shard_map/ppermute | solution.py:25
  81.3 3.9 %collective-permute-start.26 = (f32[72,256]{1,0:T(8,128)S(1)}, f32[72,256]{1,0:T(8,128)S(1)}, u32[]{:S(2)}, u32[]{:S(2)}) collective-permute-start(f32[72,256]{1,0:T(8,128)S(1)} %get-tuple-element.90), channel_id=1, source_target_pairs={{0,1},{1,0},{2,3},{3,2},{4,5},{5,4},{6,7},{7,6},{8,9},{9,8},{10,11... | collective-permute-start | bytes 221192 | tf_op jit(solution)/shard_map/ppermute | solution.py:25
  85.3 4.8 %collective-permute-start.27 = (f32[72,256]{1,0:T(8,128)S(1)}, f32[72,256]{1,0:T(8,128)S(1)}, u32[]{:S(2)}, u32[]{:S(2)}) collective-permute-start(f32[72,256]{1,0:T(8,128)S(1)} %add.31.refs_3_), channel_id=1, source_target_pairs={{0,2},{1,3},{2,0},{3,1},{4,6},{5,7},{6,4},{7,5},{8,10},{9,11},{10,... | collective-permute-start | bytes 221192 | tf_op jit(solution)/shard_map/ppermute | solution.py:25
